TPU v7x, 256 devices: a whole 4x4x8 slice. The times are simulated.
256 devices in a mesh: pos: 8 (over y_hi, x), beam: 32 (over z, y_lo, core).
Axes of the slice: x: 4, y: 4 (y_hi: 2, y_lo: 2; y = y_hi * 2 + y_lo), z: 8, core: 2. Of those that a mesh axis runs over, the one named last changes fastest.
Arguments:
- s_matrix: bfloat16 [2048, 2, 144, 256], P('beam'), may hold values from -0.119628906 to 0.119628906
- beam_index: int32 [2048, 2], P('beam'), may hold values from -24 to 24
- amplitude: float32 [2048], P('beam'), may hold values from 0.3 to 3
- phase: float32 [2048], P('beam'), may hold values from -3.140625 to 3.140625
- offsets_y: int32 [32], replicated, may hold values from 0 to 16
- offsets_x: int32 [32], replicated, may hold values from 0 to 128
- measured: float32 [32, 128, 128], P('pos'), may hold values from 0.3 to 2
Outputs:
- s_gradient: float32 [2048, 2, 144, 256], P('beam', None, 'pos')
All inputs are finite; a program needn't handle non-finite values.
Results may differ from a plain program's by a relative error of at most 0.007.
Values sent between devices are 32-bit elements; how exact they have to be, the bound alone decides.
No kernel may reach another device: no remote copies, remote signals or barrier semaphores. Data moves between devices by JAX's collectives and lax.ppermute only.
A program may use at most 128 MiB of HBM per device.

v0:
```python
import math

import jax
import jax.numpy as jnp
from jax import lax
from jax.sharding import PartitionSpec as P

WIN = 128
FIELD_Y = 144
FIELD_X = 256


def beam_weights(rows_y, cols_x, beam_index, amplitude, phase):
    wave_y = beam_index[:, 0]
    wave_x = beam_index[:, 1]
    turns = jnp.mod(
        rows_y[:, None] * wave_y[None, :] * FIELD_X + cols_x[:, None] * wave_x[None, :] * FIELD_Y,
        FIELD_Y * FIELD_X,
    )
    angles = phase[None, :] - 2.0 * math.pi / (FIELD_Y * FIELD_X) * turns.astype(jnp.float32)
    real_coef = (amplitude[None, :] * jnp.cos(angles)).astype(jnp.bfloat16)
    imag_coef = (amplitude[None, :] * jnp.sin(angles)).astype(jnp.bfloat16)
    return (real_coef, imag_coef)


def mixing(real_coef, imag_coef):
    upper = jnp.stack([real_coef, -imag_coef], axis=-1).reshape(-1)
    lower = jnp.stack([imag_coef, real_coef], axis=-1).reshape(-1)
    return jnp.stack([upper, lower])


def crop_window(full_wave, row_y, col_x):
    anchor = jnp.zeros((), jnp.int32)
    return lax.dynamic_slice(full_wave, (anchor, row_y, col_x), (2, WIN, WIN))


def all_waves(s_matrix, rows_y, cols_x, real_coef, imag_coef):
    beams_here = s_matrix.shape[0]
    count = real_coef.shape[0]
    mixers = jax.vmap(mixing)(real_coef, imag_coef).reshape(count * 2, beams_here * 2)
    flat = s_matrix.reshape(beams_here * 2, FIELD_Y * FIELD_X)
    full_waves = jnp.dot(mixers, flat, preferred_element_type=jnp.float32).reshape(
        count, 2, FIELD_Y, FIELD_X
    )
    return jax.vmap(crop_window)(full_waves, rows_y, cols_x)


def gradient_matrix(real_coef, imag_coef):
    real_wide = real_coef.astype(jnp.float32).T
    imag_wide = imag_coef.astype(jnp.float32).T
    upper = jnp.stack([real_wide, imag_wide], axis=-1)
    lower = jnp.stack([-imag_wide, real_wide], axis=-1)
    return jnp.stack([upper, lower], axis=1).reshape(real_wide.shape[0] * 2, -1)


def place_band(plane, top_row, col_x, band_rows):
    frame = jnp.zeros((2, band_rows + 2 * WIN, FIELD_X), jnp.float32)
    frame = lax.dynamic_update_slice(frame, plane, (jnp.zeros((), jnp.int32), top_row, col_x))
    return frame[:, WIN : WIN + band_rows]


def tables():
    counter = jnp.arange(WIN, dtype=jnp.int32)
    product = jnp.mod(counter[:, None] * counter[None, :], WIN).astype(jnp.float32)
    angles = 2.0 * math.pi / WIN * product
    norming = 1.0 / math.sqrt(WIN)
    return (jnp.cos(angles) * norming, jnp.sin(angles) * norming)


def transform(real_part, imag_part, cos_table, sin_table, direction):
    highest = lax.Precision.HIGHEST
    signed_sin = direction * sin_table
    last_real = jnp.einsum("pyn,kn->pyk", real_part, cos_table, precision=highest) - jnp.einsum(
        "pyn,kn->pyk", imag_part, signed_sin, precision=highest
    )
    last_imag = jnp.einsum("pyn,kn->pyk", real_part, signed_sin, precision=highest) + jnp.einsum(
        "pyn,kn->pyk", imag_part, cos_table, precision=highest
    )
    out_real = jnp.einsum("pnx,kn->pkx", last_real, cos_table, precision=highest) - jnp.einsum(
        "pnx,kn->pkx", last_imag, signed_sin, precision=highest
    )
    out_imag = jnp.einsum("pnx,kn->pkx", last_real, signed_sin, precision=highest) + jnp.einsum(
        "pnx,kn->pkx", last_imag, cos_table, precision=highest
    )
    return (out_real, out_imag)


def project(spec_real, spec_imag, target):
    modulus = jnp.sqrt(spec_real * spec_real + spec_imag * spec_imag)
    factor = 1.0 - target / jnp.maximum(modulus, 0.5)
    return (spec_real * factor, spec_imag * factor)


def body(s_matrix, beam_index, amplitude, phase, offsets_y, offsets_x, measured):
    local_count = measured.shape[0]
    beams_here = s_matrix.shape[0]
    group_index = lax.axis_index("pos")
    own_y = lax.dynamic_slice_in_dim(offsets_y, group_index * local_count, local_count)
    own_x = lax.dynamic_slice_in_dim(offsets_x, group_index * local_count, local_count)
    real_coef, imag_coef = beam_weights(own_y, own_x, beam_index, amplitude, phase)
    partial_waves = all_waves(s_matrix, own_y, own_x, real_coef, imag_coef)
    cos_table, sin_table = tables()
    summed = lax.psum(partial_waves, "beam")
    spec_real, spec_imag = transform(summed[:, 0], summed[:, 1], cos_table, sin_table, -1.0)
    resid_real, resid_imag = project(spec_real, spec_imag, measured)
    back_real, back_imag = transform(resid_real, resid_imag, cos_table, sin_table, 1.0)
    planes = jnp.stack([back_real, back_imag], axis=1)
    band_rows = FIELD_Y // lax.axis_size("pos")
    first_row = group_index * band_rows
    pieces = lax.all_gather(planes, "pos", axis=0, tiled=True)
    number = pieces.shape[0]
    coef_real, coef_imag = beam_weights(offsets_y, offsets_x, beam_index, amplitude, phase)
    placed = jax.vmap(
        lambda plane, row_y, col_x: place_band(plane, row_y - first_row + WIN, col_x, band_rows)
    )(pieces, offsets_y, offsets_x)
    weights = gradient_matrix(coef_real, coef_imag)
    folded = jnp.dot(
        weights, placed.reshape(number * 2, band_rows * FIELD_X), precision=lax.Precision.HIGHEST
    )
    band = folded.reshape(beams_here, 2, band_rows, FIELD_X)
    return band


def solution(mesh):
    return jax.shard_map(
        body,
        mesh=mesh,
        in_specs=(
            P("beam", None, None, None),
            P("beam", None),
            P("beam"),
            P("beam"),
            P(),
            P(),
            P("pos", None, None),
        ),
        out_specs=P("beam", None, "pos", None),
        check_vma=False,
    )
```

profile of v0, /device:TPU:1, one launch (start us, length us, event | category | flops | bytes accessed | tf_op | source)
XLA Modules:
  0.0 800.1 jit_solution(6031265043073735059)
XLA Ops:
  10.1 11.4 %copy.60 = bf16[16,8,144,256]{3,1,2,0:T(8,128)(2,1)} copy(bf16[16,8,144,256]{3,2,1,0:T(8,128)(2,1)} %bitcast.163) | data formatting | bytes 18874368
  21.5 12.6 %copy.46 = bf16[36864,128]{1,0:T(8,128)(2,1)} copy(bf16[36864,128]{0,1:T(8,128)(2,1)} %bitcast.161) | data formatting | bytes 18874368 | tf_op jit(solution)/shard_map/dot_general | solution.py:42
  34.3 6.2 fusion.76
  40.5 14.3 %while.2 = (s32[]{:T(128)}, f32[4,2,144,256]{3,0,2,1:T(4,128)S(1)}, s32[4,4]{1,0:T(4,128)S(1)}, f32[4,2,128,128]{3,2,0,1:T(8,128)}, s32[]{:T(128)}) while((s32[]{:T(128)}, f32[4,2,144,256]{3,0,2,1:T(4,128)S(1)}, s32[4,4]{1,0:T(4,128)S(1)}, f32[4,2,128,128]{3,2,0,1:T(8,128)}, s32[]{:T(128)}) %tuple.56), condition=%wide.while_cond, body=%wide.while_body.sunk | while | flops 2 | bytes 524933 | solution.py:34
  55.0 228.4 %all-reduce.2.cloned.1.call-done = f32[4,2,128,128]{3,2,0,1:T(8,128)} async-done(((f32[4,2,128,128]{3,2,0,1:T(8,128)}), f32[4,2,128,128]{3,2,0,1:T(8,128)}) %all-reduce.2.cloned.1.call-update) | async-done | bytes 524304 | tf_op jit(solution)/shard_map/psum | solution.py:103
  299.2 76.1 %all-gather.2.cloned.1.call-done = f32[32,2,128,128]{3,2,0,1:T(8,128)} async-done(((f32[4,2,128,128]{3,2,0,1:T(8,128)}), f32[32,2,128,128]{3,2,0,1:T(8,128)}) %all-gather.2.cloned.1.call-update) | async-done | bytes 4194320 | tf_op jit(solution)/shard_map/all_gather | solution.py:110
  375.4 8.6 %broadcast_in_dim.14 = f32[32,2,274,256]{3,2,1,0:T(8,128)} broadcast(f32[]{:T(128)} %constant.26.clone.1), dimensions={} | broadcast | bytes 17956868 | tf_op jit(solution)/shard_map/vmap(vmap())/broadcast_in_dim;vmap()/broadcast_in_dim | solution.py:58
  383.9 402.4 %while.3 = (s32[]{:T(128)}, f32[32,2,274,256]{3,2,1,0:T(8,128)}, s32[32,4]{0,1:T(4,128)S(1)}, f32[32,2,128,128]{3,2,0,1:T(8,128)}, s32[]{:T(128)}, /*index=5*/s32[4]{0:T(128)S(1)}, s32[]{:T(128)}) while((s32[]{:T(128)}, f32[32,2,274,256]{3,2,1,0:T(8,128)}, s32[32,4]{0,1:T(4,128)S(1)}, f32[32,2,128,128]{3,2,0,1:T(8,128)}, s32[]{:T(128)}, ...), condition=%wide.while_cond.1, body=%wide.while_body.1.sunk | while | flops 32797 | bytes 655559 | solution.py:58
  416.6 5.2 dynamic-update-slice.8
  429.3 5.2 dynamic-update-slice.8
  442.0 5.2 dynamic-update-slice.8
  478.8 5.3 dynamic-update-slice.8
  491.5 5.2 dynamic-update-slice.8
  553.3 5.2 dynamic-update-slice.8
  565.9 5.2 dynamic-update-slice.8
  578.6 5.3 dynamic-update-slice.8
  591.3 5.2 dynamic-update-slice.8
  603.9 5.2 dynamic-update-slice.8
  667.1 5.3 dynamic-update-slice.8
  692.5 5.3 dynamic-update-slice.8
  705.2 5.2 dynamic-update-slice.8
  717.9 5.2 dynamic-update-slice.8
  755.8 5.2 dynamic-update-slice.8
  781.1 5.3 dynamic-update-slice.8
  (223 shorter events, 358.9 us)
Async XLA Ops:
  6.5 276.8 %all-reduce.2.cloned.1.call-start = ((), (), s32[]{:S(2)}) async-start(), calls=%async_computation | async-start | bytes 1048576 | tf_op jit(solution)/shard_map/psum | solution.py:103
  40.5 251.1 %copy-start.6 = (f32[4,128,128]{2,1,0:T(8,128)S(1)}, f32[4,128,128]{2,1,0:T(8,128)}, u32[]{:S(2)}) copy-start(f32[4,128,128]{2,1,0:T(8,128)} %param.13) | copy-start | bytes 786436
  54.8 320.6 %all-gather.2.cloned.1.call-start = ((), (), s32[]{:S(2)}) async-start(), calls=%async_computation.1 | async-start | bytes 4718592 | tf_op jit(solution)/shard_map/all_gather | solution.py:110
  292.4 6.2 copy-start.1
  292.4 6.2 copy-start.2
  292.4 6.2 copy-start.3
  292.4 6.2 copy-start.4
  293.1 6.0 copy-start.5
  299.2 84.7 %copy-start = (s32[4]{0:T(128)S(1)}, s32[4]{0:T(128)}, u32[]{:S(2)}) copy-start(s32[4]{0:T(128)} %constant.315) | copy-start | bytes 52
Sparse Core Ops, SparseCore 0:
  54.9 228.4 all-reduce.1
  298.8 76.5 all-gather.1
where the time goes:
time: 815 us; the launch traced here: 800 us
  waiting for transfers between devices  305 us (37%)
  local copies, waits for them, and re-layouts  239 us (29%)
  other arithmetic  220 us (27%)
  matrix products  22.6 us (3%)
  between operations  13.7 us (2%)
    psum x1, waiting for transfers between devices, body(): summed = lax.psum(partial_waves, 'beam')  228 us
    scatter x64, other arithmetic  217 us
    scatter x96, local copies, waits for them, and re-layouts  185 us
    all_gather x1, waiting for transfers between devices, body(): pieces = lax.all_gather(planes, 'pos', axis=0, tiled=True)  76.1 us
  transfers between devices with their start and end apart: 2, of which 2 were waited for; matrix products, arithmetic and copies ran while one was open for 0% of the time, Pallas kernels for 0%

commit v1 on v0

v1 whole, which is shorter than its diff:
```python
import math

import jax
import jax.numpy as jnp
import numpy as np
from jax import lax
from jax.experimental import pallas as pl
from jax.experimental.pallas import tpu as pltpu
from jax.sharding import Mesh
from jax.sharding import PartitionSpec as P

WIN = 128
FIELD_Y = 144
FIELD_X = 256
BANDS = 8
BAND = FIELD_Y // BANDS
BLOCK = 40
ROWS = 16
LIMIT = 48 * 1024 * 1024


def beam_weights(rows_y, cols_x, beam_index, amplitude, phase):
    wave_y = beam_index[:, 0]
    wave_x = beam_index[:, 1]
    turns = jnp.mod(
        rows_y[:, None] * wave_y[None, :] * FIELD_X + cols_x[:, None] * wave_x[None, :] * FIELD_Y,
        FIELD_Y * FIELD_X,
    )
    angles = phase[None, :] - 2.0 * math.pi / (FIELD_Y * FIELD_X) * turns.astype(jnp.float32)
    real_coef = (amplitude[None, :] * jnp.cos(angles)).astype(jnp.bfloat16)
    imag_coef = (amplitude[None, :] * jnp.sin(angles)).astype(jnp.bfloat16)
    return (real_coef, imag_coef)


def transform_tables():
    counter = np.arange(WIN)
    angles = 2.0 * np.pi / WIN * np.mod(counter[:, None] * counter[None, :], WIN)
    cos_table, sin_table = np.cos(angles) / math.sqrt(WIN), np.sin(angles) / math.sqrt(WIN)
    table = np.block([[cos_table, -sin_table], [sin_table, cos_table]]).astype(np.float32)
    pair = np.stack([table, table.T])
    high = pair.astype(jnp.bfloat16)
    low = (pair - high.astype(np.float32)).astype(jnp.bfloat16)
    return np.stack([high, low], axis=1)


def waves_kernel(oy_ref, ox_ref, coef_ref, s_ref, out_ref, mix_ref, full_ref):
    step = pl.program_id(0)
    outs, depth = coef_ref.shape

    @pl.when(step == 0)
    def _():
        wide = depth * ROWS
        source = lax.broadcasted_iota(jnp.int32, (depth, wide), 0)
        column = lax.broadcasted_iota(jnp.int32, (depth, wide), 1)
        k = column // ROWS
        pick = jnp.where(source == (k % 2) * (depth // 2) + k // 2, 1.0, 0.0).astype(jnp.bfloat16)
        coef = coef_ref[...].astype(jnp.float32)
        tall = jnp.broadcast_to(coef[:, None, :], (outs, ROWS, depth)).reshape(outs * ROWS, depth)
        spread = jnp.dot(tall.astype(jnp.bfloat16), pick, preferred_element_type=jnp.float32)
        row = lax.broadcasted_iota(jnp.int32, (outs * ROWS, wide), 0)
        column = lax.broadcasted_iota(jnp.int32, (outs * ROWS, wide), 1)
        mix_ref[...] = jnp.where(row % ROWS == column % ROWS, spread, 0.0).astype(jnp.bfloat16)

    part = jnp.dot(
        mix_ref[...],
        s_ref[...].reshape(depth * ROWS, FIELD_X),
        preferred_element_type=jnp.float32,
    )
    full_ref[:, pl.ds(pl.multiple_of(step * ROWS, ROWS), ROWS), :] = part.reshape(
        outs, ROWS, FIELD_X
    )

    @pl.when(step == pl.num_programs(0) - 1)
    def _():
        for slot in range(outs // 2):
            up = lax.rem(FIELD_Y - oy_ref[slot], FIELD_Y)
            left = lax.rem(FIELD_X - ox_ref[slot], FIELD_X)
            for plane in range(2):
                rows = pltpu.roll(full_ref[2 * slot + plane], up, 0)[:WIN]
                out_ref[slot, plane] = pltpu.roll(rows, left, 1)[:, :WIN]


def own_waves(s_flat, coef, rows_y, cols_x):
    depth = s_flat.shape[0]
    outs = coef.shape[0]
    return pl.pallas_call(
        waves_kernel,
        grid_spec=pltpu.PrefetchScalarGridSpec(
            num_scalar_prefetch=2,
            grid=(FIELD_Y // ROWS,),
            in_specs=[
                pl.BlockSpec((outs, depth), lambda i, *_: (0, 0)),
                pl.BlockSpec((depth, ROWS, FIELD_X), lambda i, *_: (0, i, 0)),
            ],
            out_specs=pl.BlockSpec((outs // 2, 2, WIN, WIN), lambda i, *_: (0, 0, 0, 0)),
            scratch_shapes=[
                pltpu.VMEM((outs * ROWS, depth * ROWS), jnp.bfloat16),
                pltpu.VMEM((outs, FIELD_Y, FIELD_X), jnp.float32),
            ],
        ),
        out_shape=jax.ShapeDtypeStruct((outs // 2, 2, WIN, WIN), jnp.float32),
        compiler_params=pltpu.CompilerParams(vmem_limit_bytes=LIMIT),
    )(rows_y, cols_x, coef, s_flat)


def split(value):
    high = value.astype(jnp.bfloat16)
    return high, (value - high.astype(jnp.float32)).astype(jnp.bfloat16)


def product(left, right):
    def dot(a, b):
        return jnp.dot(a, b, preferred_element_type=jnp.float32)

    return dot(left[0], right[0]) + (dot(left[1], right[0]) + dot(left[0], right[1]))


def misfit_kernel(info_ref, wave_ref, measured_ref, table_ref, out_ref, field_ref):
    forward = (table_ref[0, 0], table_ref[0, 1])
    inverse = (table_ref[1, 0], table_ref[1, 1])

    def side(value):
        return jnp.concatenate([value[:WIN], value[WIN:]], axis=1)

    def stack(value):
        return jnp.concatenate([value[:, :WIN], value[:, WIN:]], axis=0)

    wave = jnp.concatenate([wave_ref[0], wave_ref[1]], axis=1)
    far = product(inverse, split(stack(product(split(wave), forward))))
    far_real, far_imag = far[:WIN], far[WIN:]
    modulus = jnp.sqrt(far_real * far_real + far_imag * far_imag)
    factor = 1.0 - measured_ref[...] / jnp.maximum(modulus, 0.5)
    resid = jnp.concatenate([far_real * factor, far_imag * factor], axis=0)
    back = product(split(side(product(forward, split(resid)))), inverse)
    back = jnp.concatenate([back, jnp.zeros((FIELD_Y - WIN, 2 * WIN), jnp.float32)], axis=0)
    back = pltpu.roll(back, info_ref[1], 0)
    for plane in range(2):
        field_ref[plane] = back[:, plane * WIN : (plane + 1) * WIN]
    copies = out_ref.shape[1]
    zeros = jnp.zeros((BLOCK - 2 * BAND, WIN), jnp.float32)
    for band in range(BANDS):
        rows = slice(band * BAND, (band + 1) * BAND)
        block = jnp.concatenate([field_ref[0, rows], field_ref[1, rows], zeros], axis=0)
        for copy in range(copies):
            out_ref[band, copy] = block


def misfit_blocks(info, wave, measured, tables, copies):
    return pl.pallas_call(
        misfit_kernel,
        grid_spec=pltpu.PrefetchScalarGridSpec(
            num_scalar_prefetch=1,
            grid=(1,),
            in_specs=[
                pl.BlockSpec((2, WIN, WIN), lambda i, info: (0, 0, 0)),
                pl.BlockSpec((None, WIN, WIN), lambda i, info: (info[0], 0, 0)),
                pl.BlockSpec((2, 2, 2 * WIN, 2 * WIN), lambda i, info: (0, 0, 0, 0)),
            ],
            out_specs=pl.BlockSpec((BANDS, copies, BLOCK, WIN), lambda i, info: (0, 0, 0, 0)),
            scratch_shapes=[pltpu.VMEM((2, FIELD_Y, WIN), jnp.float32)],
        ),
        out_shape=jax.ShapeDtypeStruct((BANDS, copies, BLOCK, WIN), jnp.float32),
        compiler_params=pltpu.CompilerParams(vmem_limit_bytes=LIMIT),
    )(info, wave, measured, tables)


TILE = 8
TILES = -(-BAND // TILE)


def fold_kernel(ox_ref, weight_ref, own_ref, other_ref, out_ref, placed_ref):
    half = own_ref.shape[0]
    depth = weight_ref.shape[1]

    @pl.when(pl.program_id(0) == 0)
    def _():
        blank = jnp.zeros((TILES * TILE, FIELD_X - WIN), jnp.float32)
        for side, ref in enumerate((own_ref, other_ref)):
            for n in range(half):
                shift = ox_ref[side * half + n]
                planes = []
                for plane in range(2):
                    piece = ref[n, plane * BAND : min(plane * BAND + TILES * TILE, BLOCK), :]
                    short = TILES * TILE - piece.shape[0]
                    if short:
                        tail = jnp.zeros((short, WIN), jnp.float32)
                        piece = jnp.concatenate([piece, tail], axis=0)
                    planes.append(pltpu.roll(jnp.concatenate([piece, blank], axis=1), shift, 1))
                for t in range(TILES):
                    rows = slice(t * TILE, (t + 1) * TILE)
                    pair = jnp.concatenate([planes[0][rows], planes[1][rows]], axis=0)
                    at = (side * half + n) * 2 * TILE
                    placed_ref[t, at : at + 2 * TILE, :] = pair.astype(jnp.bfloat16)

    rows, wide = weight_ref.shape[0], depth * TILE
    source = lax.broadcasted_iota(jnp.int32, (depth, wide), 0)
    column = lax.broadcasted_iota(jnp.int32, (depth, wide), 1)
    pick = jnp.where(source == column // TILE, 1.0, 0.0).astype(jnp.bfloat16)
    weight = weight_ref[...].astype(jnp.float32)
    tall = jnp.broadcast_to(weight[:, None, :], (rows, TILE, depth)).reshape(rows * TILE, depth)
    spread = jnp.dot(tall.astype(jnp.bfloat16), pick, preferred_element_type=jnp.float32)
    row = lax.broadcasted_iota(jnp.int32, (rows * TILE, wide), 0)
    column = lax.broadcasted_iota(jnp.int32, (rows * TILE, wide), 1)
    kron = jnp.where(row % TILE == column % TILE, spread, 0.0).astype(jnp.bfloat16)
    for t in range(TILES):
        part = jnp.dot(kron, placed_ref[t], preferred_element_type=jnp.float32)
        part = part.reshape(rows, TILE, FIELD_X)
        left = min(TILE, BAND - t * TILE)
        out_ref[:, t * TILE : t * TILE + left, :] = part[:, :left]


def fold(cols_x, weights, own, other):
    rows, depth = weights.shape
    chunk = rows // 4
    half = own.shape[0]
    return pl.pallas_call(
        fold_kernel,
        grid_spec=pltpu.PrefetchScalarGridSpec(
            num_scalar_prefetch=1,
            grid=(rows // chunk,),
            in_specs=[
                pl.BlockSpec((chunk, depth), lambda i, *_: (i, 0)),
                pl.BlockSpec((half, BLOCK, WIN), lambda i, *_: (0, 0, 0)),
                pl.BlockSpec((half, BLOCK, WIN), lambda i, *_: (0, 0, 0)),
            ],
            out_specs=pl.BlockSpec((chunk, BAND, FIELD_X), lambda i, *_: (i, 0, 0)),
            scratch_shapes=[pltpu.VMEM((TILES, depth * TILE, FIELD_X), jnp.bfloat16)],
        ),
        out_shape=jax.ShapeDtypeStruct((rows, BAND, FIELD_X), jnp.float32),
        compiler_params=pltpu.CompilerParams(vmem_limit_bytes=LIMIT),
    )(cols_x, weights, own, other)


def swap(value, axis, pairs):
    both = [(a, b) for a, b in pairs] + [(b, a) for a, b in pairs]
    return lax.ppermute(value, axis, both)


def body(s_matrix, beam_index, amplitude, phase, offsets_y, offsets_x, measured):
    local_count = measured.shape[0]
    beams_here = s_matrix.shape[0]
    group = lax.axis_index("pos")
    core = lax.axis_index("core")
    lane = lax.axis_index("yl")
    depth = lax.axis_size("z")

    def slots(offsets):
        own = lax.dynamic_slice_in_dim(offsets, group * local_count, local_count).reshape(2, 2)
        own = jnp.where(core == 1, own[::-1], own)
        own = jnp.where(lane == 1, own[:, ::-1], own)
        return own.reshape(-1)

    own_y, own_x = slots(offsets_y), slots(offsets_x)
    real_coef, imag_coef = beam_weights(own_y, own_x, beam_index, amplitude, phase)
    upper = jnp.concatenate([real_coef, -imag_coef], axis=1)
    lower = jnp.concatenate([imag_coef, real_coef], axis=1)
    coef = jnp.stack([upper, lower], axis=1).reshape(2 * local_count, 2 * beams_here)
    s_flat = s_matrix.reshape(beams_here * 2, FIELD_Y, FIELD_X)
    waves = own_waves(s_flat, coef, own_y, own_x)

    pair = waves[:2] + swap(waves[2:], "core", [(0, 1)])
    total = pair[0] + swap(pair[1], "yl", [(0, 1)])
    for bit in (1, 2):
        total = total + swap(total, "z", [(i, i ^ bit) for i in range(depth) if not i & bit])
    total = total + swap(total, "z", [(i, depth - 1 - i) for i in range(depth // 2)])

    info = jnp.stack([2 * core + lane, own_y[0]]).astype(jnp.int32)
    copies = lax.axis_size("yl")
    blocks = misfit_blocks(info, total, measured, jnp.asarray(transform_tables()), copies)
    blocks = blocks.reshape(BANDS * copies, BLOCK, WIN)
    received = lax.all_to_all(blocks, ("pos", "yl"), 0, 0, tiled=True)
    other = swap(received, "core", [(0, 1)])

    def order(offsets):
        sides = offsets.reshape(BANDS, 2, 2).transpose(1, 0, 2)
        return jnp.where(core == 1, sides[::-1], sides).reshape(-1)

    all_y, all_x = order(offsets_y), order(offsets_x)
    real_coef, imag_coef = beam_weights(all_y, all_x, beam_index, amplitude, phase)
    real_coef, imag_coef = real_coef.T, imag_coef.T
    upper = jnp.stack([real_coef, imag_coef], axis=-1)
    lower = jnp.stack([-imag_coef, real_coef], axis=-1)
    weights = jnp.stack([upper, lower], axis=1).reshape(2 * beams_here, -1)
    gradient = fold(all_x, weights, received, other)
    return gradient.reshape(beams_here, 2, BAND, FIELD_X)


def solution(mesh):
    fine = Mesh(mesh.devices.reshape(8, 8, 2, 2), ("pos", "z", "yl", "core"))
    beam = ("z", "yl", "core")
    return jax.shard_map(
        body,
        mesh=fine,
        in_specs=(
            P(beam, None, None, None),
            P(beam, None),
            P(beam),
            P(beam),
            P(),
            P(),
            P("pos", None, None),
        ),
        out_specs=P(beam, None, "pos", None),
        check_vma=False,
    )
```

time: 815 us -> 72.9 us (0.09); the launches traced: 800 us -> 72.5 us
  waiting for transfers between devices: 305 us -> 24.6 us
  local copies, waits for them, and re-layouts: 239 us -> 9.58 us
  other arithmetic: 220 us -> 2.27 us
  matrix products: 22.6 us -> 0 us
  starting transfers between devices: 0.22 us -> 21.5 us
  Pallas kernels: 0 us -> 14.3 us
  between operations: 13.7 us -> 0.26 us
    psum x1 -> x0, waiting for transfers between devices: 228 us -> none  [body(): summed = lax.psum(partial_waves, 'beam')]
    scatter x65 -> x0, other arithmetic: 217 us -> none
    scatter x96 -> x0, local copies, waits for them, and re-layouts: 185 us -> none
    all_gather x1 -> x0, waiting for transfers between devices: 76.1 us -> none  [body(): pieces = lax.all_gather(planes, 'pos', axis=0, tiled=True)]
    dot_general x18 -> x0, matrix products: 22.6 us -> none  [the longest x1 6.21 us: all_waves(): jnp.dot(mixers, flat, preferred_element_type=jnp.float32)]
    ppermute x0 -> x6, waiting for transfers between devices: none -> 17.3 us  [swap(): return lax.ppermute(value, axis, both)]
    dot_general x2 -> x0, local copies, waits for them, and re-layouts: 15.8 us -> none  [the longest x1 12.6 us: all_waves(): jnp.dot(mixers, flat, preferred_element_type=jnp.float32)]
    ppermute x0 -> x6, starting transfers between devices: none -> 14.8 us  [swap(): return lax.ppermute(value, axis, both)]
  transfers between devices with their start and end apart: 2 -> 7, of which waited for: 2 -> 6; matrix products, arithmetic and copies ran while one was open for 0% -> 6% of each run, Pallas kernels for 0% -> 0%
where the time goes in v1:
time: 72.9 us; the launch traced here: 72.5 us
  waiting for transfers between devices  24.6 us (34%)
  starting transfers between devices  21.5 us (29%)
  Pallas kernels  14.3 us (20%)
  local copies, waits for them, and re-layouts  9.58 us (13%)
  other arithmetic  2.27 us (3%)
    ppermute x6, waiting for transfers between devices, swap(): return lax.ppermute(value, axis, both)  17.3 us
    ppermute x6, starting transfers between devices, swap(): return lax.ppermute(value, axis, both)  14.8 us
    pallas_call x1, Pallas kernels, own_waves(): pl.pallas_call(waves_kernel, grid_spec=pltpu.PrefetchScalarGridSpec(num_s...  9.19 us
    all_to_all x1, waiting for transfers between devices, body(): received = lax.all_to_all(blocks, ('pos', 'yl'), 0, 0, tiled=True)  7.27 us
    all_to_all x1, starting transfers between devices, body(): received = lax.all_to_all(blocks, ('pos', 'yl'), 0, 0, tiled=True)  6.75 us
    reshape x2, local copies, waits for them, and re-layouts, body(): weights = jnp.stack([upper, lower], axis=1).reshape(2 * beams_here, -1)  3.68 us
    pallas_call x1, Pallas kernels, fold(): pl.pallas_call(fold_kernel, grid_spec=pltpu.PrefetchScalarGridSpec(num_sc...  2.78 us
    reshape x1, local copies, waits for them, and re-layouts, body(): return gradient.reshape(beams_here, 2, BAND, FIELD_X)  2.62 us
  transfers between devices with their start and end apart: 7, of which 6 were waited for; matrix products, arithmetic and copies ran while one was open for 6% of the time, Pallas kernels for 0%

profile of v1, /device:TPU:1, one launch (start us, length us, event | category | flops | bytes accessed | tf_op | source)
XLA Modules:
  0.0 72.5 jit_solution(11001833361380155209)
XLA Ops:
  0.0 0.7 %dynamic_slice.6 = s32[4]{0:T(128)S(1)} dynamic-slice(s32[32]{0:T(128)} %param.12, s32[]{:T(128)S(6)} %select_n.74), dynamic_slice_sizes={4} | dynamic-slice | bytes 36 | tf_op jit(solution)/shard_map/dynamic_slice | solution.py:248
  0.7 0.7 %dynamic_slice.7 = s32[4]{0:T(128)S(1)} dynamic-slice(s32[32]{0:T(128)} %param.13, s32[]{:T(128)S(6)} %select_n.74), dynamic_slice_sizes={4} | dynamic-slice | bytes 36 | tf_op jit(solution)/shard_map/dynamic_slice | solution.py:248
  2.1 0.8 %slice_bitcast_fusion.3 = (s32[64]{0:T(128)S(1)}, s32[64]{0:T(128)S(1)}) fusion(s32[64,2]{0,1:T(2,128)} %param.9), kind=kLoop, calls=%fused_computation.35 | loop fusion | bytes 1024 | tf_op jit(solution)/shard_map/mul | solution.py:26
  2.8 0.8 %multiply_convert_fusion.3 = bf16[4,64]{1,0:T(4,128)(2,1)S(1)} fusion(f32[64]{0:T(128)} %param.10, s32[64]{0:T(128)S(1)} %get-tuple-element.14, s32[4]{0:T(128)S(1)} %reshape.548.ox_ref, s32[64]{0:T(128)S(1)} %get-tuple-element.13, s32[4]{0:T(128)S(1)} %reshape.546.oy_ref, f32[64]{0:T(128)} %param.11), kind=kLoop, calls=%fused_computation.25 | loop fusion | flops 4096 | bytes 1568 | tf_op jit(solution)/shard_map/convert_element_type | solution.py:30
  3.6 0.8 %fusion.11 = (bf16[4,64]{1,0:T(4,128)(2,1)S(1)}, bf16[4,64]{1,0:T(4,128)(2,1)S(1)}) fusion(s32[64]{0:T(128)S(1)} %get-tuple-element.14, s32[4]{0:T(128)S(1)} %reshape.548.ox_ref, s32[64]{0:T(128)S(1)} %get-tuple-element.13, s32[4]{0:T(128)S(1)} %reshape.546.oy_ref, f32[64]{0:T(128)} %param.11, f32[64]{0:T(128)} %param.10), kind=kLoop, calls=%fused_computation.37 | loop fusion | flops 4864 | bytes 2080 | tf_op jit(solution)/shard_map/neg | solution.py:255
  4.5 9.2 %shard_map.82 = f32[4,2,128,128]{3,2,1,0:T(8,128)S(1)} custom-call(s32[4]{0:T(128)S(1)} %reshape.546.oy_ref, s32[4]{0:T(128)S(1)} %reshape.548.ox_ref, bf16[8,128]{1,0:T(8,128)(2,1)S(1)} %bitcast.31, bf16[128,144,256]{2,1,0:T(8,128)(2,1)} %bitcast.33), custom_call_target="tpu_custom_call" | custom-call | tf_op jit(solution)/shard_map/pallas_call | solution.py:86
  13.8 3.3 %collective-permute-start = (f32[2,2,128,128]{3,2,1,0:T(8,128)S(1)}, f32[2,2,128,128]{3,2,1,0:T(8,128)S(1)}, u32[]{:S(2)}, u32[]{:S(2)}) collective-permute-start(f32[2,2,128,128]{3,2,1,0:T(8,128)S(1)} %slice.31), channel_id=1, source_target_pairs={{0,1},{1,0},{2,3},{3,2},{4,5},{5,4},{6,7},{7,6},{8,9},{9,8},{10,11... | collective-permute-start | bytes 786440 | tf_op jit(solution)/shard_map/ppermute | solution.py:236
  17.1 1.2 %collective-permute-done = f32[2,2,128,128]{3,2,1,0:T(8,128)S(1)} collective-permute-done((f32[2,2,128,128]{3,2,1,0:T(8,128)S(1)}, f32[2,2,128,128]{3,2,1,0:T(8,128)S(1)}, u32[]{:S(2)}, u32[]{:S(2)}) %collective-permute-start) | collective-permute-done | bytes 262176 | tf_op jit(solution)/shard_map/ppermute | solution.py:236
  18.4 4.7 %collective-permute-done.1 = f32[2,128,128]{2,1,0:T(8,128)S(1)} collective-permute-done((f32[2,128,128]{2,1,0:T(8,128)S(1)}, f32[2,128,128]{2,1,0:T(8,128)S(1)}, u32[]{:S(2)}, u32[]{:S(2)}) %collective-permute-start.1) | collective-permute-done | bytes 131104 | tf_op jit(solution)/shard_map/ppermute | solution.py:236
  23.3 3.8 %collective-permute-done.2 = f32[2,128,128]{2,1,0:T(8,128)S(1)} collective-permute-done((f32[2,128,128]{2,1,0:T(8,128)S(1)}, f32[2,128,128]{2,1,0:T(8,128)S(1)}, u32[]{:S(2)}, u32[]{:S(2)}) %collective-permute-start.2) | collective-permute-done | bytes 131104 | tf_op jit(solution)/shard_map/ppermute | solution.py:236
  27.1 1.5 %collective-permute-start.3 = (f32[2,128,128]{2,1,0:T(8,128)S(1)}, f32[2,128,128]{2,1,0:T(8,128)S(1)}, u32[]{:S(2)}, u32[]{:S(2)}) collective-permute-start(f32[2,128,128]{2,1,0:T(8,128)S(1)} %add.82), channel_id=1, source_target_pairs={{0,8},{4,12},{16,24},{20,28},{8,0},{12,4},{24,16},{28,20},{1,9},{5... | collective-permute-start | bytes 393224 | tf_op jit(solution)/shard_map/ppermute | solution.py:236
  28.6 4.7 %collective-permute-done.3 = f32[2,128,128]{2,1,0:T(8,128)S(1)} collective-permute-done((f32[2,128,128]{2,1,0:T(8,128)S(1)}, f32[2,128,128]{2,1,0:T(8,128)S(1)}, u32[]{:S(2)}, u32[]{:S(2)}) %collective-permute-start.3) | collective-permute-done | bytes 131104 | tf_op jit(solution)/shard_map/ppermute | solution.py:236
  33.3 3.9 %collective-permute-start.4 = (f32[2,128,128]{2,1,0:T(8,128)S(1)}, f32[2,128,128]{2,1,0:T(8,128)S(1)}, u32[]{:S(2)}, u32[]{:S(2)}) collective-permute-start(f32[2,128,128]{2,1,0:T(8,128)S(1)} %add.83), channel_id=1, source_target_pairs={{0,28},{4,24},{8,20},{12,16},{28,0},{24,4},{20,8},{16,12},{1,29},{... | collective-permute-start | bytes 393224 | tf_op jit(solution)/shard_map/ppermute | solution.py:236
  37.6 2.9 %collective-permute-done.4 = f32[2,128,128]{2,1,0:T(8,128)S(1)} collective-permute-done((f32[2,128,128]{2,1,0:T(8,128)S(1)}, f32[2,128,128]{2,1,0:T(8,128)S(1)}, u32[]{:S(2)}, u32[]{:S(2)}) %collective-permute-start.4) | collective-permute-done | bytes 131104 | tf_op jit(solution)/shard_map/ppermute | solution.py:236
  40.6 2.4 %shard_map.83 = f32[8,2,40,128]{3,2,1,0:T(8,128)} custom-call(s32[2]{0:T(128)S(1)} %pad_add_fusion.info_ref, f32[2,128,128]{2,1,0:T(8,128)S(1)} %add.84.wave_ref, f32[4,128,128]{2,1,0:T(8,128)S(1)} %copy-done.1, bf16[2,2,256,256]{3,2,1,0:T(8,128)(2,1)S(1)} %copy-done), custom_call_target="tpu_custom_call" | custom-call | tf_op jit(solution)/shard_map/pallas_call | solution.py:149
  43.0 6.7 %all-to-all-start = ((f32[16,40,128]{2,1,0:T(8,128)}), f32[16,40,128]{2,1,0:T(8,128)S(1)}, u32[]{:S(2)}, u32[]{:S(2)}) async-start(f32[16,40,128]{2,1,0:T(8,128)} %bitcast.13), calls=%async_computation | async-start | bytes 655360 | tf_op jit(solution)/shard_map/all_to_all | solution.py:271
  50.0 0.2 multiply_convert_fusion
  50.1 7.3 %all-to-all-done.own_ref = f32[16,40,128]{2,1,0:T(8,128)S(1)} async-done(((f32[16,40,128]{2,1,0:T(8,128)}), f32[16,40,128]{2,1,0:T(8,128)S(1)}, u32[]{:S(2)}, u32[]{:S(2)}) %all-to-all-start) | async-done | bytes 327712 | tf_op jit(solution)/shard_map/all_to_all | solution.py:271
  57.4 5.8 %collective-permute-start.5 = (f32[16,40,128]{2,1,0:T(8,128)S(1)}, f32[16,40,128]{2,1,0:T(8,128)S(1)}, u32[]{:S(2)}, u32[]{:S(2)}) collective-permute-start(f32[16,40,128]{2,1,0:T(8,128)S(1)} %all-to-all-done.own_ref), channel_id=1, source_target_pairs={{0,1},{1,0},{2,3},{3,2},{4,5},{5,4},{6,7},{7,6},{8,9},{9,8},{10,11... | collective-permute-start | bytes 983048 | tf_op jit(solution)/shard_map/ppermute | solution.py:236
  63.2 0.2 fusion.10
  63.4 1.8 %copy.26 = bf16[64,2,32,2]{3,2,1,0:T(8,128)(2,1)S(1)} copy(bf16[64,2,32,2]{0,2,3,1:T(8,128)(2,1)S(1)} %pad_maximum_fusion) | data formatting | bytes 32768 | tf_op jit(solution)/shard_map/reshape | solution.py:283
  65.2 1.9 %reshape.553.weight_ref = bf16[128,64]{1,0:T(8,128)(2,1)S(1)} reshape(bf16[64,2,32,2]{3,2,1,0:T(8,128)(2,1)S(1)} %copy.26) | data formatting | bytes 32768 | tf_op jit(solution)/shard_map/reshape | solution.py:283
  67.1 2.8 %shard_map.84 = f32[128,18,256]{2,1,0:T(8,128)S(1)} custom-call(s32[32]{0:T(128)S(1)} %reshape.542.ox_ref, bf16[128,64]{1,0:T(8,128)(2,1)S(1)} %reshape.553.weight_ref, f32[16,40,128]{2,1,0:T(8,128)S(1)} %all-to-all-done.own_ref, f32[16,40,128]{2,1,0:T(8,128)S(1)} %collective-permute-done.5.other_ref), custom_call_target="tpu_custom_call" | custom-call | tf_op jit(solution)/shard_map/pallas_call | solution.py:216
  69.9 2.6 %copy.25 = f32[64,2,18,256]{3,1,2,0:T(2,128)} copy(f32[64,2,18,256]{3,2,1,0:T(8,128)S(1)} %bitcast.30) | data formatting | bytes 4718592 | tf_op jit(solution)/shard_map/reshape | solution.py:285
  (48 shorter events, 1.6 us)
Async XLA Ops:
  4.5 32.7 %copy-start.4 = (s32[32]{0:T(128)S(1)}, s32[32]{0:T(128)}, u32[]{:S(2)}) copy-start(s32[32]{0:T(128)} %param.12) | copy-start | bytes 388
  4.5 32.8 %copy-start.5 = (s32[32]{0:T(128)S(1)}, s32[32]{0:T(128)}, u32[]{:S(2)}) copy-start(s32[32]{0:T(128)} %param.13) | copy-start | bytes 388
  13.7 26.9 %copy-start = (bf16[2,2,256,256]{3,2,1,0:T(8,128)(2,1)S(1)}, bf16[2,2,256,256]{3,2,1,0:T(8,128)(2,1)}, u32[]{:S(2)}) copy-start(bf16[2,2,256,256]{3,2,1,0:T(8,128)(2,1)} %constant.50.clone.table_ref) | copy-start | bytes 1572868
  13.8 26.8 %copy-start.1 = (f32[4,128,128]{2,1,0:T(8,128)S(1)}, f32[4,128,128]{2,1,0:T(8,128)}, u32[]{:S(2)}) copy-start(f32[4,128,128]{2,1,0:T(8,128)} %measured_ref.1) | copy-start | bytes 786436
  13.8 36.2 %copy-start.2 = (f32[64]{0:T(128)S(1)}, f32[64]{0:T(128)}, u32[]{:S(2)}) copy-start(f32[64]{0:T(128)} %param.11) | copy-start | bytes 772
  13.8 36.2 %copy-start.3 = (f32[64]{0:T(128)S(1)}, f32[64]{0:T(128)}, u32[]{:S(2)}) copy-start(f32[64]{0:T(128)} %param.10) | copy-start | bytes 772
  13.8 4.5 %collective-permute-start = (f32[2,2,128,128]{3,2,1,0:T(8,128)S(1)}, f32[2,2,128,128]{3,2,1,0:T(8,128)S(1)}, u32[]{:S(2)}, u32[]{:S(2)}) collective-permute-start(f32[2,2,128,128]{3,2,1,0:T(8,128)S(1)} %slice.31), channel_id=1, source_target_pairs={{0,1},{1,0},{2,3},{3,2},{4,5},{5,4},{6,7},{7,6},{8,9},{9,8},{10,11... | collective-permute-start | bytes 786440 | tf_op jit(solution)/shard_map/ppermute | solution.py:236
  18.3 4.8 %collective-permute-start.1 = (f32[2,128,128]{2,1,0:T(8,128)S(1)}, f32[2,128,128]{2,1,0:T(8,128)S(1)}, u32[]{:S(2)}, u32[]{:S(2)}) collective-permute-start(f32[2,128,128]{2,1,0:T(8,128)S(1)} %slice_bitcast_fusion), channel_id=1, source_target_pairs={{0,2},{2,0},{1,3},{3,1},{4,6},{6,4},{5,7},{7,5},{8,10},{10,8},{9,1... | collective-permute-start | bytes 393224 | tf_op jit(solution)/shard_map/ppermute | solution.py:236
  23.2 3.9 %collective-permute-start.2 = (f32[2,128,128]{2,1,0:T(8,128)S(1)}, f32[2,128,128]{2,1,0:T(8,128)S(1)}, u32[]{:S(2)}, u32[]{:S(2)}) collective-permute-start(f32[2,128,128]{2,1,0:T(8,128)S(1)} %fusion), channel_id=1, source_target_pairs={{0,4},{8,12},{16,20},{24,28},{4,0},{12,8},{20,16},{28,24},{1,5},{9... | collective-permute-start | bytes 393224 | tf_op jit(solution)/shard_map/ppermute | solution.py:236
  27.1 6.2 %collective-permute-start.3 = (f32[2,128,128]{2,1,0:T(8,128)S(1)}, f32[2,128,128]{2,1,0:T(8,128)S(1)}, u32[]{:S(2)}, u32[]{:S(2)}) collective-permute-start(f32[2,128,128]{2,1,0:T(8,128)S(1)} %add.82), channel_id=1, source_target_pairs={{0,8},{4,12},{16,24},{20,28},{8,0},{12,4},{24,16},{28,20},{1,9},{5... | collective-permute-start | bytes 393224 | tf_op jit(solution)/shard_map/ppermute | solution.py:236
  33.3 7.2 %collective-permute-start.4 = (f32[2,128,128]{2,1,0:T(8,128)S(1)}, f32[2,128,128]{2,1,0:T(8,128)S(1)}, u32[]{:S(2)}, u32[]{:S(2)}) collective-permute-start(f32[2,128,128]{2,1,0:T(8,128)S(1)} %add.83), channel_id=1, source_target_pairs={{0,28},{4,24},{8,20},{12,16},{28,0},{24,4},{20,8},{16,12},{1,29},{... | collective-permute-start | bytes 393224 | tf_op jit(solution)/shard_map/ppermute | solution.py:236
  43.0 14.4 %all-to-all-start = ((f32[16,40,128]{2,1,0:T(8,128)}), f32[16,40,128]{2,1,0:T(8,128)S(1)}, u32[]{:S(2)}, u32[]{:S(2)}) async-start(f32[16,40,128]{2,1,0:T(8,128)} %bitcast.13), calls=%async_computation | async-start | bytes 655360 | tf_op jit(solution)/shard_map/all_to_all | solution.py:271
  57.4 9.7 %collective-permute-start.5 = (f32[16,40,128]{2,1,0:T(8,128)S(1)}, f32[16,40,128]{2,1,0:T(8,128)S(1)}, u32[]{:S(2)}, u32[]{:S(2)}) collective-permute-start(f32[16,40,128]{2,1,0:T(8,128)S(1)} %all-to-all-done.own_ref), channel_id=1, source_target_pairs={{0,1},{1,0},{2,3},{3,2},{4,5},{5,4},{6,7},{7,6},{8,9},{9,8},{10,11... | collective-permute-start | bytes 983048 | tf_op jit(solution)/shard_map/ppermute | solution.py:236

commit v2 on v1

v2 whole, which is shorter than its diff:
```python
import math

import jax
import jax.numpy as jnp
import numpy as np
from jax import lax
from jax.experimental import pallas as pl
from jax.experimental.pallas import tpu as pltpu
from jax.sharding import Mesh
from jax.sharding import PartitionSpec as P

WIN = 128
FIELD_Y = 144
FIELD_X = 256
BANDS = 8
BAND = FIELD_Y // BANDS
BLOCK = 40
ROWS = 16
LIMIT = 48 * 1024 * 1024
WHOLE = 60 * 1024 * 1024


def beam_weights(rows_y, cols_x, beams):
    wave_y, wave_x, amplitude, phase = beams
    cells = FIELD_Y * FIELD_X
    count = rows_y * wave_y * FIELD_X + cols_x * wave_x * FIELD_Y
    whole = jnp.floor(count.astype(jnp.float32) * (1.0 / cells)).astype(jnp.int32)
    turns = count - whole * cells
    turns = jnp.where(turns < 0, turns + cells, turns)
    turns = jnp.where(turns >= cells, turns - cells, turns)
    angles = phase - 2.0 * math.pi / cells * turns.astype(jnp.float32)
    return amplitude * jnp.cos(angles), amplitude * jnp.sin(angles)


def places(count, offset_of, shape):
    row = lax.broadcasted_iota(jnp.int32, shape, 0)
    value = jnp.zeros(shape, jnp.int32)
    for n in range(count):
        value = jnp.where(row == n, offset_of(n), value)
    return value


def one_hot(condition):
    return jnp.where(condition, 1.0, 0.0).astype(jnp.bfloat16)


def iota2(shape):
    return [lax.broadcasted_iota(jnp.int32, shape, axis) for axis in range(2)]


def dot(left, right):
    return jnp.dot(left, right, preferred_element_type=jnp.float32)


def transform_tables():
    counter = np.arange(WIN)
    angles = 2.0 * np.pi / WIN * np.mod(counter[:, None] * counter[None, :], WIN)
    cos_table, sin_table = np.cos(angles) / math.sqrt(WIN), np.sin(angles) / math.sqrt(WIN)
    table = np.block([[cos_table, -sin_table], [sin_table, cos_table]]).astype(np.float32)
    pair = np.stack([table, table.T])
    high = pair.astype(jnp.bfloat16)
    low = (pair - high.astype(np.float32)).astype(jnp.bfloat16)
    return np.stack([high, low], axis=1)


def slot_position(slot):
    core = lax.axis_index("core") ^ (slot // 2)
    lane = lax.axis_index("yl") ^ (slot % 2)
    return lax.axis_index("pos") * 4 + 2 * core + lane


GROUPS = ((0, 6), (6, 9))


def waves_kernel(
    oy_hbm, ox_hbm, index_hbm, amplitude_hbm, phase_hbm, s_hbm,
    keep_ref, send_ref,
    oy_ref, ox_ref, index_ref, amplitude_ref, phase_ref, s_ref, mix_ref, full_ref, part_ref, small_sem, tile_sem,
):
    depth, tiles = s_ref.shape[0], FIELD_Y // ROWS
    beams = depth // 2
    small = [
        pltpu.make_async_copy(source, target, small_sem.at[i])
        for i, (source, target) in enumerate(
            [
                (oy_hbm, oy_ref),
                (ox_hbm, ox_ref),
                (index_hbm, index_ref),
                (amplitude_hbm, amplitude_ref),
                (phase_hbm, phase_ref),
            ]
        )
    ]
    large = []
    for i in range(tiles):
        rows = pl.ds(i * ROWS, ROWS)
        large.append(pltpu.make_async_copy(s_hbm.at[:, rows], s_ref.at[:, rows], tile_sem.at[i]))
    for copy in small + large:
        copy.start()

    outs, wide = 8, depth * ROWS
    source, column = iota2((beams, wide))
    same = source == column // (2 * ROWS)
    first = column % (2 * ROWS) < ROWS
    picks = [one_hot(same & first), one_hot(same & ~first)]
    for copy in small:
        copy.wait()
    slots = [slot_position(slot) for slot in range(4)]
    shape = (outs, beams)
    rows_y = places(outs, lambda n: oy_ref[slots[n // 2]], shape)
    cols_x = places(outs, lambda n: ox_ref[slots[n // 2]], shape)
    waves = [index_ref[0:1], index_ref[1:2], amplitude_ref[...], phase_ref[...]]
    real, imag = beam_weights(rows_y, cols_x, waves)
    is_real = iota2(shape)[0] % 2 == 0
    spread = jnp.zeros((outs * ROWS, wide), jnp.float32)
    for coef, pick in zip(
        (jnp.where(is_real, real, imag), jnp.where(is_real, -imag, real)), picks, strict=True
    ):
        tall = jnp.broadcast_to(coef[:, None, :], (outs, ROWS, beams)).reshape(outs * ROWS, beams)
        spread += dot(tall.astype(jnp.bfloat16), pick)
    row = lax.broadcasted_iota(jnp.int32, (outs * ROWS, 1), 0)
    moved = row
    for slot in range(4):
        moved += jnp.where(row // (2 * ROWS) == slot, oy_ref[slots[slot]], 0)
    column = iota2((outs * ROWS, wide))[1]
    mix_ref[...] = jnp.where(moved % ROWS == column % ROWS, spread, 0.0).astype(jnp.bfloat16)

    lefts = [lax.rem(FIELD_X - ox_ref[slots[slot]], FIELD_X) for slot in range(4)]

    def multiply(span):
        for i in range(*span):
            tile = s_ref[:, i * ROWS : (i + 1) * ROWS, :].reshape(wide, FIELD_X)
            full_ref[i] = dot(mix_ref[...], tile)

    def crop(span):
        for i in range(*span):
            for slot in range(4):
                both = full_ref[i, 2 * slot * ROWS : 2 * (slot + 1) * ROWS]
                part_ref[slot, i] = pltpu.roll(both, lefts[slot], 1)[:, :WIN]
        low, high = max(span[0] - 2, 0), span[1] - 2
        if span[1] == tiles:
            high = WIN // ROWS
        for slot in range(4):
            offset = oy_ref[slots[slot]]
            skip, rest = offset // ROWS, ROWS - offset % ROWS
            upper = iota2((2 * ROWS, WIN))[0] % ROWS < rest
            ref = (keep_ref, send_ref)[slot // 2]
            for u in range(low, high):
                after = jnp.minimum(u + skip + 1, tiles - 1)
                value = jnp.where(upper, part_ref[slot, u + skip], part_ref[slot, after])
                for plane in range(2):
                    rows = slice(u * ROWS, (u + 1) * ROWS)
                    ref[slot % 2, plane, rows] = value[plane * ROWS : (plane + 1) * ROWS]

    for number, span in enumerate(GROUPS):
        for i in range(*span):
            large[i].wait()
        multiply(span)
        if number:
            crop(GROUPS[number - 1])
    crop(GROUPS[-1])


def own_waves(s_flat, offsets_y, offsets_x, beams):
    depth = s_flat.shape[0]
    half = pltpu.VMEM((2, 2, WIN, WIN), jnp.float32)
    small = (offsets_y, offsets_x, *beams)
    operands = (*small, s_flat)
    return pl.pallas_call(
        waves_kernel,
        in_specs=[pl.BlockSpec(memory_space=pl.ANY)] * len(operands),
        out_specs=[pl.BlockSpec(memory_space=pltpu.VMEM)] * 2,
        out_shape=[half, half],
        scratch_shapes=[
            pltpu.SMEM(offsets_y.shape, jnp.int32),
            pltpu.SMEM(offsets_x.shape, jnp.int32),
            *[pltpu.VMEM(array.shape, array.dtype) for array in beams],
            pltpu.VMEM(s_flat.shape, s_flat.dtype),
            pltpu.VMEM((8 * ROWS, depth * ROWS), jnp.bfloat16),
            pltpu.VMEM((FIELD_Y // ROWS, 8 * ROWS, FIELD_X), jnp.float32),
            pltpu.VMEM((4, FIELD_Y // ROWS, 2 * ROWS, WIN), jnp.float32),
            pltpu.SemaphoreType.DMA((len(small),)),
            pltpu.SemaphoreType.DMA((FIELD_Y // ROWS,)),
        ],
        compiler_params=pltpu.CompilerParams(vmem_limit_bytes=WHOLE),
    )(*operands)


def split(value):
    high = value.astype(jnp.bfloat16)
    return high, (value - high.astype(jnp.float32)).astype(jnp.bfloat16)


def product(left, right):
    return dot(left[0], right[0]) + (dot(left[1], right[0]) + dot(left[0], right[1]))


def misfit_kernel(oy_ref, wave_ref, measured_ref, table_ref, out_ref, field_ref):
    forward = (table_ref[0, 0], table_ref[0, 1])
    inverse = (table_ref[1, 0], table_ref[1, 1])

    def side(value):
        return jnp.concatenate([value[:WIN], value[WIN:]], axis=1)

    def stack(value):
        return jnp.concatenate([value[:, :WIN], value[:, WIN:]], axis=0)

    wave = jnp.concatenate([wave_ref[0], wave_ref[1]], axis=1)
    far = product(inverse, split(stack(product(split(wave), forward))))
    far_real, far_imag = far[:WIN], far[WIN:]
    modulus = jnp.sqrt(far_real * far_real + far_imag * far_imag)
    factor = 1.0 - measured_ref[lax.rem(slot_position(0), 4)] / jnp.maximum(modulus, 0.5)
    resid = jnp.concatenate([far_real * factor, far_imag * factor], axis=0)
    back = product(split(side(product(forward, split(resid)))), inverse)
    back = jnp.concatenate([back, jnp.zeros((FIELD_Y - WIN, 2 * WIN), jnp.float32)], axis=0)
    back = pltpu.roll(back, oy_ref[slot_position(0)], 0)
    for plane in range(2):
        field_ref[plane] = back[:, plane * WIN : (plane + 1) * WIN]
    copies = out_ref.shape[1]
    zeros = jnp.zeros((BLOCK - 2 * BAND, WIN), jnp.float32)
    for band in range(BANDS):
        rows = slice(band * BAND, (band + 1) * BAND)
        block = jnp.concatenate([field_ref[0, rows], field_ref[1, rows], zeros], axis=0)
        for copy in range(copies):
            out_ref[band, copy] = block


def misfit_blocks(offsets_y, wave, measured, tables, copies):
    return pl.pallas_call(
        misfit_kernel,
        in_specs=[pl.BlockSpec(memory_space=pltpu.SMEM)] + [pl.BlockSpec(memory_space=pltpu.VMEM)] * 3,
        out_specs=pl.BlockSpec(memory_space=pltpu.VMEM),
        scratch_shapes=[pltpu.VMEM((2, FIELD_Y, WIN), jnp.float32)],
        out_shape=jax.ShapeDtypeStruct((BANDS, copies, BLOCK, WIN), jnp.float32),
        compiler_params=pltpu.CompilerParams(vmem_limit_bytes=LIMIT),
    )(offsets_y, wave, measured, tables)


TILE = 8
FULL = BAND // TILE
REST = BAND - FULL * TILE
HALF = 16
LINES = 2 * FIELD_X // WIN


def side_position(side, n):
    core = lax.axis_index("core") ^ side
    return n // 2 * 4 + 2 * core + n % 2


def spread_weights(coefs, size, row_parts, shape):
    count, beams = coefs[0].shape
    beam, plane, _ = row_parts((shape[0], beams))
    pick = one_hot(beam == iota2((shape[0], beams))[1])
    real, imag = [
        lax.dot_general(pick, coef, (((1,), (1,)), ((), ())), preferred_element_type=jnp.float32)
        for coef in coefs
    ]
    first = row_parts((shape[0], count))[1] == 0
    source, column = iota2((count, shape[1]))
    same = source == column // (2 * size)
    low = column % (2 * size) < size
    spread = dot(jnp.where(first, real, -imag).astype(jnp.bfloat16), one_hot(same & low))
    spread += dot(jnp.where(first, imag, real).astype(jnp.bfloat16), one_hot(same & ~low))
    equal = row_parts(shape)[2] == iota2(shape)[1] % size
    return jnp.where(equal, spread, 0.0).astype(jnp.bfloat16)


def weights_kernel(oy_ref, ox_ref, index_ref, amplitude_ref, phase_ref, full_ref, rest_ref):
    beams, count = index_ref.shape[1], 2 * HALF
    where = [side_position(n // HALF, n % HALF) for n in range(count)]
    shape = (count, beams)
    rows_y = places(count, lambda n: oy_ref[where[n]], shape)
    cols_x = places(count, lambda n: ox_ref[where[n]], shape)
    waves = [index_ref[0:1], index_ref[1:2], amplitude_ref[...], phase_ref[...]]
    coefs = [value.astype(jnp.bfloat16) for value in beam_weights(rows_y, cols_x, waves)]

    def full_parts(shape):
        row = iota2(shape)[0]
        return row // (2 * TILE), row // TILE % 2, row % TILE

    def rest_parts(shape):
        row = iota2(shape)[0]
        return row % beams, row // (beams * REST), row // beams % REST

    full_ref[...] = spread_weights(coefs, TILE, full_parts, full_ref.shape)
    rest_ref[...] = spread_weights(coefs, REST, rest_parts, rest_ref.shape)


def fold_weights(offsets_y, offsets_x, beams):
    rows, columns = 2 * beams[1].shape[1], 4 * HALF
    shapes = [(rows * size, columns * size) for size in (TILE, REST)]
    return pl.pallas_call(
        weights_kernel,
        in_specs=[pl.BlockSpec(memory_space=pltpu.SMEM)] * 2 + [pl.BlockSpec(memory_space=pltpu.VMEM)] * 3,
        out_specs=[pl.BlockSpec(memory_space=pltpu.VMEM)] * 2,
        out_shape=[jax.ShapeDtypeStruct(shape, jnp.bfloat16) for shape in shapes],
        compiler_params=pltpu.CompilerParams(vmem_limit_bytes=LIMIT),
        cost_estimate=pl.CostEstimate(flops=100000000, bytes_accessed=1000000, transcendentals=0),
    )(offsets_y, offsets_x, *beams)


PLACED = [(FULL, 2 * HALF * TILE, FIELD_X), (2 * HALF * REST, FIELD_X)]


def place(side, ox_ref, received_ref, full_ref, rest_ref):
    blank = jnp.zeros((2 * BAND, FIELD_X - WIN), jnp.float32)
    tails = []
    for n in range(HALF):
        shift = ox_ref[side_position(side, n)]
        both = jnp.concatenate([received_ref[n, : 2 * BAND, :], blank], axis=1)
        both = pltpu.roll(both, shift, 1)
        planes = [both[:BAND], both[BAND:]]
        for t in range(FULL):
            rows = slice(t * TILE, (t + 1) * TILE)
            pair = jnp.concatenate([planes[0][rows], planes[1][rows]], axis=0)
            full_ref[t, n * 2 * TILE : (n + 1) * 2 * TILE, :] = pair.astype(jnp.bfloat16)
        tails += [plane[FULL * TILE :] for plane in planes]
    rest_ref[...] = jnp.concatenate(tails, axis=0).astype(jnp.bfloat16)


def place_kernel(ox_ref, received_ref, full_ref, rest_ref):
    place(0, ox_ref, received_ref, full_ref, rest_ref)


def place_own(offsets_x, received):
    return pl.pallas_call(
        place_kernel,
        in_specs=[pl.BlockSpec(memory_space=pltpu.SMEM), pl.BlockSpec(memory_space=pltpu.VMEM)],
        out_specs=[pl.BlockSpec(memory_space=pltpu.VMEM)] * 2,
        out_shape=[jax.ShapeDtypeStruct(shape, jnp.bfloat16) for shape in PLACED],
        compiler_params=pltpu.CompilerParams(vmem_limit_bytes=LIMIT),
        cost_estimate=pl.CostEstimate(flops=1000000, bytes_accessed=1000000, transcendentals=0),
    )(offsets_x, received)


CHUNKS = 4


def fold_kernel(
    ox_ref, weight_ref, weight_rest_ref, own_ref, own_rest_ref, other_ref,
    out_hbm,
    full_ref, rest_ref, line_ref, sem,
):
    place(1, ox_ref, other_ref, full_ref, rest_ref)
    beams = weight_ref.shape[0] // (2 * TILE)
    length = BAND * LINES
    columns = [slice(side * WIN, (side + 1) * WIN) for side in range(FIELD_X // WIN)]

    half = own_rest_ref.shape[0]
    part = dot(weight_rest_ref[:, :half], own_rest_ref[...])
    part += dot(weight_rest_ref[:, half:], rest_ref[...])
    for group in range(2 * REST):
        plane, y = divmod(group, REST)
        value = part[group * beams : (group + 1) * beams]
        for side, column in enumerate(columns):
            start = (FULL * TILE + y) * LINES + 2 * side + plane
            line_ref[pl.ds(start, beams, stride=length), :] = value[:, column]

    half = own_ref.shape[1]
    rows, lines = weight_ref.shape[0] // CHUNKS, beams * length // CHUNKS
    copies = []
    for chunk in range(CHUNKS):
        for t in range(FULL):
            at = slice(chunk * rows, (chunk + 1) * rows)
            part = dot(weight_ref[at, :half], own_ref[t]) + dot(weight_ref[at, half:], full_ref[t])
            for group in range(rows // TILE):
                beam, plane = divmod(group, 2)
                value = part[group * TILE : (group + 1) * TILE]
                for side, column in enumerate(columns):
                    start = chunk * lines + beam * length + t * TILE * LINES + 2 * side + plane
                    line_ref[pl.ds(start, TILE, stride=LINES), :] = value[:, column]
        at = pl.ds(chunk * lines, lines)
        copy = pltpu.make_async_copy(line_ref.at[at], out_hbm.at[at], sem.at[chunk])
        copy.start()
        copies.append(copy)
    for copy in copies:
        copy.wait()


def fold(offsets_x, weights, own, other):
    lines = weights[0].shape[0] // (2 * TILE) * BAND * LINES
    operands = (*weights, *own, other)
    return pl.pallas_call(
        fold_kernel,
        in_specs=[pl.BlockSpec(memory_space=pltpu.SMEM)] + [pl.BlockSpec(memory_space=pltpu.VMEM)] * len(operands),
        out_specs=pl.BlockSpec(memory_space=pl.ANY),
        out_shape=jax.ShapeDtypeStruct((lines, WIN), jnp.float32),
        scratch_shapes=[
            *[pltpu.VMEM(shape, jnp.bfloat16) for shape in PLACED],
            pltpu.VMEM((lines, WIN), jnp.float32),
            pltpu.SemaphoreType.DMA((CHUNKS,)),
        ],
        compiler_params=pltpu.CompilerParams(vmem_limit_bytes=LIMIT),
    )(offsets_x, *operands)


def swap(value, axis, pairs):
    both = [(a, b) for a, b in pairs] + [(b, a) for a, b in pairs]
    return lax.ppermute(value, axis, both)


def body(s_matrix, beam_index, amplitude, phase, offsets_y, offsets_x, measured):
    beams_here = s_matrix.shape[0]
    depth = lax.axis_size("z")
    beams = (beam_index.T, amplitude[None, :], phase[None, :])
    s_flat = s_matrix.reshape(beams_here * 2, FIELD_Y, FIELD_X)

    keep, send = own_waves(s_flat, offsets_y, offsets_x, beams)
    pair = keep + swap(send, "core", [(0, 1)])
    total = pair[0] + swap(pair[1], "yl", [(0, 1)])
    weights = fold_weights(offsets_y, offsets_x, beams)
    for bit in (1, 2):
        other = swap(total, "z", [(i, i ^ bit) for i in range(depth) if not i & bit])
        if bit == 1:
            other, weights = lax.optimization_barrier((other, weights))
        total = total + other
    total = total + swap(total, "z", [(i, depth - 1 - i) for i in range(depth // 2)])

    copies = lax.axis_size("yl")
    blocks = misfit_blocks(offsets_y, total, measured, jnp.asarray(transform_tables()), copies)
    blocks = blocks.reshape(BANDS * copies, BLOCK, WIN)
    received = lax.all_to_all(blocks, ("pos", "yl"), 0, 0, tiled=True)
    other = swap(received, "core", [(0, 1)])
    own = place_own(offsets_x, received)
    lines = fold(offsets_x, weights, own, other)
    gradient = lines.reshape(beams_here, BAND, FIELD_X // WIN, 2, WIN).transpose(0, 3, 1, 2, 4)
    return gradient.reshape(beams_here, 2, BAND, FIELD_X)


def solution(mesh):
    fine = Mesh(mesh.devices.reshape(8, 8, 2, 2), ("pos", "z", "yl", "core"))
    beam = ("z", "yl", "core")
    return jax.shard_map(
        body,
        mesh=fine,
        in_specs=(
            P(beam, None, None, None),
            P(beam, None),
            P(beam),
            P(beam),
            P(),
            P(),
            P("pos", None, None),
        ),
        out_specs=P(beam, None, "pos", None),
        check_vma=False,
    )
```

time: 72.9 us -> 58.3 us (0.80)
  blocking collectives: 0 us -> 14.2 us
  local copies, waits for them, and re-layouts: 9.58 us -> 0.04 us
  waiting for transfers between devices: 24.6 us -> 16.4 us
  starting transfers between devices: 21.5 us -> 14.8 us
  other arithmetic: 2.27 us -> 0.11 us
  Pallas kernels: 14.3 us -> 12.4 us
    all_to_all x0 -> x1, blocking collectives: none -> 14.2 us  [body(): received = lax.all_to_all(blocks, ('pos', 'yl'), 0, 0, tiled=True)]
    all_to_all x1 -> x0, waiting for transfers between devices: 7.27 us -> none  [body(): received = lax.all_to_all(blocks, ('pos', 'yl'), 0, 0, tiled=True)]
    reshape x10 -> x0, local copies, waits for them, and re-layouts: 6.89 us -> none  [the longest x2 3.68 us: body(): weights = jnp.stack([upper, lower], axis=1).reshape(2 * beams_here, -1)]
    all_to_all x1 -> x0, starting transfers between devices: 6.75 us -> none  [body(): received = lax.all_to_all(blocks, ('pos', 'yl'), 0, 0, tiled=True)]
    pallas_call x3 -> x5, Pallas kernels: 14.3 us -> 12.4 us  [the longest x1 5.88 us: own_waves(): pl.pallas_call(waves_kernel, in_specs=[pl.BlockSpec(memory_space=pl.ANY)]...]
    dynamic_slice x2 -> x0, local copies, waits for them, and re-layouts: 1.45 us -> none  [slots(): lax.dynamic_slice_in_dim(offsets, group * local_count, local_count)]
    neg x2 -> x0, other arithmetic: 0.96 us -> none  [the longest x1 0.8 us: body(): upper = jnp.concatenate([real_coef, -imag_coef], axis=1)]
    convert_element_type x2 -> x0, other arithmetic: 0.96 us -> none  [the longest x1 0.8 us: beam_weights(): real_coef = (amplitude[None, :] * jnp.cos(angles)).astype(jnp.bfloat16)]
  transfers between devices with their start and end apart: 7 -> 6, of which waited for: 6 -> 6; matrix products, arithmetic and copies ran while one was open for 6% -> 0% of each run, Pallas kernels for 0% -> 4%
where the time goes in v2:
time: 58.3 us; the launch traced here: 58.2 us
  waiting for transfers between devices  16.4 us (28%)
  starting transfers between devices  14.8 us (25%)
  blocking collectives  14.2 us (24%)
  Pallas kernels  12.4 us (21%)
    ppermute x6, waiting for transfers between devices, swap(): return lax.ppermute(value, axis, both)  16.4 us
    ppermute x6, starting transfers between devices, swap(): return lax.ppermute(value, axis, both)  14.8 us
    all_to_all x1, blocking collectives, body(): received = lax.all_to_all(blocks, ('pos', 'yl'), 0, 0, tiled=True)  14.2 us
    pallas_call x1, Pallas kernels, own_waves(): pl.pallas_call(waves_kernel, in_specs=[pl.BlockSpec(memory_space=pl.ANY)]...  5.88 us
    pallas_call x1, Pallas kernels, fold(): pl.pallas_call(fold_kernel, in_specs=[pl.BlockSpec(memory_space=pltpu.SME...  2.46 us
    pallas_call x1, Pallas kernels, fold_weights(): pl.pallas_call(weights_kernel, in_specs=[pl.BlockSpec(memory_space=pltpu....  1.71 us
    pallas_call x1, Pallas kernels, misfit_blocks(): pl.pallas_call(misfit_kernel, in_specs=[pl.BlockSpec(memory_space=pltpu.S...  1.63 us
  transfers between devices with their start and end apart: 6, of which 6 were waited for; matrix products, arithmetic and copies ran while one was open for 0% of the time, Pallas kernels for 4%

profile of v2, /device:TPU:1, one launch (start us, length us, event | category | flops | bytes accessed | tf_op | source)
XLA Modules:
  0.0 58.2 jit_solution(17626405672378305943)
XLA Ops:
  0.0 0.0 copy-start.6
  0.0 0.0 copy-start.5
  0.0 0.0 copy-start.4
  0.0 0.0 copy-start.1
  0.0 5.9 %shard_map.82 = (f32[2,2,128,128]{3,2,1,0:T(8,128)S(1)}, f32[2,2,128,128]{3,2,1,0:T(8,128)S(1)}) custom-call(s32[32]{0:T(128)} %oy_ref.3, s32[32]{0:T(128)} %ox_ref.5, s32[2,64]{1,0:T(2,128)} %bitcast.17, f32[1,64]{1,0:T(1,128)} %bitcast.19, f32[1,64]{1,0:T(1,128)} %bitcast.21, bf16[128,144,256]{2,1,0:T(8,128)(2,1)} %bitcast.23), custom_call_target="tpu_custom_call" | custom-call | tf_op jit(solution)/shard_map/pallas_call | solution.py:169
  5.9 3.3 %collective-permute-start = (f32[2,2,128,128]{3,2,1,0:T(8,128)S(1)}, f32[2,2,128,128]{3,2,1,0:T(8,128)S(1)}, u32[]{:S(2)}, u32[]{:S(2)}) collective-permute-start(f32[2,2,128,128]{3,2,1,0:T(8,128)S(1)} %get-tuple-element.15), channel_id=1, source_target_pairs={{0,1},{1,0},{2,3},{3,2},{4,5},{5,4},{6,7},{7,6},{8,9},{9,8},{10,11... | collective-permute-start | bytes 786440 | tf_op jit(solution)/shard_map/ppermute | solution.py:400
  9.2 1.2 %collective-permute-done = f32[2,2,128,128]{3,2,1,0:T(8,128)S(1)} collective-permute-done((f32[2,2,128,128]{3,2,1,0:T(8,128)S(1)}, f32[2,2,128,128]{3,2,1,0:T(8,128)S(1)}, u32[]{:S(2)}, u32[]{:S(2)}) %collective-permute-start) | collective-permute-done | bytes 262176 | tf_op jit(solution)/shard_map/ppermute | solution.py:400
  10.4 0.1 collective-permute-start.1
  10.6 4.7 %collective-permute-done.1 = f32[2,128,128]{2,1,0:T(8,128)S(1)} collective-permute-done((f32[2,128,128]{2,1,0:T(8,128)S(1)}, f32[2,128,128]{2,1,0:T(8,128)S(1)}, u32[]{:S(2)}, u32[]{:S(2)}) %collective-permute-start.1) | collective-permute-done | bytes 131104 | tf_op jit(solution)/shard_map/ppermute | solution.py:400
  15.3 0.1 collective-permute-start.2
  15.4 0.0 copy-done.2
  15.4 0.0 copy-done.3
  15.4 1.7 %shard_map.83 = (bf16[1024,512]{1,0:T(8,128)(2,1)S(1)}, bf16[256,128]{1,0:T(8,128)(2,1)S(1)}) custom-call(s32[32]{0:T(128)S(1)} %copy-done.3, s32[32]{0:T(128)S(1)} %copy-done.2, s32[2,64]{1,0:T(2,128)S(1)} %bitcast.18, f32[1,64]{1,0:T(1,128)S(1)} %bitcast.20, f32[1,64]{1,0:T(1,128)S(1)} %bitcast.22), custom_call_target="tpu_custom_call" | custom-call | flops 100000000 | bytes 1000000 | tf_op jit(solution)/shard_map/pallas_call | solution.py:293
  17.1 2.0 %collective-permute-done.2 = f32[2,128,128]{2,1,0:T(8,128)S(1)} collective-permute-done((f32[2,128,128]{2,1,0:T(8,128)S(1)}, f32[2,128,128]{2,1,0:T(8,128)S(1)}, u32[]{:S(2)}, u32[]{:S(2)}) %collective-permute-start.2) | collective-permute-done | bytes 131104 | tf_op jit(solution)/shard_map/ppermute | solution.py:400
  19.2 1.6 %collective-permute-start.3 = (f32[2,128,128]{2,1,0:T(8,128)S(1)}, f32[2,128,128]{2,1,0:T(8,128)S(1)}, u32[]{:S(2)}, u32[]{:S(2)}) collective-permute-start(f32[2,128,128]{2,1,0:T(8,128)S(1)} %add.17), channel_id=1, source_target_pairs={{0,8},{4,12},{16,24},{20,28},{8,0},{12,4},{24,16},{28,20},{1,9},{5... | collective-permute-start | bytes 393224 | tf_op jit(solution)/shard_map/ppermute | solution.py:400
  20.8 4.7 %collective-permute-done.3 = f32[2,128,128]{2,1,0:T(8,128)S(1)} collective-permute-done((f32[2,128,128]{2,1,0:T(8,128)S(1)}, f32[2,128,128]{2,1,0:T(8,128)S(1)}, u32[]{:S(2)}, u32[]{:S(2)}) %collective-permute-start.3) | collective-permute-done | bytes 131104 | tf_op jit(solution)/shard_map/ppermute | solution.py:400
  25.4 4.0 %collective-permute-start.4 = (f32[2,128,128]{2,1,0:T(8,128)S(1)}, f32[2,128,128]{2,1,0:T(8,128)S(1)}, u32[]{:S(2)}, u32[]{:S(2)}) collective-permute-start(f32[2,128,128]{2,1,0:T(8,128)S(1)} %add.18), channel_id=1, source_target_pairs={{0,28},{4,24},{8,20},{12,16},{28,0},{24,4},{20,8},{16,12},{1,29},{... | collective-permute-start | bytes 393224 | tf_op jit(solution)/shard_map/ppermute | solution.py:400
  29.4 3.3 %collective-permute-done.4 = f32[2,128,128]{2,1,0:T(8,128)S(1)} collective-permute-done((f32[2,128,128]{2,1,0:T(8,128)S(1)}, f32[2,128,128]{2,1,0:T(8,128)S(1)}, u32[]{:S(2)}, u32[]{:S(2)}) %collective-permute-start.4) | collective-permute-done | bytes 131104 | tf_op jit(solution)/shard_map/ppermute | solution.py:400
  32.7 1.6 %shard_map.84 = f32[8,2,40,128]{3,2,1,0:T(8,128)S(1)} custom-call(s32[32]{0:T(128)S(1)} %copy-done.3, f32[2,128,128]{2,1,0:T(8,128)S(1)} %add.19.wave_ref, f32[4,128,128]{2,1,0:T(8,128)S(1)} %copy-done.1, bf16[2,2,256,256]{3,2,1,0:T(8,128)(2,1)S(1)} %copy-done), custom_call_target="tpu_custom_call" | custom-call | tf_op jit(solution)/shard_map/pallas_call | solution.py:229
  34.4 14.2 %all_to_all.5.received_ref = f32[16,40,128]{2,1,0:T(8,128)S(1)} all-to-all(f32[16,40,128]{2,1,0:T(8,128)S(1)} %bitcast.16), channel_id=1, replica_groups=mesh['pos'=8,'z'=8,'yl'=2,'core'=2] {'pos','yl'}, dimensions={0} | all-to-all | bytes 655360 | tf_op jit(solution)/shard_map/all_to_all | solution.py:423
  48.6 5.8 %collective-permute-start.5 = (f32[16,40,128]{2,1,0:T(8,128)S(1)}, f32[16,40,128]{2,1,0:T(8,128)S(1)}, u32[]{:S(2)}, u32[]{:S(2)}) collective-permute-start(f32[16,40,128]{2,1,0:T(8,128)S(1)} %all_to_all.5.received_ref), channel_id=1, source_target_pairs={{0,1},{1,0},{2,3},{3,2},{4,5},{5,4},{6,7},{7,6},{8,9},{9,8},{10,11... | collective-permute-start | bytes 983048 | tf_op jit(solution)/shard_map/ppermute | solution.py:400
  54.4 0.7 %shard_map.85 = (bf16[2,256,256]{2,1,0:T(8,128)(2,1)S(1)}, bf16[64,256]{1,0:T(8,128)(2,1)S(1)}) custom-call(s32[32]{0:T(128)S(1)} %copy-done.2, f32[16,40,128]{2,1,0:T(8,128)S(1)} %all_to_all.5.received_ref), custom_call_target="tpu_custom_call" | custom-call | flops 1000000 | bytes 1000000 | tf_op jit(solution)/shard_map/pallas_call | solution.py:327
  55.2 0.5 collective-permute-done.5.other_ref
  55.7 2.5 %shard_map.86 = f32[4608,128]{1,0:T(8,128)} custom-call(s32[32]{0:T(128)S(1)} %copy-done.2, bf16[1024,512]{1,0:T(8,128)(2,1)S(1)} %get-tuple-element.18.weight_ref, bf16[256,128]{1,0:T(8,128)(2,1)S(1)} %get-tuple-element.19.weight_rest_ref, bf16[2,256,256]{2,1,0:T(8,128)(2,1)S(1)} %get-tuple-element.21.own_ref, ...), custom_call_target="tpu_custom_call" | custom-call | tf_op jit(solution)/shard_map/pallas_call | solution.py:384
  (14 shorter events, 0.1 us)
Async XLA Ops:
  0.0 32.7 %copy-start = (bf16[2,2,256,256]{3,2,1,0:T(8,128)(2,1)S(1)}, bf16[2,2,256,256]{3,2,1,0:T(8,128)(2,1)}, u32[]{:S(2)}) copy-start(bf16[2,2,256,256]{3,2,1,0:T(8,128)(2,1)} %constant.2.clone.table_ref) | copy-start | bytes 1572868
  0.0 15.4 %copy-start.2 = (s32[32]{0:T(128)S(1)}, s32[32]{0:T(128)}, u32[]{:S(2)}) copy-start(s32[32]{0:T(128)} %ox_ref.5) | copy-start | bytes 388
  0.0 15.4 %copy-start.3 = (s32[32]{0:T(128)S(1)}, s32[32]{0:T(128)}, u32[]{:S(2)}) copy-start(s32[32]{0:T(128)} %oy_ref.3) | copy-start | bytes 388
  0.0 15.4 %copy-start.6 = (f32[64]{0:T(128)S(1)}, f32[64]{0:T(128)}, u32[]{:S(2)}) copy-start(f32[64]{0:T(128)} %param.11) | copy-start | bytes 772
  0.0 15.4 %copy-start.5 = (f32[64]{0:T(128)S(1)}, f32[64]{0:T(128)}, u32[]{:S(2)}) copy-start(f32[64]{0:T(128)} %param.10) | copy-start | bytes 772
  0.0 15.4 %copy-start.4 = (s32[64,2]{0,1:T(2,128)S(1)}, s32[64,2]{0,1:T(2,128)}, u32[]{:S(2)}) copy-start(s32[64,2]{0,1:T(2,128)} %param.9) | copy-start | bytes 1540
  0.0 32.7 %copy-start.1 = (f32[4,128,128]{2,1,0:T(8,128)S(1)}, f32[4,128,128]{2,1,0:T(8,128)}, u32[]{:S(2)}) copy-start(f32[4,128,128]{2,1,0:T(8,128)} %measured_ref.1) | copy-start | bytes 786436
  5.9 4.5 %collective-permute-start = (f32[2,2,128,128]{3,2,1,0:T(8,128)S(1)}, f32[2,2,128,128]{3,2,1,0:T(8,128)S(1)}, u32[]{:S(2)}, u32[]{:S(2)}) collective-permute-start(f32[2,2,128,128]{3,2,1,0:T(8,128)S(1)} %get-tuple-element.15), channel_id=1, source_target_pairs={{0,1},{1,0},{2,3},{3,2},{4,5},{5,4},{6,7},{7,6},{8,9},{9,8},{10,11... | collective-permute-start | bytes 786440 | tf_op jit(solution)/shard_map/ppermute | solution.py:400
  10.4 4.8 %collective-permute-start.1 = (f32[2,128,128]{2,1,0:T(8,128)S(1)}, f32[2,128,128]{2,1,0:T(8,128)S(1)}, u32[]{:S(2)}, u32[]{:S(2)}) collective-permute-start(f32[2,128,128]{2,1,0:T(8,128)S(1)} %slice_bitcast_fusion), channel_id=1, source_target_pairs={{0,2},{2,0},{1,3},{3,1},{4,6},{6,4},{5,7},{7,5},{8,10},{10,8},{9,1... | collective-permute-start | bytes 393224 | tf_op jit(solution)/shard_map/ppermute | solution.py:400
  15.3 3.9 %collective-permute-start.2 = (f32[2,128,128]{2,1,0:T(8,128)S(1)}, f32[2,128,128]{2,1,0:T(8,128)S(1)}, u32[]{:S(2)}, u32[]{:S(2)}) collective-permute-start(f32[2,128,128]{2,1,0:T(8,128)S(1)} %fusion), channel_id=1, source_target_pairs={{0,4},{8,12},{16,20},{24,28},{4,0},{12,8},{20,16},{28,24},{1,5},{9... | collective-permute-start | bytes 393224 | tf_op jit(solution)/shard_map/ppermute | solution.py:400
  19.2 6.2 %collective-permute-start.3 = (f32[2,128,128]{2,1,0:T(8,128)S(1)}, f32[2,128,128]{2,1,0:T(8,128)S(1)}, u32[]{:S(2)}, u32[]{:S(2)}) collective-permute-start(f32[2,128,128]{2,1,0:T(8,128)S(1)} %add.17), channel_id=1, source_target_pairs={{0,8},{4,12},{16,24},{20,28},{8,0},{12,4},{24,16},{28,20},{1,9},{5... | collective-permute-start | bytes 393224 | tf_op jit(solution)/shard_map/ppermute | solution.py:400
  25.4 7.3 %collective-permute-start.4 = (f32[2,128,128]{2,1,0:T(8,128)S(1)}, f32[2,128,128]{2,1,0:T(8,128)S(1)}, u32[]{:S(2)}, u32[]{:S(2)}) collective-permute-start(f32[2,128,128]{2,1,0:T(8,128)S(1)} %add.18), channel_id=1, source_target_pairs={{0,28},{4,24},{8,20},{12,16},{28,0},{24,4},{20,8},{16,12},{1,29},{... | collective-permute-start | bytes 393224 | tf_op jit(solution)/shard_map/ppermute | solution.py:400
  48.6 7.1 %collective-permute-start.5 = (f32[16,40,128]{2,1,0:T(8,128)S(1)}, f32[16,40,128]{2,1,0:T(8,128)S(1)}, u32[]{:S(2)}, u32[]{:S(2)}) collective-permute-start(f32[16,40,128]{2,1,0:T(8,128)S(1)} %all_to_all.5.received_ref), channel_id=1, source_target_pairs={{0,1},{1,0},{2,3},{3,2},{4,5},{5,4},{6,7},{7,6},{8,9},{9,8},{10,11... | collective-permute-start | bytes 983048 | tf_op jit(solution)/shard_map/ppermute | solution.py:400

commit v3 on v2

--- a/solution.py
+++ b/solution.py
@@ -69,7 +69,7 @@
     return lax.axis_index("pos") * 4 + 2 * core + lane
 
 
-GROUPS = ((0, 6), (6, 9))
+GROUPS = ((0, 5), (5, 9))
 
 
 def waves_kernel(
@@ -95,8 +95,10 @@
     for i in range(tiles):
         rows = pl.ds(i * ROWS, ROWS)
         large.append(pltpu.make_async_copy(s_hbm.at[:, rows], s_ref.at[:, rows], tile_sem.at[i]))
-    for copy in small + large:
+    for copy in small + large[: GROUPS[0][1]]:
         copy.start()
+    for copy in large[GROUPS[0][1] :]:
+        copy.start(priority=1)
 
     outs, wide = 8, depth * ROWS
     source, column = iota2((beams, wide))

time: 58.3 us -> 58 us (level)
  no operation moved by 1% of the time
where the time goes in v3:
time: 58 us; the launch traced here: 57.9 us
  waiting for transfers between devices  16.4 us (28%)
  starting transfers between devices  14.8 us (26%)
  blocking collectives  14.2 us (24%)
  Pallas kernels  12.2 us (21%)
    ppermute x6, waiting for transfers between devices, swap(): return lax.ppermute(value, axis, both)  16.4 us
    ppermute x6, starting transfers between devices, swap(): return lax.ppermute(value, axis, both)  14.8 us
    all_to_all x1, blocking collectives, body(): received = lax.all_to_all(blocks, ('pos', 'yl'), 0, 0, tiled=True)  14.2 us
    pallas_call x1, Pallas kernels, own_waves(): pl.pallas_call(waves_kernel, in_specs=[pl.BlockSpec(memory_space=pl.ANY)]...  5.66 us
    pallas_call x1, Pallas kernels, fold(): pl.pallas_call(fold_kernel, in_specs=[pl.BlockSpec(memory_space=pltpu.SME...  2.46 us
    pallas_call x1, Pallas kernels, fold_weights(): pl.pallas_call(weights_kernel, in_specs=[pl.BlockSpec(memory_space=pltpu....  1.71 us
    pallas_call x1, Pallas kernels, misfit_blocks(): pl.pallas_call(misfit_kernel, in_specs=[pl.BlockSpec(memory_space=pltpu.S...  1.63 us
  transfers between devices with their start and end apart: 6, of which 6 were waited for; matrix products, arithmetic and copies ran while one was open for 0% of the time, Pallas kernels for 4%

profile of v3, /device:TPU:1, one launch (start us, length us, event | category | flops | bytes accessed | tf_op | source)
XLA Modules:
  0.0 57.9 jit_solution(2850288453636681766)
XLA Ops:
  0.0 0.0 copy-start.6
  0.0 0.0 copy-start.5
  0.0 0.0 copy-start.4
  0.0 0.0 copy-start.1
  0.0 5.7 %shard_map.82 = (f32[2,2,128,128]{3,2,1,0:T(8,128)S(1)}, f32[2,2,128,128]{3,2,1,0:T(8,128)S(1)}) custom-call(s32[32]{0:T(128)} %oy_ref.3, s32[32]{0:T(128)} %ox_ref.5, s32[2,64]{1,0:T(2,128)} %bitcast.17, f32[1,64]{1,0:T(1,128)} %bitcast.19, f32[1,64]{1,0:T(1,128)} %bitcast.21, bf16[128,144,256]{2,1,0:T(8,128)(2,1)} %bitcast.23), custom_call_target="tpu_custom_call" | custom-call | tf_op jit(solution)/shard_map/pallas_call | solution.py:171
  5.7 3.3 %collective-permute-start = (f32[2,2,128,128]{3,2,1,0:T(8,128)S(1)}, f32[2,2,128,128]{3,2,1,0:T(8,128)S(1)}, u32[]{:S(2)}, u32[]{:S(2)}) collective-permute-start(f32[2,2,128,128]{3,2,1,0:T(8,128)S(1)} %get-tuple-element.15), channel_id=1, source_target_pairs={{0,1},{1,0},{2,3},{3,2},{4,5},{5,4},{6,7},{7,6},{8,9},{9,8},{10,11... | collective-permute-start | bytes 786440 | tf_op jit(solution)/shard_map/ppermute | solution.py:402
  9.0 1.2 %collective-permute-done = f32[2,2,128,128]{3,2,1,0:T(8,128)S(1)} collective-permute-done((f32[2,2,128,128]{3,2,1,0:T(8,128)S(1)}, f32[2,2,128,128]{3,2,1,0:T(8,128)S(1)}, u32[]{:S(2)}, u32[]{:S(2)}) %collective-permute-start) | collective-permute-done | bytes 262176 | tf_op jit(solution)/shard_map/ppermute | solution.py:402
  10.3 0.1 collective-permute-start.1
  10.4 4.7 %collective-permute-done.1 = f32[2,128,128]{2,1,0:T(8,128)S(1)} collective-permute-done((f32[2,128,128]{2,1,0:T(8,128)S(1)}, f32[2,128,128]{2,1,0:T(8,128)S(1)}, u32[]{:S(2)}, u32[]{:S(2)}) %collective-permute-start.1) | collective-permute-done | bytes 131104 | tf_op jit(solution)/shard_map/ppermute | solution.py:402
  15.1 0.1 collective-permute-start.2
  15.2 0.0 copy-done.2
  15.2 0.0 copy-done.3
  15.2 1.7 %shard_map.83 = (bf16[1024,512]{1,0:T(8,128)(2,1)S(1)}, bf16[256,128]{1,0:T(8,128)(2,1)S(1)}) custom-call(s32[32]{0:T(128)S(1)} %copy-done.3, s32[32]{0:T(128)S(1)} %copy-done.2, s32[2,64]{1,0:T(2,128)S(1)} %bitcast.18, f32[1,64]{1,0:T(1,128)S(1)} %bitcast.20, f32[1,64]{1,0:T(1,128)S(1)} %bitcast.22), custom_call_target="tpu_custom_call" | custom-call | flops 100000000 | bytes 1000000 | tf_op jit(solution)/shard_map/pallas_call | solution.py:295
  16.9 2.0 %collective-permute-done.2 = f32[2,128,128]{2,1,0:T(8,128)S(1)} collective-permute-done((f32[2,128,128]{2,1,0:T(8,128)S(1)}, f32[2,128,128]{2,1,0:T(8,128)S(1)}, u32[]{:S(2)}, u32[]{:S(2)}) %collective-permute-start.2) | collective-permute-done | bytes 131104 | tf_op jit(solution)/shard_map/ppermute | solution.py:402
  19.0 1.5 %collective-permute-start.3 = (f32[2,128,128]{2,1,0:T(8,128)S(1)}, f32[2,128,128]{2,1,0:T(8,128)S(1)}, u32[]{:S(2)}, u32[]{:S(2)}) collective-permute-start(f32[2,128,128]{2,1,0:T(8,128)S(1)} %add.17), channel_id=1, source_target_pairs={{0,8},{4,12},{16,24},{20,28},{8,0},{12,4},{24,16},{28,20},{1,9},{5... | collective-permute-start | bytes 393224 | tf_op jit(solution)/shard_map/ppermute | solution.py:402
  20.5 4.7 %collective-permute-done.3 = f32[2,128,128]{2,1,0:T(8,128)S(1)} collective-permute-done((f32[2,128,128]{2,1,0:T(8,128)S(1)}, f32[2,128,128]{2,1,0:T(8,128)S(1)}, u32[]{:S(2)}, u32[]{:S(2)}) %collective-permute-start.3) | collective-permute-done | bytes 131104 | tf_op jit(solution)/shard_map/ppermute | solution.py:402
  25.2 3.9 %collective-permute-start.4 = (f32[2,128,128]{2,1,0:T(8,128)S(1)}, f32[2,128,128]{2,1,0:T(8,128)S(1)}, u32[]{:S(2)}, u32[]{:S(2)}) collective-permute-start(f32[2,128,128]{2,1,0:T(8,128)S(1)} %add.18), channel_id=1, source_target_pairs={{0,28},{4,24},{8,20},{12,16},{28,0},{24,4},{20,8},{16,12},{1,29},{... | collective-permute-start | bytes 393224 | tf_op jit(solution)/shard_map/ppermute | solution.py:402
  29.2 3.3 %collective-permute-done.4 = f32[2,128,128]{2,1,0:T(8,128)S(1)} collective-permute-done((f32[2,128,128]{2,1,0:T(8,128)S(1)}, f32[2,128,128]{2,1,0:T(8,128)S(1)}, u32[]{:S(2)}, u32[]{:S(2)}) %collective-permute-start.4) | collective-permute-done | bytes 131104 | tf_op jit(solution)/shard_map/ppermute | solution.py:402
  32.5 1.6 %shard_map.84 = f32[8,2,40,128]{3,2,1,0:T(8,128)S(1)} custom-call(s32[32]{0:T(128)S(1)} %copy-done.3, f32[2,128,128]{2,1,0:T(8,128)S(1)} %add.19.wave_ref, f32[4,128,128]{2,1,0:T(8,128)S(1)} %copy-done.1, bf16[2,2,256,256]{3,2,1,0:T(8,128)(2,1)S(1)} %copy-done), custom_call_target="tpu_custom_call" | custom-call | tf_op jit(solution)/shard_map/pallas_call | solution.py:231
  34.2 14.2 %all_to_all.5.received_ref = f32[16,40,128]{2,1,0:T(8,128)S(1)} all-to-all(f32[16,40,128]{2,1,0:T(8,128)S(1)} %bitcast.16), channel_id=1, replica_groups=mesh['pos'=8,'z'=8,'yl'=2,'core'=2] {'pos','yl'}, dimensions={0} | all-to-all | bytes 655360 | tf_op jit(solution)/shard_map/all_to_all | solution.py:425
  48.4 5.8 %collective-permute-start.5 = (f32[16,40,128]{2,1,0:T(8,128)S(1)}, f32[16,40,128]{2,1,0:T(8,128)S(1)}, u32[]{:S(2)}, u32[]{:S(2)}) collective-permute-start(f32[16,40,128]{2,1,0:T(8,128)S(1)} %all_to_all.5.received_ref), channel_id=1, source_target_pairs={{0,1},{1,0},{2,3},{3,2},{4,5},{5,4},{6,7},{7,6},{8,9},{9,8},{10,11... | collective-permute-start | bytes 983048 | tf_op jit(solution)/shard_map/ppermute | solution.py:402
  54.2 0.7 %shard_map.85 = (bf16[2,256,256]{2,1,0:T(8,128)(2,1)S(1)}, bf16[64,256]{1,0:T(8,128)(2,1)S(1)}) custom-call(s32[32]{0:T(128)S(1)} %copy-done.2, f32[16,40,128]{2,1,0:T(8,128)S(1)} %all_to_all.5.received_ref), custom_call_target="tpu_custom_call" | custom-call | flops 1000000 | bytes 1000000 | tf_op jit(solution)/shard_map/pallas_call | solution.py:329
  54.9 0.5 collective-permute-done.5.other_ref
  55.5 2.5 %shard_map.86 = f32[4608,128]{1,0:T(8,128)} custom-call(s32[32]{0:T(128)S(1)} %copy-done.2, bf16[1024,512]{1,0:T(8,128)(2,1)S(1)} %get-tuple-element.18.weight_ref, bf16[256,128]{1,0:T(8,128)(2,1)S(1)} %get-tuple-element.19.weight_rest_ref, bf16[2,256,256]{2,1,0:T(8,128)(2,1)S(1)} %get-tuple-element.21.own_ref, ...), custom_call_target="tpu_custom_call" | custom-call | tf_op jit(solution)/shard_map/pallas_call | solution.py:386
  (14 shorter events, 0.1 us)
Async XLA Ops:
  0.0 32.5 %copy-start = (bf16[2,2,256,256]{3,2,1,0:T(8,128)(2,1)S(1)}, bf16[2,2,256,256]{3,2,1,0:T(8,128)(2,1)}, u32[]{:S(2)}) copy-start(bf16[2,2,256,256]{3,2,1,0:T(8,128)(2,1)} %constant.2.clone.table_ref) | copy-start | bytes 1572868
  0.0 15.2 %copy-start.2 = (s32[32]{0:T(128)S(1)}, s32[32]{0:T(128)}, u32[]{:S(2)}) copy-start(s32[32]{0:T(128)} %ox_ref.5) | copy-start | bytes 388
  0.0 15.2 %copy-start.3 = (s32[32]{0:T(128)S(1)}, s32[32]{0:T(128)}, u32[]{:S(2)}) copy-start(s32[32]{0:T(128)} %oy_ref.3) | copy-start | bytes 388
  0.0 15.2 %copy-start.6 = (f32[64]{0:T(128)S(1)}, f32[64]{0:T(128)}, u32[]{:S(2)}) copy-start(f32[64]{0:T(128)} %param.11) | copy-start | bytes 772
  0.0 15.2 %copy-start.5 = (f32[64]{0:T(128)S(1)}, f32[64]{0:T(128)}, u32[]{:S(2)}) copy-start(f32[64]{0:T(128)} %param.10) | copy-start | bytes 772
  0.0 15.2 %copy-start.4 = (s32[64,2]{0,1:T(2,128)S(1)}, s32[64,2]{0,1:T(2,128)}, u32[]{:S(2)}) copy-start(s32[64,2]{0,1:T(2,128)} %param.9) | copy-start | bytes 1540
  0.0 32.5 %copy-start.1 = (f32[4,128,128]{2,1,0:T(8,128)S(1)}, f32[4,128,128]{2,1,0:T(8,128)}, u32[]{:S(2)}) copy-start(f32[4,128,128]{2,1,0:T(8,128)} %measured_ref.1) | copy-start | bytes 786436
  5.7 4.5 %collective-permute-start = (f32[2,2,128,128]{3,2,1,0:T(8,128)S(1)}, f32[2,2,128,128]{3,2,1,0:T(8,128)S(1)}, u32[]{:S(2)}, u32[]{:S(2)}) collective-permute-start(f32[2,2,128,128]{3,2,1,0:T(8,128)S(1)} %get-tuple-element.15), channel_id=1, source_target_pairs={{0,1},{1,0},{2,3},{3,2},{4,5},{5,4},{6,7},{7,6},{8,9},{9,8},{10,11... | collective-permute-start | bytes 786440 | tf_op jit(solution)/shard_map/ppermute | solution.py:402
  10.3 4.8 %collective-permute-start.1 = (f32[2,128,128]{2,1,0:T(8,128)S(1)}, f32[2,128,128]{2,1,0:T(8,128)S(1)}, u32[]{:S(2)}, u32[]{:S(2)}) collective-permute-start(f32[2,128,128]{2,1,0:T(8,128)S(1)} %slice_bitcast_fusion), channel_id=1, source_target_pairs={{0,2},{2,0},{1,3},{3,1},{4,6},{6,4},{5,7},{7,5},{8,10},{10,8},{9,1... | collective-permute-start | bytes 393224 | tf_op jit(solution)/shard_map/ppermute | solution.py:402
  15.1 3.9 %collective-permute-start.2 = (f32[2,128,128]{2,1,0:T(8,128)S(1)}, f32[2,128,128]{2,1,0:T(8,128)S(1)}, u32[]{:S(2)}, u32[]{:S(2)}) collective-permute-start(f32[2,128,128]{2,1,0:T(8,128)S(1)} %fusion), channel_id=1, source_target_pairs={{0,4},{8,12},{16,20},{24,28},{4,0},{12,8},{20,16},{28,24},{1,5},{9... | collective-permute-start | bytes 393224 | tf_op jit(solution)/shard_map/ppermute | solution.py:402
  19.0 6.2 %collective-permute-start.3 = (f32[2,128,128]{2,1,0:T(8,128)S(1)}, f32[2,128,128]{2,1,0:T(8,128)S(1)}, u32[]{:S(2)}, u32[]{:S(2)}) collective-permute-start(f32[2,128,128]{2,1,0:T(8,128)S(1)} %add.17), channel_id=1, source_target_pairs={{0,8},{4,12},{16,24},{20,28},{8,0},{12,4},{24,16},{28,20},{1,9},{5... | collective-permute-start | bytes 393224 | tf_op jit(solution)/shard_map/ppermute | solution.py:402
  25.2 7.2 %collective-permute-start.4 = (f32[2,128,128]{2,1,0:T(8,128)S(1)}, f32[2,128,128]{2,1,0:T(8,128)S(1)}, u32[]{:S(2)}, u32[]{:S(2)}) collective-permute-start(f32[2,128,128]{2,1,0:T(8,128)S(1)} %add.18), channel_id=1, source_target_pairs={{0,28},{4,24},{8,20},{12,16},{28,0},{24,4},{20,8},{16,12},{1,29},{... | collective-permute-start | bytes 393224 | tf_op jit(solution)/shard_map/ppermute | solution.py:402
  48.4 7.1 %collective-permute-start.5 = (f32[16,40,128]{2,1,0:T(8,128)S(1)}, f32[16,40,128]{2,1,0:T(8,128)S(1)}, u32[]{:S(2)}, u32[]{:S(2)}) collective-permute-start(f32[16,40,128]{2,1,0:T(8,128)S(1)} %all_to_all.5.received_ref), channel_id=1, source_target_pairs={{0,1},{1,0},{2,3},{3,2},{4,5},{5,4},{6,7},{7,6},{8,9},{9,8},{10,11... | collective-permute-start | bytes 983048 | tf_op jit(solution)/shard_map/ppermute | solution.py:402

commit v4 on v3

--- a/solution.py
+++ b/solution.py
@@ -69,13 +69,14 @@
     return lax.axis_index("pos") * 4 + 2 * core + lane
 
 
-GROUPS = ((0, 5), (5, 9))
+PIECE = 16
+FIRST = 4
 
 
 def waves_kernel(
     oy_hbm, ox_hbm, index_hbm, amplitude_hbm, phase_hbm, s_hbm,
     keep_ref, send_ref,
-    oy_ref, ox_ref, index_ref, amplitude_ref, phase_ref, s_ref, mix_ref, full_ref, part_ref, small_sem, tile_sem,
+    oy_ref, ox_ref, index_ref, amplitude_ref, phase_ref, s_ref, mix_ref, full_ref, part_ref, small_sem, piece_sem,
 ):
     depth, tiles = s_ref.shape[0], FIELD_Y // ROWS
     beams = depth // 2
@@ -92,12 +93,12 @@
         )
     ]
     large = []
-    for i in range(tiles):
-        rows = pl.ds(i * ROWS, ROWS)
-        large.append(pltpu.make_async_copy(s_hbm.at[:, rows], s_ref.at[:, rows], tile_sem.at[i]))
-    for copy in small + large[: GROUPS[0][1]]:
+    for i in range(depth // PIECE):
+        planes = pl.ds(i * PIECE, PIECE)
+        large.append(pltpu.make_async_copy(s_hbm.at[planes], s_ref.at[planes], piece_sem.at[i]))
+    for copy in small + large[:FIRST]:
         copy.start()
-    for copy in large[GROUPS[0][1] :]:
+    for copy in large[FIRST:]:
         copy.start(priority=1)
 
     outs, wide = 8, depth * ROWS
@@ -129,38 +130,40 @@
 
     lefts = [lax.rem(FIELD_X - ox_ref[slots[slot]], FIELD_X) for slot in range(4)]
 
-    def multiply(span):
-        for i in range(*span):
-            tile = s_ref[:, i * ROWS : (i + 1) * ROWS, :].reshape(wide, FIELD_X)
-            full_ref[i] = dot(mix_ref[...], tile)
-
-    def crop(span):
-        for i in range(*span):
-            for slot in range(4):
-                both = full_ref[i, 2 * slot * ROWS : 2 * (slot + 1) * ROWS]
-                part_ref[slot, i] = pltpu.roll(both, lefts[slot], 1)[:, :WIN]
-        low, high = max(span[0] - 2, 0), span[1] - 2
-        if span[1] == tiles:
-            high = WIN // ROWS
+    def multiply(i, low, high):
+        tile = s_ref[low:high, i * ROWS : (i + 1) * ROWS, :].reshape((high - low) * ROWS, FIELD_X)
+        return dot(mix_ref[:, low * ROWS : high * ROWS], tile)
+
+    def crop_columns(i):
+        for slot in range(4):
+            both = full_ref[i, 2 * slot * ROWS : 2 * (slot + 1) * ROWS]
+            part_ref[slot, i] = pltpu.roll(both, lefts[slot], 1)[:, :WIN]
+
+    def crop_rows(u):
         for slot in range(4):
             offset = oy_ref[slots[slot]]
             skip, rest = offset // ROWS, ROWS - offset % ROWS
             upper = iota2((2 * ROWS, WIN))[0] % ROWS < rest
+            after = jnp.minimum(u + skip + 1, tiles - 1)
+            value = jnp.where(upper, part_ref[slot, u + skip], part_ref[slot, after])
             ref = (keep_ref, send_ref)[slot // 2]
-            for u in range(low, high):
-                after = jnp.minimum(u + skip + 1, tiles - 1)
-                value = jnp.where(upper, part_ref[slot, u + skip], part_ref[slot, after])
-                for plane in range(2):
-                    rows = slice(u * ROWS, (u + 1) * ROWS)
-                    ref[slot % 2, plane, rows] = value[plane * ROWS : (plane + 1) * ROWS]
-
-    for number, span in enumerate(GROUPS):
-        for i in range(*span):
-            large[i].wait()
-        multiply(span)
-        if number:
-            crop(GROUPS[number - 1])
-    crop(GROUPS[-1])
+            for plane in range(2):
+                rows = slice(u * ROWS, (u + 1) * ROWS)
+                ref[slot % 2, plane, rows] = value[plane * ROWS : (plane + 1) * ROWS]
+
+    middle = FIRST * PIECE
+    for copy in large[:FIRST]:
+        copy.wait()
+    for i in range(tiles):
+        full_ref[i] = multiply(i, 0, middle)
+    for copy in large[FIRST:]:
+        copy.wait()
+    for i in range(tiles):
+        full_ref[i] += multiply(i, middle, depth)
+        crop_columns(i)
+        if i >= 2:
+            crop_rows(i - 2)
+    crop_rows(tiles - 2)
 
 
 def own_waves(s_flat, offsets_y, offsets_x, beams):
@@ -182,7 +185,7 @@
             pltpu.VMEM((FIELD_Y // ROWS, 8 * ROWS, FIELD_X), jnp.float32),
             pltpu.VMEM((4, FIELD_Y // ROWS, 2 * ROWS, WIN), jnp.float32),
             pltpu.SemaphoreType.DMA((len(small),)),
-            pltpu.SemaphoreType.DMA((FIELD_Y // ROWS,)),
+            pltpu.SemaphoreType.DMA((depth // PIECE,)),
         ],
         compiler_params=pltpu.CompilerParams(vmem_limit_bytes=WHOLE),
     )(*operands)
@@ -390,7 +393,7 @@
         out_shape=jax.ShapeDtypeStruct((lines, WIN), jnp.float32),
         scratch_shapes=[
             *[pltpu.VMEM(shape, jnp.bfloat16) for shape in PLACED],
-            pltpu.VMEM((lines, WIN), jnp.float32),
+            pltpu.VMEM((lines + BAND * LINES, WIN), jnp.float32),
             pltpu.SemaphoreType.DMA((CHUNKS,)),
         ],
         compiler_params=pltpu.CompilerParams(vmem_limit_bytes=LIMIT),

time: 58 us -> 57.8 us (level)
  no operation moved by 1% of the time
where the time goes in v4:
time: 57.8 us; the launch traced here: 57.7 us
  waiting for transfers between devices  16.4 us (28%)
  starting transfers between devices  14.8 us (26%)
  blocking collectives  14.2 us (25%)
  Pallas kernels  11.9 us (21%)
    ppermute x6, waiting for transfers between devices, swap(): return lax.ppermute(value, axis, both)  16.4 us
    ppermute x6, starting transfers between devices, swap(): return lax.ppermute(value, axis, both)  14.8 us
    all_to_all x1, blocking collectives, body(): received = lax.all_to_all(blocks, ('pos', 'yl'), 0, 0, tiled=True)  14.2 us
    pallas_call x1, Pallas kernels, own_waves(): pl.pallas_call(waves_kernel, in_specs=[pl.BlockSpec(memory_space=pl.ANY)]...  5.4 us
    pallas_call x1, Pallas kernels, fold(): pl.pallas_call(fold_kernel, in_specs=[pl.BlockSpec(memory_space=pltpu.SME...  2.46 us
    pallas_call x1, Pallas kernels, fold_weights(): pl.pallas_call(weights_kernel, in_specs=[pl.BlockSpec(memory_space=pltpu....  1.72 us
    pallas_call x1, Pallas kernels, misfit_blocks(): pl.pallas_call(misfit_kernel, in_specs=[pl.BlockSpec(memory_space=pltpu.S...  1.63 us
  transfers between devices with their start and end apart: 6, of which 6 were waited for; matrix products, arithmetic and copies ran while one was open for 0% of the time, Pallas kernels for 4%

profile of v4, /device:TPU:1, one launch (start us, length us, event | category | flops | bytes accessed | tf_op | source)
XLA Modules:
  0.0 57.7 jit_solution(355437257932688196)
XLA Ops:
  0.0 0.0 copy-start.6
  0.0 5.4 %shard_map.82 = (f32[2,2,128,128]{3,2,1,0:T(8,128)S(1)}, f32[2,2,128,128]{3,2,1,0:T(8,128)S(1)}) custom-call(s32[32]{0:T(128)} %oy_ref.3, s32[32]{0:T(128)} %ox_ref.5, s32[2,64]{1,0:T(2,128)} %bitcast.17, f32[1,64]{1,0:T(1,128)} %bitcast.19, f32[1,64]{1,0:T(1,128)} %bitcast.21, bf16[128,144,256]{2,1,0:T(8,128)(2,1)} %bitcast.23), custom_call_target="tpu_custom_call" | custom-call | tf_op jit(solution)/shard_map/pallas_call | solution.py:174
  5.5 3.3 %collective-permute-start = (f32[2,2,128,128]{3,2,1,0:T(8,128)S(1)}, f32[2,2,128,128]{3,2,1,0:T(8,128)S(1)}, u32[]{:S(2)}, u32[]{:S(2)}) collective-permute-start(f32[2,2,128,128]{3,2,1,0:T(8,128)S(1)} %get-tuple-element.15), channel_id=1, source_target_pairs={{0,1},{1,0},{2,3},{3,2},{4,5},{5,4},{6,7},{7,6},{8,9},{9,8},{10,11... | collective-permute-start | bytes 786440 | tf_op jit(solution)/shard_map/ppermute | solution.py:405
  8.8 1.2 %collective-permute-done = f32[2,2,128,128]{3,2,1,0:T(8,128)S(1)} collective-permute-done((f32[2,2,128,128]{3,2,1,0:T(8,128)S(1)}, f32[2,2,128,128]{3,2,1,0:T(8,128)S(1)}, u32[]{:S(2)}, u32[]{:S(2)}) %collective-permute-start) | collective-permute-done | bytes 262176 | tf_op jit(solution)/shard_map/ppermute | solution.py:405
  10.0 0.1 collective-permute-start.1
  10.1 4.7 %collective-permute-done.1 = f32[2,128,128]{2,1,0:T(8,128)S(1)} collective-permute-done((f32[2,128,128]{2,1,0:T(8,128)S(1)}, f32[2,128,128]{2,1,0:T(8,128)S(1)}, u32[]{:S(2)}, u32[]{:S(2)}) %collective-permute-start.1) | collective-permute-done | bytes 131104 | tf_op jit(solution)/shard_map/ppermute | solution.py:405
  14.8 0.1 collective-permute-start.2
  14.9 0.0 copy-done.2
  14.9 0.0 copy-done.3
  14.9 0.0 copy-done.6
  14.9 0.0 copy-done.5
  14.9 0.0 copy-done.4
  15.0 1.7 %shard_map.83 = (bf16[1024,512]{1,0:T(8,128)(2,1)S(1)}, bf16[256,128]{1,0:T(8,128)(2,1)S(1)}) custom-call(s32[32]{0:T(128)S(1)} %copy-done.3, s32[32]{0:T(128)S(1)} %copy-done.2, s32[2,64]{1,0:T(2,128)S(1)} %bitcast.18, f32[1,64]{1,0:T(1,128)S(1)} %bitcast.20, f32[1,64]{1,0:T(1,128)S(1)} %bitcast.22), custom_call_target="tpu_custom_call" | custom-call | flops 100000000 | bytes 1000000 | tf_op jit(solution)/shard_map/pallas_call | solution.py:298
  16.7 2.0 %collective-permute-done.2 = f32[2,128,128]{2,1,0:T(8,128)S(1)} collective-permute-done((f32[2,128,128]{2,1,0:T(8,128)S(1)}, f32[2,128,128]{2,1,0:T(8,128)S(1)}, u32[]{:S(2)}, u32[]{:S(2)}) %collective-permute-start.2) | collective-permute-done | bytes 131104 | tf_op jit(solution)/shard_map/ppermute | solution.py:405
  18.7 1.5 %collective-permute-start.3 = (f32[2,128,128]{2,1,0:T(8,128)S(1)}, f32[2,128,128]{2,1,0:T(8,128)S(1)}, u32[]{:S(2)}, u32[]{:S(2)}) collective-permute-start(f32[2,128,128]{2,1,0:T(8,128)S(1)} %add.17), channel_id=1, source_target_pairs={{0,8},{4,12},{16,24},{20,28},{8,0},{12,4},{24,16},{28,20},{1,9},{5... | collective-permute-start | bytes 393224 | tf_op jit(solution)/shard_map/ppermute | solution.py:405
  20.3 4.7 %collective-permute-done.3 = f32[2,128,128]{2,1,0:T(8,128)S(1)} collective-permute-done((f32[2,128,128]{2,1,0:T(8,128)S(1)}, f32[2,128,128]{2,1,0:T(8,128)S(1)}, u32[]{:S(2)}, u32[]{:S(2)}) %collective-permute-start.3) | collective-permute-done | bytes 131104 | tf_op jit(solution)/shard_map/ppermute | solution.py:405
  25.0 3.9 %collective-permute-start.4 = (f32[2,128,128]{2,1,0:T(8,128)S(1)}, f32[2,128,128]{2,1,0:T(8,128)S(1)}, u32[]{:S(2)}, u32[]{:S(2)}) collective-permute-start(f32[2,128,128]{2,1,0:T(8,128)S(1)} %add.18), channel_id=1, source_target_pairs={{0,28},{4,24},{8,20},{12,16},{28,0},{24,4},{20,8},{16,12},{1,29},{... | collective-permute-start | bytes 393224 | tf_op jit(solution)/shard_map/ppermute | solution.py:405
  28.9 3.3 %collective-permute-done.4 = f32[2,128,128]{2,1,0:T(8,128)S(1)} collective-permute-done((f32[2,128,128]{2,1,0:T(8,128)S(1)}, f32[2,128,128]{2,1,0:T(8,128)S(1)}, u32[]{:S(2)}, u32[]{:S(2)}) %collective-permute-start.4) | collective-permute-done | bytes 131104 | tf_op jit(solution)/shard_map/ppermute | solution.py:405
  32.3 1.6 %shard_map.84 = f32[8,2,40,128]{3,2,1,0:T(8,128)S(1)} custom-call(s32[32]{0:T(128)S(1)} %copy-done.3, f32[2,128,128]{2,1,0:T(8,128)S(1)} %add.19.wave_ref, f32[4,128,128]{2,1,0:T(8,128)S(1)} %copy-done.1, bf16[2,2,256,256]{3,2,1,0:T(8,128)(2,1)S(1)} %copy-done), custom_call_target="tpu_custom_call" | custom-call | tf_op jit(solution)/shard_map/pallas_call | solution.py:234
  33.9 14.2 %all_to_all.5.received_ref = f32[16,40,128]{2,1,0:T(8,128)S(1)} all-to-all(f32[16,40,128]{2,1,0:T(8,128)S(1)} %bitcast.16), channel_id=1, replica_groups=mesh['pos'=8,'z'=8,'yl'=2,'core'=2] {'pos','yl'}, dimensions={0} | all-to-all | bytes 655360 | tf_op jit(solution)/shard_map/all_to_all | solution.py:428
  48.1 5.8 %collective-permute-start.5 = (f32[16,40,128]{2,1,0:T(8,128)S(1)}, f32[16,40,128]{2,1,0:T(8,128)S(1)}, u32[]{:S(2)}, u32[]{:S(2)}) collective-permute-start(f32[16,40,128]{2,1,0:T(8,128)S(1)} %all_to_all.5.received_ref), channel_id=1, source_target_pairs={{0,1},{1,0},{2,3},{3,2},{4,5},{5,4},{6,7},{7,6},{8,9},{9,8},{10,11... | collective-permute-start | bytes 983048 | tf_op jit(solution)/shard_map/ppermute | solution.py:405
  53.9 0.7 %shard_map.85 = (bf16[2,256,256]{2,1,0:T(8,128)(2,1)S(1)}, bf16[64,256]{1,0:T(8,128)(2,1)S(1)}) custom-call(s32[32]{0:T(128)S(1)} %copy-done.2, f32[16,40,128]{2,1,0:T(8,128)S(1)} %all_to_all.5.received_ref), custom_call_target="tpu_custom_call" | custom-call | flops 1000000 | bytes 1000000 | tf_op jit(solution)/shard_map/pallas_call | solution.py:332
  54.7 0.5 collective-permute-done.5.other_ref
  55.2 2.5 %shard_map.86 = f32[4608,128]{1,0:T(8,128)} custom-call(s32[32]{0:T(128)S(1)} %copy-done.2, bf16[1024,512]{1,0:T(8,128)(2,1)S(1)} %get-tuple-element.18.weight_ref, bf16[256,128]{1,0:T(8,128)(2,1)S(1)} %get-tuple-element.19.weight_rest_ref, bf16[2,256,256]{2,1,0:T(8,128)(2,1)S(1)} %get-tuple-element.21.own_ref, ...), custom_call_target="tpu_custom_call" | custom-call | tf_op jit(solution)/shard_map/pallas_call | solution.py:389
  (14 shorter events, 0.1 us)
Async XLA Ops:
  0.0 32.2 %copy-start = (bf16[2,2,256,256]{3,2,1,0:T(8,128)(2,1)S(1)}, bf16[2,2,256,256]{3,2,1,0:T(8,128)(2,1)}, u32[]{:S(2)}) copy-start(bf16[2,2,256,256]{3,2,1,0:T(8,128)(2,1)} %constant.2.clone.table_ref) | copy-start | bytes 1572868
  0.0 14.9 %copy-start.2 = (s32[32]{0:T(128)S(1)}, s32[32]{0:T(128)}, u32[]{:S(2)}) copy-start(s32[32]{0:T(128)} %ox_ref.5) | copy-start | bytes 388
  0.0 14.9 %copy-start.3 = (s32[32]{0:T(128)S(1)}, s32[32]{0:T(128)}, u32[]{:S(2)}) copy-start(s32[32]{0:T(128)} %oy_ref.3) | copy-start | bytes 388
  0.0 14.9 %copy-start.6 = (f32[64]{0:T(128)S(1)}, f32[64]{0:T(128)}, u32[]{:S(2)}) copy-start(f32[64]{0:T(128)} %param.11) | copy-start | bytes 772
  0.0 14.9 %copy-start.5 = (f32[64]{0:T(128)S(1)}, f32[64]{0:T(128)}, u32[]{:S(2)}) copy-start(f32[64]{0:T(128)} %param.10) | copy-start | bytes 772
  0.0 14.9 %copy-start.4 = (s32[64,2]{0,1:T(2,128)S(1)}, s32[64,2]{0,1:T(2,128)}, u32[]{:S(2)}) copy-start(s32[64,2]{0,1:T(2,128)} %param.9) | copy-start | bytes 1540
  0.0 32.2 %copy-start.1 = (f32[4,128,128]{2,1,0:T(8,128)S(1)}, f32[4,128,128]{2,1,0:T(8,128)}, u32[]{:S(2)}) copy-start(f32[4,128,128]{2,1,0:T(8,128)} %measured_ref.1) | copy-start | bytes 786436
  5.5 4.5 %collective-permute-start = (f32[2,2,128,128]{3,2,1,0:T(8,128)S(1)}, f32[2,2,128,128]{3,2,1,0:T(8,128)S(1)}, u32[]{:S(2)}, u32[]{:S(2)}) collective-permute-start(f32[2,2,128,128]{3,2,1,0:T(8,128)S(1)} %get-tuple-element.15), channel_id=1, source_target_pairs={{0,1},{1,0},{2,3},{3,2},{4,5},{5,4},{6,7},{7,6},{8,9},{9,8},{10,11... | collective-permute-start | bytes 786440 | tf_op jit(solution)/shard_map/ppermute | solution.py:405
  10.0 4.8 %collective-permute-start.1 = (f32[2,128,128]{2,1,0:T(8,128)S(1)}, f32[2,128,128]{2,1,0:T(8,128)S(1)}, u32[]{:S(2)}, u32[]{:S(2)}) collective-permute-start(f32[2,128,128]{2,1,0:T(8,128)S(1)} %slice_bitcast_fusion), channel_id=1, source_target_pairs={{0,2},{2,0},{1,3},{3,1},{4,6},{6,4},{5,7},{7,5},{8,10},{10,8},{9,1... | collective-permute-start | bytes 393224 | tf_op jit(solution)/shard_map/ppermute | solution.py:405
  14.8 3.9 %collective-permute-start.2 = (f32[2,128,128]{2,1,0:T(8,128)S(1)}, f32[2,128,128]{2,1,0:T(8,128)S(1)}, u32[]{:S(2)}, u32[]{:S(2)}) collective-permute-start(f32[2,128,128]{2,1,0:T(8,128)S(1)} %fusion), channel_id=1, source_target_pairs={{0,4},{8,12},{16,20},{24,28},{4,0},{12,8},{20,16},{28,24},{1,5},{9... | collective-permute-start | bytes 393224 | tf_op jit(solution)/shard_map/ppermute | solution.py:405
  18.7 6.2 %collective-permute-start.3 = (f32[2,128,128]{2,1,0:T(8,128)S(1)}, f32[2,128,128]{2,1,0:T(8,128)S(1)}, u32[]{:S(2)}, u32[]{:S(2)}) collective-permute-start(f32[2,128,128]{2,1,0:T(8,128)S(1)} %add.17), channel_id=1, source_target_pairs={{0,8},{4,12},{16,24},{20,28},{8,0},{12,4},{24,16},{28,20},{1,9},{5... | collective-permute-start | bytes 393224 | tf_op jit(solution)/shard_map/ppermute | solution.py:405
  25.0 7.2 %collective-permute-start.4 = (f32[2,128,128]{2,1,0:T(8,128)S(1)}, f32[2,128,128]{2,1,0:T(8,128)S(1)}, u32[]{:S(2)}, u32[]{:S(2)}) collective-permute-start(f32[2,128,128]{2,1,0:T(8,128)S(1)} %add.18), channel_id=1, source_target_pairs={{0,28},{4,24},{8,20},{12,16},{28,0},{24,4},{20,8},{16,12},{1,29},{... | collective-permute-start | bytes 393224 | tf_op jit(solution)/shard_map/ppermute | solution.py:405
  48.1 7.1 %collective-permute-start.5 = (f32[16,40,128]{2,1,0:T(8,128)S(1)}, f32[16,40,128]{2,1,0:T(8,128)S(1)}, u32[]{:S(2)}, u32[]{:S(2)}) collective-permute-start(f32[16,40,128]{2,1,0:T(8,128)S(1)} %all_to_all.5.received_ref), channel_id=1, source_target_pairs={{0,1},{1,0},{2,3},{3,2},{4,5},{5,4},{6,7},{7,6},{8,9},{9,8},{10,11... | collective-permute-start | bytes 983048 | tf_op jit(solution)/shard_map/ppermute | solution.py:405

commit v5 on v4

--- a/solution.py
+++ b/solution.py
@@ -70,7 +70,7 @@
 
 
 PIECE = 16
-FIRST = 4
+STAGES = (3, 6, 8)
 
 
 def waves_kernel(
@@ -96,9 +96,9 @@
     for i in range(depth // PIECE):
         planes = pl.ds(i * PIECE, PIECE)
         large.append(pltpu.make_async_copy(s_hbm.at[planes], s_ref.at[planes], piece_sem.at[i]))
-    for copy in small + large[:FIRST]:
+    for copy in small + large[: STAGES[0]]:
         copy.start()
-    for copy in large[FIRST:]:
+    for copy in large[STAGES[0] :]:
         copy.start(priority=1)
 
     outs, wide = 8, depth * ROWS
@@ -131,6 +131,7 @@
     lefts = [lax.rem(FIELD_X - ox_ref[slots[slot]], FIELD_X) for slot in range(4)]
 
     def multiply(i, low, high):
+        low, high = low * PIECE, high * PIECE
         tile = s_ref[low:high, i * ROWS : (i + 1) * ROWS, :].reshape((high - low) * ROWS, FIELD_X)
         return dot(mix_ref[:, low * ROWS : high * ROWS], tile)
 
@@ -151,18 +152,16 @@
                 rows = slice(u * ROWS, (u + 1) * ROWS)
                 ref[slot % 2, plane, rows] = value[plane * ROWS : (plane + 1) * ROWS]
 
-    middle = FIRST * PIECE
-    for copy in large[:FIRST]:
-        copy.wait()
-    for i in range(tiles):
-        full_ref[i] = multiply(i, 0, middle)
-    for copy in large[FIRST:]:
-        copy.wait()
-    for i in range(tiles):
-        full_ref[i] += multiply(i, middle, depth)
-        crop_columns(i)
-        if i >= 2:
-            crop_rows(i - 2)
+    for low, high in zip((0, *STAGES), STAGES):
+        for copy in large[low:high]:
+            copy.wait()
+        for i in range(tiles):
+            part = multiply(i, low, high)
+            full_ref[i] = full_ref[i] + part if low else part
+            if high == len(large):
+                crop_columns(i)
+                if i >= 2:
+                    crop_rows(i - 2)
     crop_rows(tiles - 2)
 
 

time: 57.8 us -> 57.4 us (level)
  no operation moved by 1% of the time
where the time goes in v5:
time: 57.4 us; the launch traced here: 57.3 us
  waiting for transfers between devices  16.4 us (29%)
  starting transfers between devices  14.8 us (26%)
  blocking collectives  14.2 us (25%)
  Pallas kernels  11.6 us (20%)
    ppermute x6, waiting for transfers between devices, swap(): return lax.ppermute(value, axis, both)  16.4 us
    ppermute x6, starting transfers between devices, swap(): return lax.ppermute(value, axis, both)  14.8 us
    all_to_all x1, blocking collectives, body(): received = lax.all_to_all(blocks, ('pos', 'yl'), 0, 0, tiled=True)  14.2 us
    pallas_call x1, Pallas kernels, own_waves(): pl.pallas_call(waves_kernel, in_specs=[pl.BlockSpec(memory_space=pl.ANY)]...  5.07 us
    pallas_call x1, Pallas kernels, fold(): pl.pallas_call(fold_kernel, in_specs=[pl.BlockSpec(memory_space=pltpu.SME...  2.46 us
    pallas_call x1, Pallas kernels, fold_weights(): pl.pallas_call(weights_kernel, in_specs=[pl.BlockSpec(memory_space=pltpu....  1.71 us
    pallas_call x1, Pallas kernels, misfit_blocks(): pl.pallas_call(misfit_kernel, in_specs=[pl.BlockSpec(memory_space=pltpu.S...  1.63 us
  transfers between devices with their start and end apart: 6, of which 6 were waited for; matrix products, arithmetic and copies ran while one was open for 0% of the time, Pallas kernels for 4%

profile of v5, /device:TPU:1, one launch (start us, length us, event | category | flops | bytes accessed | tf_op | source)
XLA Modules:
  0.0 57.3 jit_solution(15483004223679305279)
XLA Ops:
  0.0 0.0 copy-start.6
  0.0 0.0 copy-start.5
  0.0 0.0 copy-start.4
  0.0 0.0 copy-start.1
  0.0 5.1 %shard_map.82 = (f32[2,2,128,128]{3,2,1,0:T(8,128)S(1)}, f32[2,2,128,128]{3,2,1,0:T(8,128)S(1)}) custom-call(s32[32]{0:T(128)} %oy_ref.3, s32[32]{0:T(128)} %ox_ref.5, s32[2,64]{1,0:T(2,128)} %bitcast.17, f32[1,64]{1,0:T(1,128)} %bitcast.19, f32[1,64]{1,0:T(1,128)} %bitcast.21, bf16[128,144,256]{2,1,0:T(8,128)(2,1)} %bitcast.23), custom_call_target="tpu_custom_call" | custom-call | tf_op jit(solution)/shard_map/pallas_call | solution.py:173
  5.1 3.3 %collective-permute-start = (f32[2,2,128,128]{3,2,1,0:T(8,128)S(1)}, f32[2,2,128,128]{3,2,1,0:T(8,128)S(1)}, u32[]{:S(2)}, u32[]{:S(2)}) collective-permute-start(f32[2,2,128,128]{3,2,1,0:T(8,128)S(1)} %get-tuple-element.15), channel_id=1, source_target_pairs={{0,1},{1,0},{2,3},{3,2},{4,5},{5,4},{6,7},{7,6},{8,9},{9,8},{10,11... | collective-permute-start | bytes 786440 | tf_op jit(solution)/shard_map/ppermute | solution.py:404
  8.4 1.2 %collective-permute-done = f32[2,2,128,128]{3,2,1,0:T(8,128)S(1)} collective-permute-done((f32[2,2,128,128]{3,2,1,0:T(8,128)S(1)}, f32[2,2,128,128]{3,2,1,0:T(8,128)S(1)}, u32[]{:S(2)}, u32[]{:S(2)}) %collective-permute-start) | collective-permute-done | bytes 262176 | tf_op jit(solution)/shard_map/ppermute | solution.py:404
  9.7 0.1 collective-permute-start.1
  9.8 4.7 %collective-permute-done.1 = f32[2,128,128]{2,1,0:T(8,128)S(1)} collective-permute-done((f32[2,128,128]{2,1,0:T(8,128)S(1)}, f32[2,128,128]{2,1,0:T(8,128)S(1)}, u32[]{:S(2)}, u32[]{:S(2)}) %collective-permute-start.1) | collective-permute-done | bytes 131104 | tf_op jit(solution)/shard_map/ppermute | solution.py:404
  14.5 0.1 collective-permute-start.2
  14.6 1.7 %shard_map.83 = (bf16[1024,512]{1,0:T(8,128)(2,1)S(1)}, bf16[256,128]{1,0:T(8,128)(2,1)S(1)}) custom-call(s32[32]{0:T(128)S(1)} %copy-done.3, s32[32]{0:T(128)S(1)} %copy-done.2, s32[2,64]{1,0:T(2,128)S(1)} %bitcast.18, f32[1,64]{1,0:T(1,128)S(1)} %bitcast.20, f32[1,64]{1,0:T(1,128)S(1)} %bitcast.22), custom_call_target="tpu_custom_call" | custom-call | flops 100000000 | bytes 1000000 | tf_op jit(solution)/shard_map/pallas_call | solution.py:297
  16.4 2.0 %collective-permute-done.2 = f32[2,128,128]{2,1,0:T(8,128)S(1)} collective-permute-done((f32[2,128,128]{2,1,0:T(8,128)S(1)}, f32[2,128,128]{2,1,0:T(8,128)S(1)}, u32[]{:S(2)}, u32[]{:S(2)}) %collective-permute-start.2) | collective-permute-done | bytes 131104 | tf_op jit(solution)/shard_map/ppermute | solution.py:404
  18.4 1.5 %collective-permute-start.3 = (f32[2,128,128]{2,1,0:T(8,128)S(1)}, f32[2,128,128]{2,1,0:T(8,128)S(1)}, u32[]{:S(2)}, u32[]{:S(2)}) collective-permute-start(f32[2,128,128]{2,1,0:T(8,128)S(1)} %add.17), channel_id=1, source_target_pairs={{0,8},{4,12},{16,24},{20,28},{8,0},{12,4},{24,16},{28,20},{1,9},{5... | collective-permute-start | bytes 393224 | tf_op jit(solution)/shard_map/ppermute | solution.py:404
  19.9 4.7 %collective-permute-done.3 = f32[2,128,128]{2,1,0:T(8,128)S(1)} collective-permute-done((f32[2,128,128]{2,1,0:T(8,128)S(1)}, f32[2,128,128]{2,1,0:T(8,128)S(1)}, u32[]{:S(2)}, u32[]{:S(2)}) %collective-permute-start.3) | collective-permute-done | bytes 131104 | tf_op jit(solution)/shard_map/ppermute | solution.py:404
  24.6 3.9 %collective-permute-start.4 = (f32[2,128,128]{2,1,0:T(8,128)S(1)}, f32[2,128,128]{2,1,0:T(8,128)S(1)}, u32[]{:S(2)}, u32[]{:S(2)}) collective-permute-start(f32[2,128,128]{2,1,0:T(8,128)S(1)} %add.18), channel_id=1, source_target_pairs={{0,28},{4,24},{8,20},{12,16},{28,0},{24,4},{20,8},{16,12},{1,29},{... | collective-permute-start | bytes 393224 | tf_op jit(solution)/shard_map/ppermute | solution.py:404
  28.6 3.3 %collective-permute-done.4 = f32[2,128,128]{2,1,0:T(8,128)S(1)} collective-permute-done((f32[2,128,128]{2,1,0:T(8,128)S(1)}, f32[2,128,128]{2,1,0:T(8,128)S(1)}, u32[]{:S(2)}, u32[]{:S(2)}) %collective-permute-start.4) | collective-permute-done | bytes 131104 | tf_op jit(solution)/shard_map/ppermute | solution.py:404
  31.9 0.0 copy-done
  31.9 0.0 copy-done.1
  31.9 1.6 %shard_map.84 = f32[8,2,40,128]{3,2,1,0:T(8,128)S(1)} custom-call(s32[32]{0:T(128)S(1)} %copy-done.3, f32[2,128,128]{2,1,0:T(8,128)S(1)} %add.19.wave_ref, f32[4,128,128]{2,1,0:T(8,128)S(1)} %copy-done.1, bf16[2,2,256,256]{3,2,1,0:T(8,128)(2,1)S(1)} %copy-done), custom_call_target="tpu_custom_call" | custom-call | tf_op jit(solution)/shard_map/pallas_call | solution.py:233
  33.6 14.2 %all_to_all.5.received_ref = f32[16,40,128]{2,1,0:T(8,128)S(1)} all-to-all(f32[16,40,128]{2,1,0:T(8,128)S(1)} %bitcast.16), channel_id=1, replica_groups=mesh['pos'=8,'z'=8,'yl'=2,'core'=2] {'pos','yl'}, dimensions={0} | all-to-all | bytes 655360 | tf_op jit(solution)/shard_map/all_to_all | solution.py:427
  47.8 5.8 %collective-permute-start.5 = (f32[16,40,128]{2,1,0:T(8,128)S(1)}, f32[16,40,128]{2,1,0:T(8,128)S(1)}, u32[]{:S(2)}, u32[]{:S(2)}) collective-permute-start(f32[16,40,128]{2,1,0:T(8,128)S(1)} %all_to_all.5.received_ref), channel_id=1, source_target_pairs={{0,1},{1,0},{2,3},{3,2},{4,5},{5,4},{6,7},{7,6},{8,9},{9,8},{10,11... | collective-permute-start | bytes 983048 | tf_op jit(solution)/shard_map/ppermute | solution.py:404
  53.6 0.7 %shard_map.85 = (bf16[2,256,256]{2,1,0:T(8,128)(2,1)S(1)}, bf16[64,256]{1,0:T(8,128)(2,1)S(1)}) custom-call(s32[32]{0:T(128)S(1)} %copy-done.2, f32[16,40,128]{2,1,0:T(8,128)S(1)} %all_to_all.5.received_ref), custom_call_target="tpu_custom_call" | custom-call | flops 1000000 | bytes 1000000 | tf_op jit(solution)/shard_map/pallas_call | solution.py:331
  54.4 0.5 collective-permute-done.5.other_ref
  54.9 2.5 %shard_map.86 = f32[4608,128]{1,0:T(8,128)} custom-call(s32[32]{0:T(128)S(1)} %copy-done.2, bf16[1024,512]{1,0:T(8,128)(2,1)S(1)} %get-tuple-element.18.weight_ref, bf16[256,128]{1,0:T(8,128)(2,1)S(1)} %get-tuple-element.19.weight_rest_ref, bf16[2,256,256]{2,1,0:T(8,128)(2,1)S(1)} %get-tuple-element.21.own_ref, ...), custom_call_target="tpu_custom_call" | custom-call | tf_op jit(solution)/shard_map/pallas_call | solution.py:388
  (14 shorter events, 0.1 us)
Async XLA Ops:
  0.0 31.9 %copy-start = (bf16[2,2,256,256]{3,2,1,0:T(8,128)(2,1)S(1)}, bf16[2,2,256,256]{3,2,1,0:T(8,128)(2,1)}, u32[]{:S(2)}) copy-start(bf16[2,2,256,256]{3,2,1,0:T(8,128)(2,1)} %constant.2.clone.table_ref) | copy-start | bytes 1572868
  0.0 14.6 %copy-start.2 = (s32[32]{0:T(128)S(1)}, s32[32]{0:T(128)}, u32[]{:S(2)}) copy-start(s32[32]{0:T(128)} %ox_ref.5) | copy-start | bytes 388
  0.0 14.6 %copy-start.3 = (s32[32]{0:T(128)S(1)}, s32[32]{0:T(128)}, u32[]{:S(2)}) copy-start(s32[32]{0:T(128)} %oy_ref.3) | copy-start | bytes 388
  0.0 14.6 %copy-start.6 = (f32[64]{0:T(128)S(1)}, f32[64]{0:T(128)}, u32[]{:S(2)}) copy-start(f32[64]{0:T(128)} %param.11) | copy-start | bytes 772
  0.0 14.6 %copy-start.5 = (f32[64]{0:T(128)S(1)}, f32[64]{0:T(128)}, u32[]{:S(2)}) copy-start(f32[64]{0:T(128)} %param.10) | copy-start | bytes 772
  0.0 14.6 %copy-start.4 = (s32[64,2]{0,1:T(2,128)S(1)}, s32[64,2]{0,1:T(2,128)}, u32[]{:S(2)}) copy-start(s32[64,2]{0,1:T(2,128)} %param.9) | copy-start | bytes 1540
  0.0 31.9 %copy-start.1 = (f32[4,128,128]{2,1,0:T(8,128)S(1)}, f32[4,128,128]{2,1,0:T(8,128)}, u32[]{:S(2)}) copy-start(f32[4,128,128]{2,1,0:T(8,128)} %measured_ref.1) | copy-start | bytes 786436
  5.1 4.5 %collective-permute-start = (f32[2,2,128,128]{3,2,1,0:T(8,128)S(1)}, f32[2,2,128,128]{3,2,1,0:T(8,128)S(1)}, u32[]{:S(2)}, u32[]{:S(2)}) collective-permute-start(f32[2,2,128,128]{3,2,1,0:T(8,128)S(1)} %get-tuple-element.15), channel_id=1, source_target_pairs={{0,1},{1,0},{2,3},{3,2},{4,5},{5,4},{6,7},{7,6},{8,9},{9,8},{10,11... | collective-permute-start | bytes 786440 | tf_op jit(solution)/shard_map/ppermute | solution.py:404
  9.7 4.8 %collective-permute-start.1 = (f32[2,128,128]{2,1,0:T(8,128)S(1)}, f32[2,128,128]{2,1,0:T(8,128)S(1)}, u32[]{:S(2)}, u32[]{:S(2)}) collective-permute-start(f32[2,128,128]{2,1,0:T(8,128)S(1)} %slice_bitcast_fusion), channel_id=1, source_target_pairs={{0,2},{2,0},{1,3},{3,1},{4,6},{6,4},{5,7},{7,5},{8,10},{10,8},{9,1... | collective-permute-start | bytes 393224 | tf_op jit(solution)/shard_map/ppermute | solution.py:404
  14.5 3.9 %collective-permute-start.2 = (f32[2,128,128]{2,1,0:T(8,128)S(1)}, f32[2,128,128]{2,1,0:T(8,128)S(1)}, u32[]{:S(2)}, u32[]{:S(2)}) collective-permute-start(f32[2,128,128]{2,1,0:T(8,128)S(1)} %fusion), channel_id=1, source_target_pairs={{0,4},{8,12},{16,20},{24,28},{4,0},{12,8},{20,16},{28,24},{1,5},{9... | collective-permute-start | bytes 393224 | tf_op jit(solution)/shard_map/ppermute | solution.py:404
  18.4 6.2 %collective-permute-start.3 = (f32[2,128,128]{2,1,0:T(8,128)S(1)}, f32[2,128,128]{2,1,0:T(8,128)S(1)}, u32[]{:S(2)}, u32[]{:S(2)}) collective-permute-start(f32[2,128,128]{2,1,0:T(8,128)S(1)} %add.17), channel_id=1, source_target_pairs={{0,8},{4,12},{16,24},{20,28},{8,0},{12,4},{24,16},{28,20},{1,9},{5... | collective-permute-start | bytes 393224 | tf_op jit(solution)/shard_map/ppermute | solution.py:404
  24.6 7.3 %collective-permute-start.4 = (f32[2,128,128]{2,1,0:T(8,128)S(1)}, f32[2,128,128]{2,1,0:T(8,128)S(1)}, u32[]{:S(2)}, u32[]{:S(2)}) collective-permute-start(f32[2,128,128]{2,1,0:T(8,128)S(1)} %add.18), channel_id=1, source_target_pairs={{0,28},{4,24},{8,20},{12,16},{28,0},{24,4},{20,8},{16,12},{1,29},{... | collective-permute-start | bytes 393224 | tf_op jit(solution)/shard_map/ppermute | solution.py:404
  47.8 7.1 %collective-permute-start.5 = (f32[16,40,128]{2,1,0:T(8,128)S(1)}, f32[16,40,128]{2,1,0:T(8,128)S(1)}, u32[]{:S(2)}, u32[]{:S(2)}) collective-permute-start(f32[16,40,128]{2,1,0:T(8,128)S(1)} %all_to_all.5.received_ref), channel_id=1, source_target_pairs={{0,1},{1,0},{2,3},{3,2},{4,5},{5,4},{6,7},{7,6},{8,9},{9,8},{10,11... | collective-permute-start | bytes 983048 | tf_op jit(solution)/shard_map/ppermute | solution.py:404

commit v6 on v5

--- a/solution.py
+++ b/solution.py
@@ -75,7 +75,7 @@
 
 def waves_kernel(
     oy_hbm, ox_hbm, index_hbm, amplitude_hbm, phase_hbm, s_hbm,
-    keep_ref, send_ref,
+    slot0_ref, slot1_ref, slot2_ref, slot3_ref,
     oy_ref, ox_ref, index_ref, amplitude_ref, phase_ref, s_ref, mix_ref, full_ref, part_ref, small_sem, piece_sem,
 ):
     depth, tiles = s_ref.shape[0], FIELD_Y // ROWS
@@ -147,10 +147,10 @@
             upper = iota2((2 * ROWS, WIN))[0] % ROWS < rest
             after = jnp.minimum(u + skip + 1, tiles - 1)
             value = jnp.where(upper, part_ref[slot, u + skip], part_ref[slot, after])
-            ref = (keep_ref, send_ref)[slot // 2]
+            ref = (slot0_ref, slot1_ref, slot2_ref, slot3_ref)[slot]
             for plane in range(2):
                 rows = slice(u * ROWS, (u + 1) * ROWS)
-                ref[slot % 2, plane, rows] = value[plane * ROWS : (plane + 1) * ROWS]
+                ref[plane, rows] = value[plane * ROWS : (plane + 1) * ROWS]
 
     for low, high in zip((0, *STAGES), STAGES):
         for copy in large[low:high]:
@@ -167,14 +167,13 @@
 
 def own_waves(s_flat, offsets_y, offsets_x, beams):
     depth = s_flat.shape[0]
-    half = pltpu.VMEM((2, 2, WIN, WIN), jnp.float32)
     small = (offsets_y, offsets_x, *beams)
     operands = (*small, s_flat)
     return pl.pallas_call(
         waves_kernel,
         in_specs=[pl.BlockSpec(memory_space=pl.ANY)] * len(operands),
-        out_specs=[pl.BlockSpec(memory_space=pltpu.VMEM)] * 2,
-        out_shape=[half, half],
+        out_specs=[pl.BlockSpec(memory_space=pltpu.VMEM)] * 4,
+        out_shape=[pltpu.VMEM((2, WIN, WIN), jnp.float32)] * 4,
         scratch_shapes=[
             pltpu.SMEM(offsets_y.shape, jnp.int32),
             pltpu.SMEM(offsets_x.shape, jnp.int32),
@@ -196,7 +195,12 @@
 
 
 def product(left, right):
-    return dot(left[0], right[0]) + (dot(left[1], right[0]) + dot(left[0], right[1]))
+    rows, columns = left[0].shape[0], right[0].shape[1]
+    if rows < columns:
+        both = dot(jnp.concatenate(left, axis=0), right[0])
+        return both[:rows] + (both[rows:] + dot(left[0], right[1]))
+    both = dot(left[0], jnp.concatenate(right, axis=1))
+    return both[:, :columns] + (both[:, columns:] + dot(left[1], right[0]))
 
 
 def misfit_kernel(oy_ref, wave_ref, measured_ref, table_ref, out_ref, field_ref):
@@ -410,9 +414,10 @@
     beams = (beam_index.T, amplitude[None, :], phase[None, :])
     s_flat = s_matrix.reshape(beams_here * 2, FIELD_Y, FIELD_X)
 
-    keep, send = own_waves(s_flat, offsets_y, offsets_x, beams)
-    pair = keep + swap(send, "core", [(0, 1)])
-    total = pair[0] + swap(pair[1], "yl", [(0, 1)])
+    slots = own_waves(s_flat, offsets_y, offsets_x, beams)
+    onward = slots[1] + swap(slots[3], "core", [(0, 1)])
+    total = slots[0] + swap(slots[2], "core", [(0, 1)])
+    total = total + swap(onward, "yl", [(0, 1)])
     weights = fold_weights(offsets_y, offsets_x, beams)
     for bit in (1, 2):
         other = swap(total, "z", [(i, i ^ bit) for i in range(depth) if not i & bit])

time: 57.4 us -> 57.1 us (level)
    ppermute x6 -> x7, waiting for transfers between devices: 16.4 us -> 16.2 us  [swap(): return lax.ppermute(value, axis, both)]
    ppermute x6 -> x7, starting transfers between devices: 14.8 us -> 14.9 us  [swap(): return lax.ppermute(value, axis, both)]
  transfers between devices with their start and end apart: 6 -> 7, of which waited for: 6 -> 7; matrix products, arithmetic and copies ran while one was open for 0% -> 0% of each run, Pallas kernels for 4% -> 4%
where the time goes in v6:
time: 57.1 us; the launch traced here: 57 us
  waiting for transfers between devices  16.2 us (28%)
  starting transfers between devices  14.9 us (26%)
  blocking collectives  14.2 us (25%)
  Pallas kernels  11.5 us (20%)
    ppermute x7, waiting for transfers between devices, swap(): return lax.ppermute(value, axis, both)  16.2 us
    ppermute x7, starting transfers between devices, swap(): return lax.ppermute(value, axis, both)  14.9 us
    all_to_all x1, blocking collectives, body(): received = lax.all_to_all(blocks, ('pos', 'yl'), 0, 0, tiled=True)  14.2 us
    pallas_call x1, Pallas kernels, own_waves(): pl.pallas_call(waves_kernel, in_specs=[pl.BlockSpec(memory_space=pl.ANY)]...  5.07 us
    pallas_call x1, Pallas kernels, fold(): pl.pallas_call(fold_kernel, in_specs=[pl.BlockSpec(memory_space=pltpu.SME...  2.46 us
    pallas_call x1, Pallas kernels, fold_weights(): pl.pallas_call(weights_kernel, in_specs=[pl.BlockSpec(memory_space=pltpu....  1.72 us
    pallas_call x1, Pallas kernels, misfit_blocks(): pl.pallas_call(misfit_kernel, in_specs=[pl.BlockSpec(memory_space=pltpu.S...  1.51 us
  transfers between devices with their start and end apart: 7, of which 7 were waited for; matrix products, arithmetic and copies ran while one was open for 0% of the time, Pallas kernels for 4%

profile of v6, /device:TPU:1, one launch (start us, length us, event | category | flops | bytes accessed | tf_op | source)
XLA Modules:
  0.0 57.0 jit_solution(816536871779186770)
XLA Ops:
  0.0 0.0 copy-start.6
  0.0 0.0 copy-start.5
  0.0 5.1 %shard_map.82 = (f32[2,128,128]{2,1,0:T(8,128)S(1)}, f32[2,128,128]{2,1,0:T(8,128)S(1)}, f32[2,128,128]{2,1,0:T(8,128)S(1)}, f32[2,128,128]{2,1,0:T(8,128)S(1)}) custom-call(s32[32]{0:T(128)} %oy_ref.3, s32[32]{0:T(128)} %ox_ref.5, s32[2,64]{1,0:T(2,128)} %bitcast.11, f32[1,64]{1,0:T(1,128)} %bitcast.13, f32[1,64]{1,0:T(1,128)} %bitcast.15, ...), custom_call_target="tpu_custom_call" | custom-call | tf_op jit(solution)/shard_map/pallas_call | solution.py:172
  5.1 3.3 %collective-permute-start.1 = (f32[2,128,128]{2,1,0:T(8,128)S(1)}, f32[2,128,128]{2,1,0:T(8,128)S(1)}, u32[]{:S(2)}, u32[]{:S(2)}) collective-permute-start(f32[2,128,128]{2,1,0:T(8,128)S(1)} %get-tuple-element.19), channel_id=1, source_target_pairs={{0,1},{1,0},{2,3},{3,2},{4,5},{5,4},{6,7},{7,6},{8,9},{9,8},{10,11... | collective-permute-start | bytes 393224 | tf_op jit(solution)/shard_map/ppermute | solution.py:408
  8.4 0.1 collective-permute-start
  8.5 0.9 %collective-permute-done.1 = f32[2,128,128]{2,1,0:T(8,128)S(1)} collective-permute-done((f32[2,128,128]{2,1,0:T(8,128)S(1)}, f32[2,128,128]{2,1,0:T(8,128)S(1)}, u32[]{:S(2)}, u32[]{:S(2)}) %collective-permute-start.1) | collective-permute-done | bytes 131104 | tf_op jit(solution)/shard_map/ppermute | solution.py:408
  9.5 0.1 collective-permute-start.2
  9.6 0.2 collective-permute-done
  9.8 4.5 %collective-permute-done.2 = f32[2,128,128]{2,1,0:T(8,128)S(1)} collective-permute-done((f32[2,128,128]{2,1,0:T(8,128)S(1)}, f32[2,128,128]{2,1,0:T(8,128)S(1)}, u32[]{:S(2)}, u32[]{:S(2)}) %collective-permute-start.2) | collective-permute-done | bytes 131104 | tf_op jit(solution)/shard_map/ppermute | solution.py:408
  14.3 0.1 collective-permute-start.3
  14.4 1.7 %shard_map.83 = (bf16[1024,512]{1,0:T(8,128)(2,1)S(1)}, bf16[256,128]{1,0:T(8,128)(2,1)S(1)}) custom-call(s32[32]{0:T(128)S(1)} %copy-done.3, s32[32]{0:T(128)S(1)} %copy-done.2, s32[2,64]{1,0:T(2,128)S(1)} %bitcast.12, f32[1,64]{1,0:T(1,128)S(1)} %bitcast.14, f32[1,64]{1,0:T(1,128)S(1)} %bitcast.16), custom_call_target="tpu_custom_call" | custom-call | flops 100000000 | bytes 1000000 | tf_op jit(solution)/shard_map/pallas_call | solution.py:301
  16.2 2.0 %collective-permute-done.3 = f32[2,128,128]{2,1,0:T(8,128)S(1)} collective-permute-done((f32[2,128,128]{2,1,0:T(8,128)S(1)}, f32[2,128,128]{2,1,0:T(8,128)S(1)}, u32[]{:S(2)}, u32[]{:S(2)}) %collective-permute-start.3) | collective-permute-done | bytes 131104 | tf_op jit(solution)/shard_map/ppermute | solution.py:408
  18.2 1.5 %collective-permute-start.4 = (f32[2,128,128]{2,1,0:T(8,128)S(1)}, f32[2,128,128]{2,1,0:T(8,128)S(1)}, u32[]{:S(2)}, u32[]{:S(2)}) collective-permute-start(f32[2,128,128]{2,1,0:T(8,128)S(1)} %add.21), channel_id=1, source_target_pairs={{0,8},{4,12},{16,24},{20,28},{8,0},{12,4},{24,16},{28,20},{1,9},{5... | collective-permute-start | bytes 393224 | tf_op jit(solution)/shard_map/ppermute | solution.py:408
  19.8 4.7 %collective-permute-done.4 = f32[2,128,128]{2,1,0:T(8,128)S(1)} collective-permute-done((f32[2,128,128]{2,1,0:T(8,128)S(1)}, f32[2,128,128]{2,1,0:T(8,128)S(1)}, u32[]{:S(2)}, u32[]{:S(2)}) %collective-permute-start.4) | collective-permute-done | bytes 131104 | tf_op jit(solution)/shard_map/ppermute | solution.py:408
  24.5 3.9 %collective-permute-start.5 = (f32[2,128,128]{2,1,0:T(8,128)S(1)}, f32[2,128,128]{2,1,0:T(8,128)S(1)}, u32[]{:S(2)}, u32[]{:S(2)}) collective-permute-start(f32[2,128,128]{2,1,0:T(8,128)S(1)} %add.22), channel_id=1, source_target_pairs={{0,28},{4,24},{8,20},{12,16},{28,0},{24,4},{20,8},{16,12},{1,29},{... | collective-permute-start | bytes 393224 | tf_op jit(solution)/shard_map/ppermute | solution.py:408
  28.4 3.3 %collective-permute-done.5 = f32[2,128,128]{2,1,0:T(8,128)S(1)} collective-permute-done((f32[2,128,128]{2,1,0:T(8,128)S(1)}, f32[2,128,128]{2,1,0:T(8,128)S(1)}, u32[]{:S(2)}, u32[]{:S(2)}) %collective-permute-start.5) | collective-permute-done | bytes 131104 | tf_op jit(solution)/shard_map/ppermute | solution.py:408
  31.7 0.0 copy-done
  31.7 0.0 copy-done.1
  31.7 1.5 %shard_map.84 = f32[8,2,40,128]{3,2,1,0:T(8,128)S(1)} custom-call(s32[32]{0:T(128)S(1)} %copy-done.3, f32[2,128,128]{2,1,0:T(8,128)S(1)} %add.23.wave_ref, f32[4,128,128]{2,1,0:T(8,128)S(1)} %copy-done.1, bf16[2,2,256,256]{3,2,1,0:T(8,128)(2,1)S(1)} %copy-done), custom_call_target="tpu_custom_call" | custom-call | tf_op jit(solution)/shard_map/pallas_call | solution.py:237
  33.2 14.2 %all_to_all.5.received_ref = f32[16,40,128]{2,1,0:T(8,128)S(1)} all-to-all(f32[16,40,128]{2,1,0:T(8,128)S(1)} %bitcast.10), channel_id=1, replica_groups=mesh['pos'=8,'z'=8,'yl'=2,'core'=2] {'pos','yl'}, dimensions={0} | all-to-all | bytes 655360 | tf_op jit(solution)/shard_map/all_to_all | solution.py:432
  47.5 5.8 %collective-permute-start.6 = (f32[16,40,128]{2,1,0:T(8,128)S(1)}, f32[16,40,128]{2,1,0:T(8,128)S(1)}, u32[]{:S(2)}, u32[]{:S(2)}) collective-permute-start(f32[16,40,128]{2,1,0:T(8,128)S(1)} %all_to_all.5.received_ref), channel_id=1, source_target_pairs={{0,1},{1,0},{2,3},{3,2},{4,5},{5,4},{6,7},{7,6},{8,9},{9,8},{10,11... | collective-permute-start | bytes 983048 | tf_op jit(solution)/shard_map/ppermute | solution.py:408
  53.3 0.7 %shard_map.85 = (bf16[2,256,256]{2,1,0:T(8,128)(2,1)S(1)}, bf16[64,256]{1,0:T(8,128)(2,1)S(1)}) custom-call(s32[32]{0:T(128)S(1)} %copy-done.2, f32[16,40,128]{2,1,0:T(8,128)S(1)} %all_to_all.5.received_ref), custom_call_target="tpu_custom_call" | custom-call | flops 1000000 | bytes 1000000 | tf_op jit(solution)/shard_map/pallas_call | solution.py:335
  54.0 0.5 collective-permute-done.6.other_ref
  54.6 2.5 %shard_map.86 = f32[4608,128]{1,0:T(8,128)} custom-call(s32[32]{0:T(128)S(1)} %copy-done.2, bf16[1024,512]{1,0:T(8,128)(2,1)S(1)} %get-tuple-element.22.weight_ref, bf16[256,128]{1,0:T(8,128)(2,1)S(1)} %get-tuple-element.23.weight_rest_ref, bf16[2,256,256]{2,1,0:T(8,128)(2,1)S(1)} %get-tuple-element.25.own_ref, ...), custom_call_target="tpu_custom_call" | custom-call | tf_op jit(solution)/shard_map/pallas_call | solution.py:392
  (15 shorter events, 0.1 us)
Async XLA Ops:
  0.0 31.7 %copy-start = (bf16[2,2,256,256]{3,2,1,0:T(8,128)(2,1)S(1)}, bf16[2,2,256,256]{3,2,1,0:T(8,128)(2,1)}, u32[]{:S(2)}) copy-start(bf16[2,2,256,256]{3,2,1,0:T(8,128)(2,1)} %constant.2.clone.table_ref) | copy-start | bytes 1572868
  0.0 14.4 %copy-start.2 = (s32[32]{0:T(128)S(1)}, s32[32]{0:T(128)}, u32[]{:S(2)}) copy-start(s32[32]{0:T(128)} %ox_ref.5) | copy-start | bytes 388
  0.0 14.4 %copy-start.3 = (s32[32]{0:T(128)S(1)}, s32[32]{0:T(128)}, u32[]{:S(2)}) copy-start(s32[32]{0:T(128)} %oy_ref.3) | copy-start | bytes 388
  0.0 14.4 %copy-start.6 = (f32[64]{0:T(128)S(1)}, f32[64]{0:T(128)}, u32[]{:S(2)}) copy-start(f32[64]{0:T(128)} %param.11) | copy-start | bytes 772
  0.0 14.4 %copy-start.5 = (f32[64]{0:T(128)S(1)}, f32[64]{0:T(128)}, u32[]{:S(2)}) copy-start(f32[64]{0:T(128)} %param.10) | copy-start | bytes 772
  0.0 14.4 %copy-start.4 = (s32[64,2]{0,1:T(2,128)S(1)}, s32[64,2]{0,1:T(2,128)}, u32[]{:S(2)}) copy-start(s32[64,2]{0,1:T(2,128)} %param.9) | copy-start | bytes 1540
  0.0 31.7 %copy-start.1 = (f32[4,128,128]{2,1,0:T(8,128)S(1)}, f32[4,128,128]{2,1,0:T(8,128)}, u32[]{:S(2)}) copy-start(f32[4,128,128]{2,1,0:T(8,128)} %measured_ref.1) | copy-start | bytes 786436
  5.1 4.3 %collective-permute-start.1 = (f32[2,128,128]{2,1,0:T(8,128)S(1)}, f32[2,128,128]{2,1,0:T(8,128)S(1)}, u32[]{:S(2)}, u32[]{:S(2)}) collective-permute-start(f32[2,128,128]{2,1,0:T(8,128)S(1)} %get-tuple-element.19), channel_id=1, source_target_pairs={{0,1},{1,0},{2,3},{3,2},{4,5},{5,4},{6,7},{7,6},{8,9},{9,8},{10,11... | collective-permute-start | bytes 393224 | tf_op jit(solution)/shard_map/ppermute | solution.py:408
  8.4 1.3 %collective-permute-start = (f32[2,128,128]{2,1,0:T(8,128)S(1)}, f32[2,128,128]{2,1,0:T(8,128)S(1)}, u32[]{:S(2)}, u32[]{:S(2)}) collective-permute-start(f32[2,128,128]{2,1,0:T(8,128)S(1)} %get-tuple-element.17), channel_id=1, source_target_pairs={{0,1},{1,0},{2,3},{3,2},{4,5},{5,4},{6,7},{7,6},{8,9},{9,8},{10,11... | collective-permute-start | bytes 393224 | tf_op jit(solution)/shard_map/ppermute | solution.py:408
  9.5 4.8 %collective-permute-start.2 = (f32[2,128,128]{2,1,0:T(8,128)S(1)}, f32[2,128,128]{2,1,0:T(8,128)S(1)}, u32[]{:S(2)}, u32[]{:S(2)}) collective-permute-start(f32[2,128,128]{2,1,0:T(8,128)S(1)} %add.19), channel_id=1, source_target_pairs={{0,2},{2,0},{1,3},{3,1},{4,6},{6,4},{5,7},{7,5},{8,10},{10,8},{9,1... | collective-permute-start | bytes 393224 | tf_op jit(solution)/shard_map/ppermute | solution.py:408
  14.3 3.9 %collective-permute-start.3 = (f32[2,128,128]{2,1,0:T(8,128)S(1)}, f32[2,128,128]{2,1,0:T(8,128)S(1)}, u32[]{:S(2)}, u32[]{:S(2)}) collective-permute-start(f32[2,128,128]{2,1,0:T(8,128)S(1)} %add_add_fusion), channel_id=1, source_target_pairs={{0,4},{8,12},{16,20},{24,28},{4,0},{12,8},{20,16},{28,24},{1,5},{9... | collective-permute-start | bytes 393224 | tf_op jit(solution)/shard_map/ppermute | solution.py:408
  18.2 6.2 %collective-permute-start.4 = (f32[2,128,128]{2,1,0:T(8,128)S(1)}, f32[2,128,128]{2,1,0:T(8,128)S(1)}, u32[]{:S(2)}, u32[]{:S(2)}) collective-permute-start(f32[2,128,128]{2,1,0:T(8,128)S(1)} %add.21), channel_id=1, source_target_pairs={{0,8},{4,12},{16,24},{20,28},{8,0},{12,4},{24,16},{28,20},{1,9},{5... | collective-permute-start | bytes 393224 | tf_op jit(solution)/shard_map/ppermute | solution.py:408
  24.5 7.2 %collective-permute-start.5 = (f32[2,128,128]{2,1,0:T(8,128)S(1)}, f32[2,128,128]{2,1,0:T(8,128)S(1)}, u32[]{:S(2)}, u32[]{:S(2)}) collective-permute-start(f32[2,128,128]{2,1,0:T(8,128)S(1)} %add.22), channel_id=1, source_target_pairs={{0,28},{4,24},{8,20},{12,16},{28,0},{24,4},{20,8},{16,12},{1,29},{... | collective-permute-start | bytes 393224 | tf_op jit(solution)/shard_map/ppermute | solution.py:408
  47.5 7.1 %collective-permute-start.6 = (f32[16,40,128]{2,1,0:T(8,128)S(1)}, f32[16,40,128]{2,1,0:T(8,128)S(1)}, u32[]{:S(2)}, u32[]{:S(2)}) collective-permute-start(f32[16,40,128]{2,1,0:T(8,128)S(1)} %all_to_all.5.received_ref), channel_id=1, source_target_pairs={{0,1},{1,0},{2,3},{3,2},{4,5},{5,4},{6,7},{7,6},{8,9},{9,8},{10,11... | collective-permute-start | bytes 983048 | tf_op jit(solution)/shard_map/ppermute | solution.py:408

commit v7 on v6

--- a/solution.py
+++ b/solution.py
@@ -217,7 +217,7 @@
     far = product(inverse, split(stack(product(split(wave), forward))))
     far_real, far_imag = far[:WIN], far[WIN:]
     modulus = jnp.sqrt(far_real * far_real + far_imag * far_imag)
-    factor = 1.0 - measured_ref[lax.rem(slot_position(0), 4)] / jnp.maximum(modulus, 0.5)
+    factor = 1.0 - measured_ref[...] / jnp.maximum(modulus, 0.5)
     resid = jnp.concatenate([far_real * factor, far_imag * factor], axis=0)
     back = product(split(side(product(forward, split(resid)))), inverse)
     back = jnp.concatenate([back, jnp.zeros((FIELD_Y - WIN, 2 * WIN), jnp.float32)], axis=0)
@@ -274,7 +274,17 @@
     return jnp.where(equal, spread, 0.0).astype(jnp.bfloat16)
 
 
-def weights_kernel(oy_ref, ox_ref, index_ref, amplitude_ref, phase_ref, full_ref, rest_ref):
+def weights_kernel(
+    oy_ref, ox_ref, index_ref, amplitude_ref, phase_ref, measured_hbm, table_hbm,
+    full_ref, rest_ref, measured_ref, table_ref,
+    sem,
+):
+    copies = [
+        pltpu.make_async_copy(measured_hbm.at[lax.rem(slot_position(0), 4)], measured_ref, sem.at[0]),
+        pltpu.make_async_copy(table_hbm, table_ref, sem.at[1]),
+    ]
+    for copy in copies:
+        copy.start()
     beams, count = index_ref.shape[1], 2 * HALF
     where = [side_position(n // HALF, n % HALF) for n in range(count)]
     shape = (count, beams)
@@ -293,19 +303,28 @@
 
     full_ref[...] = spread_weights(coefs, TILE, full_parts, full_ref.shape)
     rest_ref[...] = spread_weights(coefs, REST, rest_parts, rest_ref.shape)
-
-
-def fold_weights(offsets_y, offsets_x, beams):
+    for copy in copies:
+        copy.wait()
+
+
+def fold_weights(offsets_y, offsets_x, beams, measured, tables):
     rows, columns = 2 * beams[1].shape[1], 4 * HALF
     shapes = [(rows * size, columns * size) for size in (TILE, REST)]
     return pl.pallas_call(
         weights_kernel,
-        in_specs=[pl.BlockSpec(memory_space=pltpu.SMEM)] * 2 + [pl.BlockSpec(memory_space=pltpu.VMEM)] * 3,
-        out_specs=[pl.BlockSpec(memory_space=pltpu.VMEM)] * 2,
-        out_shape=[jax.ShapeDtypeStruct(shape, jnp.bfloat16) for shape in shapes],
-        compiler_params=pltpu.CompilerParams(vmem_limit_bytes=LIMIT),
+        in_specs=[pl.BlockSpec(memory_space=pltpu.SMEM)] * 2
+        + [pl.BlockSpec(memory_space=pltpu.VMEM)] * 3
+        + [pl.BlockSpec(memory_space=pl.ANY)] * 2,
+        out_specs=[pl.BlockSpec(memory_space=pltpu.VMEM)] * 4,
+        out_shape=[
+            *[pltpu.VMEM(shape, jnp.bfloat16) for shape in shapes],
+            pltpu.VMEM(measured.shape[1:], measured.dtype),
+            pltpu.VMEM(tables.shape, tables.dtype),
+        ],
+        scratch_shapes=[pltpu.SemaphoreType.DMA((2,))],
+        compiler_params=pltpu.CompilerParams(vmem_limit_bytes=WHOLE),
         cost_estimate=pl.CostEstimate(flops=100000000, bytes_accessed=1000000, transcendentals=0),
-    )(offsets_y, offsets_x, *beams)
+    )(offsets_y, offsets_x, *beams, measured, tables)
 
 
 PLACED = [(FULL, 2 * HALF * TILE, FIELD_X), (2 * HALF * REST, FIELD_X)]
@@ -418,16 +437,18 @@
     onward = slots[1] + swap(slots[3], "core", [(0, 1)])
     total = slots[0] + swap(slots[2], "core", [(0, 1)])
     total = total + swap(onward, "yl", [(0, 1)])
-    weights = fold_weights(offsets_y, offsets_x, beams)
+    tables = jnp.asarray(transform_tables())
+    fetched = fold_weights(offsets_y, offsets_x, beams, measured, tables)
     for bit in (1, 2):
         other = swap(total, "z", [(i, i ^ bit) for i in range(depth) if not i & bit])
         if bit == 1:
-            other, weights = lax.optimization_barrier((other, weights))
+            other, fetched = lax.optimization_barrier((other, fetched))
         total = total + other
     total = total + swap(total, "z", [(i, depth - 1 - i) for i in range(depth // 2)])
 
+    *weights, own_measured, tables = fetched
     copies = lax.axis_size("yl")
-    blocks = misfit_blocks(offsets_y, total, measured, jnp.asarray(transform_tables()), copies)
+    blocks = misfit_blocks(offsets_y, total, own_measured, tables, copies)
     blocks = blocks.reshape(BANDS * copies, BLOCK, WIN)
     received = lax.all_to_all(blocks, ("pos", "yl"), 0, 0, tiled=True)
     other = swap(received, "core", [(0, 1)])

time: 57.1 us -> 56.9 us (level)
  blocking collectives: 14.2 us -> 17.6 us
  starting transfers between devices: 14.9 us -> 12.4 us
  waiting for transfers between devices: 16.2 us -> 14.5 us
  Pallas kernels: 11.5 us -> 12.1 us
    all_to_all x1, blocking collectives: 14.2 us -> 17.6 us  [body(): received = lax.all_to_all(blocks, ('pos', 'yl'), 0, 0, tiled=True)]
    ppermute x7, starting transfers between devices: 14.9 us -> 12.4 us  [swap(): return lax.ppermute(value, axis, both)]
    ppermute x7, waiting for transfers between devices: 16.2 us -> 14.5 us  [swap(): return lax.ppermute(value, axis, both)]
    pallas_call x1, Pallas kernels: 1.72 us -> 2.9 us  [fold_weights(): pl.pallas_call(weights_kernel, in_specs=[pl.BlockSpec(memory_space=pltpu....]
  transfers between devices with their start and end apart: 7 -> 7, of which waited for: 7 -> 7; matrix products, arithmetic and copies ran while one was open for 0% -> 0% of each run, Pallas kernels for 4% -> 6%
where the time goes in v7:
time: 56.9 us; the launch traced here: 56.8 us
  blocking collectives  17.6 us (31%)
  waiting for transfers between devices  14.5 us (25%)
  starting transfers between devices  12.4 us (22%)
  Pallas kernels  12.1 us (21%)
    all_to_all x1, blocking collectives, body(): received = lax.all_to_all(blocks, ('pos', 'yl'), 0, 0, tiled=True)  17.6 us
    ppermute x7, waiting for transfers between devices, swap(): return lax.ppermute(value, axis, both)  14.5 us
    ppermute x7, starting transfers between devices, swap(): return lax.ppermute(value, axis, both)  12.4 us
    pallas_call x1, Pallas kernels, own_waves(): pl.pallas_call(waves_kernel, in_specs=[pl.BlockSpec(memory_space=pl.ANY)]...  4.56 us
    pallas_call x1, Pallas kernels, fold_weights(): pl.pallas_call(weights_kernel, in_specs=[pl.BlockSpec(memory_space=pltpu....  2.9 us
    pallas_call x1, Pallas kernels, fold(): pl.pallas_call(fold_kernel, in_specs=[pl.BlockSpec(memory_space=pltpu.SME...  2.45 us
    pallas_call x1, Pallas kernels, misfit_blocks(): pl.pallas_call(misfit_kernel, in_specs=[pl.BlockSpec(memory_space=pltpu.S...  1.51 us
  transfers between devices with their start and end apart: 7, of which 7 were waited for; matrix products, arithmetic and copies ran while one was open for 0% of the time, Pallas kernels for 6%

profile of v7, /device:TPU:1, one launch (start us, length us, event | category | flops | bytes accessed | tf_op | source)
XLA Modules:
  0.0 56.8 jit_solution(4666851493712709850)
XLA Ops:
  0.0 0.0 copy-start
  0.0 0.0 copy-start.1
  0.0 4.6 %shard_map.82 = (f32[2,128,128]{2,1,0:T(8,128)S(1)}, f32[2,128,128]{2,1,0:T(8,128)S(1)}, f32[2,128,128]{2,1,0:T(8,128)S(1)}, f32[2,128,128]{2,1,0:T(8,128)S(1)}) custom-call(s32[32]{0:T(128)} %oy_ref.3, s32[32]{0:T(128)} %ox_ref.5, s32[2,64]{1,0:T(2,128)} %bitcast.12, f32[1,64]{1,0:T(1,128)} %bitcast.14, f32[1,64]{1,0:T(1,128)} %bitcast.16, ...), custom_call_target="tpu_custom_call" | custom-call | tf_op jit(solution)/shard_map/pallas_call | solution.py:172
  4.6 3.3 %collective-permute-start.1 = (f32[2,128,128]{2,1,0:T(8,128)S(1)}, f32[2,128,128]{2,1,0:T(8,128)S(1)}, u32[]{:S(2)}, u32[]{:S(2)}) collective-permute-start(f32[2,128,128]{2,1,0:T(8,128)S(1)} %get-tuple-element.23), channel_id=1, source_target_pairs={{0,1},{1,0},{2,3},{3,2},{4,5},{5,4},{6,7},{7,6},{8,9},{9,8},{10,11... | collective-permute-start | bytes 393224 | tf_op jit(solution)/shard_map/ppermute | solution.py:427
  7.9 0.1 collective-permute-start
  8.0 0.9 %collective-permute-done.1 = f32[2,128,128]{2,1,0:T(8,128)S(1)} collective-permute-done((f32[2,128,128]{2,1,0:T(8,128)S(1)}, f32[2,128,128]{2,1,0:T(8,128)S(1)}, u32[]{:S(2)}, u32[]{:S(2)}) %collective-permute-start.1) | collective-permute-done | bytes 131104 | tf_op jit(solution)/shard_map/ppermute | solution.py:427
  8.9 0.1 collective-permute-start.2
  9.0 0.2 collective-permute-done
  9.2 4.5 %collective-permute-done.2 = f32[2,128,128]{2,1,0:T(8,128)S(1)} collective-permute-done((f32[2,128,128]{2,1,0:T(8,128)S(1)}, f32[2,128,128]{2,1,0:T(8,128)S(1)}, u32[]{:S(2)}, u32[]{:S(2)}) %collective-permute-start.2) | collective-permute-done | bytes 131104 | tf_op jit(solution)/shard_map/ppermute | solution.py:427
  13.7 0.1 collective-permute-start.3
  13.8 2.9 %shard_map.83 = (bf16[1024,512]{1,0:T(8,128)(2,1)S(1)}, bf16[256,128]{1,0:T(8,128)(2,1)S(1)}, f32[128,128]{1,0:T(8,128)S(1)}, bf16[2,2,256,256]{3,2,1,0:T(8,128)(2,1)S(1)}) custom-call(s32[32]{0:T(128)} %oy_ref.3, s32[32]{0:T(128)} %ox_ref.5, s32[2,64]{1,0:T(2,128)} %bitcast.13, f32[1,64]{1,0:T(1,128)} %bitcast.15, f32[1,64]{1,0:T(1,128)} %bitcast.17, ...), custom_call_target="tpu_custom_call" | custom-call | flops 100000000 | bytes 1000000 | tf_op jit(solution)/shard_map/pallas_call | solution.py:313
  16.8 0.9 %collective-permute-done.3 = f32[2,128,128]{2,1,0:T(8,128)S(1)} collective-permute-done((f32[2,128,128]{2,1,0:T(8,128)S(1)}, f32[2,128,128]{2,1,0:T(8,128)S(1)}, u32[]{:S(2)}, u32[]{:S(2)}) %collective-permute-start.3) | collective-permute-done | bytes 131104 | tf_op jit(solution)/shard_map/ppermute | solution.py:427
  17.7 2.1 %collective-permute-start.4 = (f32[2,128,128]{2,1,0:T(8,128)S(1)}, f32[2,128,128]{2,1,0:T(8,128)S(1)}, u32[]{:S(2)}, u32[]{:S(2)}) collective-permute-start(f32[2,128,128]{2,1,0:T(8,128)S(1)} %add.21), channel_id=1, source_target_pairs={{0,8},{4,12},{16,24},{20,28},{8,0},{12,4},{24,16},{28,20},{1,9},{5... | collective-permute-start | bytes 393224 | tf_op jit(solution)/shard_map/ppermute | solution.py:427
  19.7 4.1 %collective-permute-done.4 = f32[2,128,128]{2,1,0:T(8,128)S(1)} collective-permute-done((f32[2,128,128]{2,1,0:T(8,128)S(1)}, f32[2,128,128]{2,1,0:T(8,128)S(1)}, u32[]{:S(2)}, u32[]{:S(2)}) %collective-permute-start.4) | collective-permute-done | bytes 131104 | tf_op jit(solution)/shard_map/ppermute | solution.py:427
  23.9 3.9 %collective-permute-start.5 = (f32[2,128,128]{2,1,0:T(8,128)S(1)}, f32[2,128,128]{2,1,0:T(8,128)S(1)}, u32[]{:S(2)}, u32[]{:S(2)}) collective-permute-start(f32[2,128,128]{2,1,0:T(8,128)S(1)} %add.22), channel_id=1, source_target_pairs={{0,28},{4,24},{8,20},{12,16},{28,0},{24,4},{20,8},{16,12},{1,29},{... | collective-permute-start | bytes 393224 | tf_op jit(solution)/shard_map/ppermute | solution.py:427
  27.8 3.3 %collective-permute-done.5 = f32[2,128,128]{2,1,0:T(8,128)S(1)} collective-permute-done((f32[2,128,128]{2,1,0:T(8,128)S(1)}, f32[2,128,128]{2,1,0:T(8,128)S(1)}, u32[]{:S(2)}, u32[]{:S(2)}) %collective-permute-start.5) | collective-permute-done | bytes 131104 | tf_op jit(solution)/shard_map/ppermute | solution.py:427
  31.2 0.0 copy-done.1
  31.2 1.5 %shard_map.84 = f32[8,2,40,128]{3,2,1,0:T(8,128)S(1)} custom-call(s32[32]{0:T(128)S(1)} %copy-done.1, f32[2,128,128]{2,1,0:T(8,128)S(1)} %add.23.wave_ref, f32[128,128]{1,0:T(8,128)S(1)} %get-tuple-element.31.measured_ref, bf16[2,2,256,256]{3,2,1,0:T(8,128)(2,1)S(1)} %get-tuple-element.32.table_ref), custom_call_target="tpu_custom_call" | custom-call | tf_op jit(solution)/shard_map/pallas_call | solution.py:237
  32.7 17.6 %all_to_all.5.received_ref = f32[16,40,128]{2,1,0:T(8,128)S(1)} all-to-all(f32[16,40,128]{2,1,0:T(8,128)S(1)} %bitcast.10), channel_id=1, replica_groups=mesh['pos'=8,'z'=8,'yl'=2,'core'=2] {'pos','yl'}, dimensions={0} | all-to-all | bytes 655360 | tf_op jit(solution)/shard_map/all_to_all | solution.py:453
  50.2 2.8 %collective-permute-start.6 = (f32[16,40,128]{2,1,0:T(8,128)S(1)}, f32[16,40,128]{2,1,0:T(8,128)S(1)}, u32[]{:S(2)}, u32[]{:S(2)}) collective-permute-start(f32[16,40,128]{2,1,0:T(8,128)S(1)} %all_to_all.5.received_ref), channel_id=1, source_target_pairs={{0,1},{1,0},{2,3},{3,2},{4,5},{5,4},{6,7},{7,6},{8,9},{9,8},{10,11... | collective-permute-start | bytes 983048 | tf_op jit(solution)/shard_map/ppermute | solution.py:427
  53.1 0.0 copy-done
  53.1 0.7 %shard_map.85 = (bf16[2,256,256]{2,1,0:T(8,128)(2,1)S(1)}, bf16[64,256]{1,0:T(8,128)(2,1)S(1)}) custom-call(s32[32]{0:T(128)S(1)} %copy-done, f32[16,40,128]{2,1,0:T(8,128)S(1)} %all_to_all.5.received_ref), custom_call_target="tpu_custom_call" | custom-call | flops 1000000 | bytes 1000000 | tf_op jit(solution)/shard_map/pallas_call | solution.py:354
  53.8 0.5 collective-permute-done.6.other_ref
  54.3 2.5 %shard_map.86 = f32[4608,128]{1,0:T(8,128)} custom-call(s32[32]{0:T(128)S(1)} %copy-done, bf16[1024,512]{1,0:T(8,128)(2,1)S(1)} %get-tuple-element.28.weight_ref, bf16[256,128]{1,0:T(8,128)(2,1)S(1)} %get-tuple-element.29.weight_rest_ref, bf16[2,256,256]{2,1,0:T(8,128)(2,1)S(1)} %get-tuple-element.33.own_ref, ...), custom_call_target="tpu_custom_call" | custom-call | tf_op jit(solution)/shard_map/pallas_call | solution.py:411
  (5 shorter events, 0.1 us)
Async XLA Ops:
  0.0 53.1 %copy-start = (s32[32]{0:T(128)S(1)}, s32[32]{0:T(128)}, u32[]{:S(2)}) copy-start(s32[32]{0:T(128)} %ox_ref.5) | copy-start | bytes 388
  0.0 31.2 %copy-start.1 = (s32[32]{0:T(128)S(1)}, s32[32]{0:T(128)}, u32[]{:S(2)}) copy-start(s32[32]{0:T(128)} %oy_ref.3) | copy-start | bytes 388
  4.6 4.3 %collective-permute-start.1 = (f32[2,128,128]{2,1,0:T(8,128)S(1)}, f32[2,128,128]{2,1,0:T(8,128)S(1)}, u32[]{:S(2)}, u32[]{:S(2)}) collective-permute-start(f32[2,128,128]{2,1,0:T(8,128)S(1)} %get-tuple-element.23), channel_id=1, source_target_pairs={{0,1},{1,0},{2,3},{3,2},{4,5},{5,4},{6,7},{7,6},{8,9},{9,8},{10,11... | collective-permute-start | bytes 393224 | tf_op jit(solution)/shard_map/ppermute | solution.py:427
  7.9 1.3 %collective-permute-start = (f32[2,128,128]{2,1,0:T(8,128)S(1)}, f32[2,128,128]{2,1,0:T(8,128)S(1)}, u32[]{:S(2)}, u32[]{:S(2)}) collective-permute-start(f32[2,128,128]{2,1,0:T(8,128)S(1)} %get-tuple-element.21), channel_id=1, source_target_pairs={{0,1},{1,0},{2,3},{3,2},{4,5},{5,4},{6,7},{7,6},{8,9},{9,8},{10,11... | collective-permute-start | bytes 393224 | tf_op jit(solution)/shard_map/ppermute | solution.py:427
  8.9 4.8 %collective-permute-start.2 = (f32[2,128,128]{2,1,0:T(8,128)S(1)}, f32[2,128,128]{2,1,0:T(8,128)S(1)}, u32[]{:S(2)}, u32[]{:S(2)}) collective-permute-start(f32[2,128,128]{2,1,0:T(8,128)S(1)} %add.19), channel_id=1, source_target_pairs={{0,2},{2,0},{1,3},{3,1},{4,6},{6,4},{5,7},{7,5},{8,10},{10,8},{9,1... | collective-permute-start | bytes 393224 | tf_op jit(solution)/shard_map/ppermute | solution.py:427
  13.7 3.9 %collective-permute-start.3 = (f32[2,128,128]{2,1,0:T(8,128)S(1)}, f32[2,128,128]{2,1,0:T(8,128)S(1)}, u32[]{:S(2)}, u32[]{:S(2)}) collective-permute-start(f32[2,128,128]{2,1,0:T(8,128)S(1)} %add_add_fusion), channel_id=1, source_target_pairs={{0,4},{8,12},{16,20},{24,28},{4,0},{12,8},{20,16},{28,24},{1,5},{9... | collective-permute-start | bytes 393224 | tf_op jit(solution)/shard_map/ppermute | solution.py:427
  17.7 6.2 %collective-permute-start.4 = (f32[2,128,128]{2,1,0:T(8,128)S(1)}, f32[2,128,128]{2,1,0:T(8,128)S(1)}, u32[]{:S(2)}, u32[]{:S(2)}) collective-permute-start(f32[2,128,128]{2,1,0:T(8,128)S(1)} %add.21), channel_id=1, source_target_pairs={{0,8},{4,12},{16,24},{20,28},{8,0},{12,4},{24,16},{28,20},{1,9},{5... | collective-permute-start | bytes 393224 | tf_op jit(solution)/shard_map/ppermute | solution.py:427
  23.9 7.2 %collective-permute-start.5 = (f32[2,128,128]{2,1,0:T(8,128)S(1)}, f32[2,128,128]{2,1,0:T(8,128)S(1)}, u32[]{:S(2)}, u32[]{:S(2)}) collective-permute-start(f32[2,128,128]{2,1,0:T(8,128)S(1)} %add.22), channel_id=1, source_target_pairs={{0,28},{4,24},{8,20},{12,16},{28,0},{24,4},{20,8},{16,12},{1,29},{... | collective-permute-start | bytes 393224 | tf_op jit(solution)/shard_map/ppermute | solution.py:427
  50.2 4.1 %collective-permute-start.6 = (f32[16,40,128]{2,1,0:T(8,128)S(1)}, f32[16,40,128]{2,1,0:T(8,128)S(1)}, u32[]{:S(2)}, u32[]{:S(2)}) collective-permute-start(f32[16,40,128]{2,1,0:T(8,128)S(1)} %all_to_all.5.received_ref), channel_id=1, source_target_pairs={{0,1},{1,0},{2,3},{3,2},{4,5},{5,4},{6,7},{7,6},{8,9},{9,8},{10,11... | collective-permute-start | bytes 983048 | tf_op jit(solution)/shard_map/ppermute | solution.py:427

commit v8 on v7

--- a/solution.py
+++ b/solution.py
@@ -435,7 +435,8 @@
 
     slots = own_waves(s_flat, offsets_y, offsets_x, beams)
     onward = slots[1] + swap(slots[3], "core", [(0, 1)])
-    total = slots[0] + swap(slots[2], "core", [(0, 1)])
+    onward, later = lax.optimization_barrier((onward, slots[2]))
+    total = slots[0] + swap(later, "core", [(0, 1)])
     total = total + swap(onward, "yl", [(0, 1)])
     tables = jnp.asarray(transform_tables())
     fetched = fold_weights(offsets_y, offsets_x, beams, measured, tables)

time: 56.9 us -> 57.5 us (1.011)
  waiting for transfers between devices: 14.5 us -> 19.3 us
  blocking collectives: 17.6 us -> 14.5 us
  starting transfers between devices: 12.4 us -> 11.3 us
    ppermute x7, waiting for transfers between devices: 14.5 us -> 19.3 us  [swap(): return lax.ppermute(value, axis, both)]
    all_to_all x1, blocking collectives: 17.6 us -> 14.5 us  [body(): received = lax.all_to_all(blocks, ('pos', 'yl'), 0, 0, tiled=True)]
    ppermute x7, starting transfers between devices: 12.4 us -> 11.3 us  [swap(): return lax.ppermute(value, axis, both)]
where the time goes in v8:
time: 57.5 us; the launch traced here: 57.4 us
  waiting for transfers between devices  19.3 us (34%)
  blocking collectives  14.5 us (25%)
  Pallas kernels  12.1 us (21%)
  starting transfers between devices  11.3 us (20%)
    ppermute x7, waiting for transfers between devices, swap(): return lax.ppermute(value, axis, both)  19.3 us
    all_to_all x1, blocking collectives, body(): received = lax.all_to_all(blocks, ('pos', 'yl'), 0, 0, tiled=True)  14.5 us
    ppermute x7, starting transfers between devices, swap(): return lax.ppermute(value, axis, both)  11.3 us
    pallas_call x1, Pallas kernels, own_waves(): pl.pallas_call(waves_kernel, in_specs=[pl.BlockSpec(memory_space=pl.ANY)]...  4.56 us
    pallas_call x1, Pallas kernels, fold_weights(): pl.pallas_call(weights_kernel, in_specs=[pl.BlockSpec(memory_space=pltpu....  2.91 us
    pallas_call x1, Pallas kernels, fold(): pl.pallas_call(fold_kernel, in_specs=[pl.BlockSpec(memory_space=pltpu.SME...  2.45 us
    pallas_call x1, Pallas kernels, misfit_blocks(): pl.pallas_call(misfit_kernel, in_specs=[pl.BlockSpec(memory_space=pltpu.S...  1.51 us
  transfers between devices with their start and end apart: 7, of which 7 were waited for; matrix products, arithmetic and copies ran while one was open for 0% of the time, Pallas kernels for 6%

profile of v8, /device:TPU:1, one launch (start us, length us, event | category | flops | bytes accessed | tf_op | source)
XLA Modules:
  0.0 57.4 jit_solution(4720070282807083652)
XLA Ops:
  0.0 0.0 copy-start
  0.0 0.0 copy-start.1
  0.0 4.6 %shard_map.82 = (f32[2,128,128]{2,1,0:T(8,128)S(1)}, f32[2,128,128]{2,1,0:T(8,128)S(1)}, f32[2,128,128]{2,1,0:T(8,128)S(1)}, f32[2,128,128]{2,1,0:T(8,128)S(1)}) custom-call(s32[32]{0:T(128)} %oy_ref.3, s32[32]{0:T(128)} %ox_ref.5, s32[2,64]{1,0:T(2,128)} %bitcast.12, f32[1,64]{1,0:T(1,128)} %bitcast.14, f32[1,64]{1,0:T(1,128)} %bitcast.16, ...), custom_call_target="tpu_custom_call" | custom-call | tf_op jit(solution)/shard_map/pallas_call | solution.py:172
  4.6 3.3 %collective-permute-start = (f32[2,128,128]{2,1,0:T(8,128)S(1)}, f32[2,128,128]{2,1,0:T(8,128)S(1)}, u32[]{:S(2)}, u32[]{:S(2)}) collective-permute-start(f32[2,128,128]{2,1,0:T(8,128)S(1)} %get-tuple-element.24), channel_id=1, source_target_pairs={{0,1},{1,0},{2,3},{3,2},{4,5},{5,4},{6,7},{7,6},{8,9},{9,8},{10,11... | collective-permute-start | bytes 393224 | tf_op jit(solution)/shard_map/ppermute | solution.py:427
  7.9 1.0 %collective-permute-done = f32[2,128,128]{2,1,0:T(8,128)S(1)} collective-permute-done((f32[2,128,128]{2,1,0:T(8,128)S(1)}, f32[2,128,128]{2,1,0:T(8,128)S(1)}, u32[]{:S(2)}, u32[]{:S(2)}) %collective-permute-start) | collective-permute-done | bytes 131104 | tf_op jit(solution)/shard_map/ppermute | solution.py:427
  8.9 0.4 collective-permute-start.1
  9.4 0.0 collective-permute-start.2
  9.4 1.0 %collective-permute-done.1 = f32[2,128,128]{2,1,0:T(8,128)S(1)} collective-permute-done((f32[2,128,128]{2,1,0:T(8,128)S(1)}, f32[2,128,128]{2,1,0:T(8,128)S(1)}, u32[]{:S(2)}, u32[]{:S(2)}) %collective-permute-start.1) | collective-permute-done | bytes 131104 | tf_op jit(solution)/shard_map/ppermute | solution.py:427
  10.3 4.0 %collective-permute-done.2 = f32[2,128,128]{2,1,0:T(8,128)S(1)} collective-permute-done((f32[2,128,128]{2,1,0:T(8,128)S(1)}, f32[2,128,128]{2,1,0:T(8,128)S(1)}, u32[]{:S(2)}, u32[]{:S(2)}) %collective-permute-start.2) | collective-permute-done | bytes 131104 | tf_op jit(solution)/shard_map/ppermute | solution.py:427
  14.3 0.1 collective-permute-start.3
  14.4 2.9 %shard_map.83 = (bf16[1024,512]{1,0:T(8,128)(2,1)S(1)}, bf16[256,128]{1,0:T(8,128)(2,1)S(1)}, f32[128,128]{1,0:T(8,128)S(1)}, bf16[2,2,256,256]{3,2,1,0:T(8,128)(2,1)S(1)}) custom-call(s32[32]{0:T(128)} %oy_ref.3, s32[32]{0:T(128)} %ox_ref.5, s32[2,64]{1,0:T(2,128)} %bitcast.13, f32[1,64]{1,0:T(1,128)} %bitcast.15, f32[1,64]{1,0:T(1,128)} %bitcast.17, ...), custom_call_target="tpu_custom_call" | custom-call | flops 100000000 | bytes 1000000 | tf_op jit(solution)/shard_map/pallas_call | solution.py:313
  17.3 0.9 %collective-permute-done.3 = f32[2,128,128]{2,1,0:T(8,128)S(1)} collective-permute-done((f32[2,128,128]{2,1,0:T(8,128)S(1)}, f32[2,128,128]{2,1,0:T(8,128)S(1)}, u32[]{:S(2)}, u32[]{:S(2)}) %collective-permute-start.3) | collective-permute-done | bytes 131104 | tf_op jit(solution)/shard_map/ppermute | solution.py:427
  18.3 2.1 %collective-permute-start.4 = (f32[2,128,128]{2,1,0:T(8,128)S(1)}, f32[2,128,128]{2,1,0:T(8,128)S(1)}, u32[]{:S(2)}, u32[]{:S(2)}) collective-permute-start(f32[2,128,128]{2,1,0:T(8,128)S(1)} %add.21), channel_id=1, source_target_pairs={{0,8},{4,12},{16,24},{20,28},{8,0},{12,4},{24,16},{28,20},{1,9},{5... | collective-permute-start | bytes 393224 | tf_op jit(solution)/shard_map/ppermute | solution.py:427
  20.3 6.0 %collective-permute-done.4 = f32[2,128,128]{2,1,0:T(8,128)S(1)} collective-permute-done((f32[2,128,128]{2,1,0:T(8,128)S(1)}, f32[2,128,128]{2,1,0:T(8,128)S(1)}, u32[]{:S(2)}, u32[]{:S(2)}) %collective-permute-start.4) | collective-permute-done | bytes 131104 | tf_op jit(solution)/shard_map/ppermute | solution.py:427
  26.4 2.5 %collective-permute-start.5 = (f32[2,128,128]{2,1,0:T(8,128)S(1)}, f32[2,128,128]{2,1,0:T(8,128)S(1)}, u32[]{:S(2)}, u32[]{:S(2)}) collective-permute-start(f32[2,128,128]{2,1,0:T(8,128)S(1)} %add.22), channel_id=1, source_target_pairs={{0,28},{4,24},{8,20},{12,16},{28,0},{24,4},{20,8},{16,12},{1,29},{... | collective-permute-start | bytes 393224 | tf_op jit(solution)/shard_map/ppermute | solution.py:427
  28.9 5.9 %collective-permute-done.5 = f32[2,128,128]{2,1,0:T(8,128)S(1)} collective-permute-done((f32[2,128,128]{2,1,0:T(8,128)S(1)}, f32[2,128,128]{2,1,0:T(8,128)S(1)}, u32[]{:S(2)}, u32[]{:S(2)}) %collective-permute-start.5) | collective-permute-done | bytes 131104 | tf_op jit(solution)/shard_map/ppermute | solution.py:427
  34.8 0.0 copy-done.1
  34.8 1.5 %shard_map.84 = f32[8,2,40,128]{3,2,1,0:T(8,128)S(1)} custom-call(s32[32]{0:T(128)S(1)} %copy-done.1, f32[2,128,128]{2,1,0:T(8,128)S(1)} %add.23.wave_ref, f32[128,128]{1,0:T(8,128)S(1)} %get-tuple-element.35.measured_ref, bf16[2,2,256,256]{3,2,1,0:T(8,128)(2,1)S(1)} %get-tuple-element.36.table_ref), custom_call_target="tpu_custom_call" | custom-call | tf_op jit(solution)/shard_map/pallas_call | solution.py:237
  36.3 14.5 %all_to_all.5.received_ref = f32[16,40,128]{2,1,0:T(8,128)S(1)} all-to-all(f32[16,40,128]{2,1,0:T(8,128)S(1)} %bitcast.10), channel_id=1, replica_groups=mesh['pos'=8,'z'=8,'yl'=2,'core'=2] {'pos','yl'}, dimensions={0} | all-to-all | bytes 655360 | tf_op jit(solution)/shard_map/all_to_all | solution.py:454
  50.8 2.8 %collective-permute-start.6 = (f32[16,40,128]{2,1,0:T(8,128)S(1)}, f32[16,40,128]{2,1,0:T(8,128)S(1)}, u32[]{:S(2)}, u32[]{:S(2)}) collective-permute-start(f32[16,40,128]{2,1,0:T(8,128)S(1)} %all_to_all.5.received_ref), channel_id=1, source_target_pairs={{0,1},{1,0},{2,3},{3,2},{4,5},{5,4},{6,7},{7,6},{8,9},{9,8},{10,11... | collective-permute-start | bytes 983048 | tf_op jit(solution)/shard_map/ppermute | solution.py:427
  53.7 0.0 copy-done
  53.7 0.7 %shard_map.85 = (bf16[2,256,256]{2,1,0:T(8,128)(2,1)S(1)}, bf16[64,256]{1,0:T(8,128)(2,1)S(1)}) custom-call(s32[32]{0:T(128)S(1)} %copy-done, f32[16,40,128]{2,1,0:T(8,128)S(1)} %all_to_all.5.received_ref), custom_call_target="tpu_custom_call" | custom-call | flops 1000000 | bytes 1000000 | tf_op jit(solution)/shard_map/pallas_call | solution.py:354
  54.4 0.5 collective-permute-done.6.other_ref
  54.9 2.5 %shard_map.86 = f32[4608,128]{1,0:T(8,128)} custom-call(s32[32]{0:T(128)S(1)} %copy-done, bf16[1024,512]{1,0:T(8,128)(2,1)S(1)} %get-tuple-element.32.weight_ref, bf16[256,128]{1,0:T(8,128)(2,1)S(1)} %get-tuple-element.33.weight_rest_ref, bf16[2,256,256]{2,1,0:T(8,128)(2,1)S(1)} %get-tuple-element.37.own_ref, ...), custom_call_target="tpu_custom_call" | custom-call | tf_op jit(solution)/shard_map/pallas_call | solution.py:411
  (5 shorter events, 0.1 us)
Async XLA Ops:
  0.0 53.7 %copy-start = (s32[32]{0:T(128)S(1)}, s32[32]{0:T(128)}, u32[]{:S(2)}) copy-start(s32[32]{0:T(128)} %ox_ref.5) | copy-start | bytes 388
  0.0 34.8 %copy-start.1 = (s32[32]{0:T(128)S(1)}, s32[32]{0:T(128)}, u32[]{:S(2)}) copy-start(s32[32]{0:T(128)} %oy_ref.3) | copy-start | bytes 388
  4.6 4.3 %collective-permute-start = (f32[2,128,128]{2,1,0:T(8,128)S(1)}, f32[2,128,128]{2,1,0:T(8,128)S(1)}, u32[]{:S(2)}, u32[]{:S(2)}) collective-permute-start(f32[2,128,128]{2,1,0:T(8,128)S(1)} %get-tuple-element.24), channel_id=1, source_target_pairs={{0,1},{1,0},{2,3},{3,2},{4,5},{5,4},{6,7},{7,6},{8,9},{9,8},{10,11... | collective-permute-start | bytes 393224 | tf_op jit(solution)/shard_map/ppermute | solution.py:427
  8.9 1.4 %collective-permute-start.1 = (f32[2,128,128]{2,1,0:T(8,128)S(1)}, f32[2,128,128]{2,1,0:T(8,128)S(1)}, u32[]{:S(2)}, u32[]{:S(2)}) collective-permute-start(f32[2,128,128]{2,1,0:T(8,128)S(1)} %get-tuple-element.26), channel_id=1, source_target_pairs={{0,1},{1,0},{2,3},{3,2},{4,5},{5,4},{6,7},{7,6},{8,9},{9,8},{10,11... | collective-permute-start | bytes 393224 | tf_op jit(solution)/shard_map/ppermute | solution.py:427
  9.4 4.9 %collective-permute-start.2 = (f32[2,128,128]{2,1,0:T(8,128)S(1)}, f32[2,128,128]{2,1,0:T(8,128)S(1)}, u32[]{:S(2)}, u32[]{:S(2)}) collective-permute-start(f32[2,128,128]{2,1,0:T(8,128)S(1)} %add.18), channel_id=1, source_target_pairs={{0,2},{2,0},{1,3},{3,1},{4,6},{6,4},{5,7},{7,5},{8,10},{10,8},{9,1... | collective-permute-start | bytes 393224 | tf_op jit(solution)/shard_map/ppermute | solution.py:427
  14.3 3.9 %collective-permute-start.3 = (f32[2,128,128]{2,1,0:T(8,128)S(1)}, f32[2,128,128]{2,1,0:T(8,128)S(1)}, u32[]{:S(2)}, u32[]{:S(2)}) collective-permute-start(f32[2,128,128]{2,1,0:T(8,128)S(1)} %add_add_fusion), channel_id=1, source_target_pairs={{0,4},{8,12},{16,20},{24,28},{4,0},{12,8},{20,16},{28,24},{1,5},{9... | collective-permute-start | bytes 393224 | tf_op jit(solution)/shard_map/ppermute | solution.py:427
  18.3 8.1 %collective-permute-start.4 = (f32[2,128,128]{2,1,0:T(8,128)S(1)}, f32[2,128,128]{2,1,0:T(8,128)S(1)}, u32[]{:S(2)}, u32[]{:S(2)}) collective-permute-start(f32[2,128,128]{2,1,0:T(8,128)S(1)} %add.21), channel_id=1, source_target_pairs={{0,8},{4,12},{16,24},{20,28},{8,0},{12,4},{24,16},{28,20},{1,9},{5... | collective-permute-start | bytes 393224 | tf_op jit(solution)/shard_map/ppermute | solution.py:427
  26.4 8.4 %collective-permute-start.5 = (f32[2,128,128]{2,1,0:T(8,128)S(1)}, f32[2,128,128]{2,1,0:T(8,128)S(1)}, u32[]{:S(2)}, u32[]{:S(2)}) collective-permute-start(f32[2,128,128]{2,1,0:T(8,128)S(1)} %add.22), channel_id=1, source_target_pairs={{0,28},{4,24},{8,20},{12,16},{28,0},{24,4},{20,8},{16,12},{1,29},{... | collective-permute-start | bytes 393224 | tf_op jit(solution)/shard_map/ppermute | solution.py:427
  50.8 4.1 %collective-permute-start.6 = (f32[16,40,128]{2,1,0:T(8,128)S(1)}, f32[16,40,128]{2,1,0:T(8,128)S(1)}, u32[]{:S(2)}, u32[]{:S(2)}) collective-permute-start(f32[16,40,128]{2,1,0:T(8,128)S(1)} %all_to_all.5.received_ref), channel_id=1, source_target_pairs={{0,1},{1,0},{2,3},{3,2},{4,5},{5,4},{6,7},{7,6},{8,9},{9,8},{10,11... | collective-permute-start | bytes 983048 | tf_op jit(solution)/shard_map/ppermute | solution.py:427
